TPU v7x, 128 devices: a whole 4x4x4 slice. The times are simulated.
128 devices in a mesh: dp: 16 (over x, y), ctx: 8 (over z, core).
Axes of the slice: x: 4, y: 4, z: 4, core: 2. Of those that a mesh axis runs over, the one named last changes fastest.
Arguments:
- short_queries: bfloat16 [16, 8, 512, 2048], P('dp', 'ctx'), may hold values from -40 to 40
- short_keys: bfloat16 [16, 8, 512, 512], P('dp', 'ctx'), may hold values from -40 to 40
- short_values: bfloat16 [16, 8, 512, 512], P('dp', 'ctx'), may hold values from -6 to 6
- block_fill: int32 [16, 8, 8], P('dp', 'ctx'), may hold values from 32 to 64
- block_home: int32 [16, 8, 8], P('dp', 'ctx'), may hold values from 0 to 15, as said below
- long_queries: bfloat16 [16, 2048, 2048], P('dp', 'ctx'), may hold values from -40 to 40
- long_keys: bfloat16 [16, 2048, 512], P('dp', 'ctx'), may hold values from -40 to 40
- long_values: bfloat16 [16, 2048, 512], P('dp', 'ctx'), may hold values from -6 to 6
- long_docs: int32 [16, 2048], P('dp', 'ctx'), may hold values from 0 to 2, never falling along the last dimension, each value on 1 to 1024 neighbouring positions
Outputs:
- short_out: bfloat16 [16, 8, 512, 2048], P('dp', 'ctx')
- long_out: bfloat16 [16, 2048, 2048], P('dp', 'ctx')
Inputs may be any that keep to these rules, and one draw needn't show every extreme that they name: block_home[s, c, b] names a data group; at most 1 block of one device name the same group, and in each column c one group is named by exactly 1 block of every device.
All inputs are finite; a program needn't handle non-finite values.
Results may differ from a plain program's by a relative error of at most 0.004.
Values may be sent and summed in bfloat16 or wider, within the bound.
No kernel may reach another device: no remote copies, remote signals or barrier semaphores. Data moves between devices by JAX's collectives and lax.ppermute only.
A program may use at most 192 MiB of HBM per device.

v0:
```python
import functools

import jax
import jax.numpy as jnp
from jax import lax
from jax.experimental import pallas as pl
from jax.experimental.pallas import tpu as pltpu
from jax.sharding import PartitionSpec as P

QH = 16
KVH = 4
HD = 128
BLOCK = 64
SB = 8
GROUP = QH // KVH
SIDE = 4
GROUPS = SIDE * SIDE
RANKS = 8
ROWS = SB * BLOCK
LROWS = 256
CHUNK = 4
MASKED = -1e30
SCALE = HD**-0.5 * 1.4426950408889634
MIB = 1024 * 1024

VM = pl.BlockSpec(memory_space=pltpu.VMEM)
SM = pl.BlockSpec(memory_space=pltpu.SMEM)
HB = pl.BlockSpec(memory_space=pl.ANY)


def pairs(step):
    found = []
    for x in range(SIDE):
        for y in range(SIDE):
            for z in range(RANKS // 2):
                for core in range(2):
                    target = step(x, y, z, core)
                    if target is not None:
                        tx, ty, tz, tcore = target
                        found.append(
                            (
                                (x * SIDE + y) * RANKS + z * 2 + core,
                                (tx * SIDE + ty) * RANKS + tz * 2 + tcore,
                            )
                        )
    return found


def send(value, step):
    return lax.ppermute(value, ("dp", "ctx"), pairs(step))


def along_head(k):
    def step(x, y, z, core):
        if core == 0:
            return ((x + k) % SIDE, y, z, core)
        return (x, (y + k) % SIDE, z, core)

    return step


def along_rows(k):
    def step(x, y, z, core):
        if core == 0:
            return (x, (y + k) % SIDE, z, core)
        return ((x + k) % SIDE, y, z, core)

    return step


def up_chips(k):
    def step(x, y, z, core):
        return (x, y, z + k, core) if z + k < RANKS // 2 else None

    return step


def other_core(x, y, z, core):
    return (x, y, z, 1 - core)


def split_kv_kernel(meta, k_ref, v_ref, *outs):
    for k in range(SIDE):
        col = pl.multiple_of(((meta[0] + k) % SIDE) * HD, HD)
        outs[k][:, :HD] = k_ref[:, pl.ds(col, HD)]
        outs[k][:, HD:] = v_ref[:, pl.ds(col, HD)]


def split_kv(meta, keys, values):
    return pl.pallas_call(
        split_kv_kernel,
        out_shape=[jax.ShapeDtypeStruct((ROWS, 2 * HD), jnp.bfloat16)] * SIDE,
        in_specs=[SM, VM, VM],
        out_specs=[VM] * SIDE,
        cost_estimate=pl.CostEstimate(flops=0, bytes_accessed=2 * MIB, transcendentals=0),
    )(meta, keys, values)


def split_q_kernel(meta, q_ref, *outs):
    for k in range(SIDE):
        col = pl.multiple_of(((meta[0] + k) % SIDE) * GROUP * HD, GROUP * HD)
        outs[k][...] = q_ref[:, pl.ds(col, GROUP * HD)]


def split_q(meta, queries):
    width = GROUP * HD
    return pl.pallas_call(
        split_q_kernel,
        grid=(4,),
        out_shape=[jax.ShapeDtypeStruct((ROWS, width), jnp.bfloat16)] * SIDE,
        in_specs=[SM, pl.BlockSpec((ROWS // 4, QH * HD), lambda i: (i, 0))],
        out_specs=[pl.BlockSpec((ROWS // 4, width), lambda i: (i, 0))] * SIDE,
        cost_estimate=pl.CostEstimate(flops=0, bytes_accessed=4 * MIB, transcendentals=0),
    )(meta, queries)


def join_kernel(meta, *refs):
    out_ref = refs[-1]
    for k in range(SIDE):
        col = pl.multiple_of(((meta[0] + k) % SIDE) * GROUP * HD, GROUP * HD)
        out_ref[:, pl.ds(col, GROUP * HD)] = refs[k][...]


def join(meta, pieces):
    width = GROUP * HD
    return pl.pallas_call(
        join_kernel,
        grid=(4,),
        out_shape=jax.ShapeDtypeStruct((ROWS, QH * HD), jnp.bfloat16),
        in_specs=[SM] + [pl.BlockSpec((ROWS // 4, width), lambda i: (i, 0))] * SIDE,
        out_specs=pl.BlockSpec((ROWS // 4, QH * HD), lambda i: (i, 0)),
        cost_estimate=pl.CostEstimate(flops=0, bytes_accessed=4 * MIB, transcendentals=0),
    )(meta, *pieces)


def table_kernel(meta, hf_ref, slot_ref, fill_ref, rank_ref, count_ref):
    head, line, core = meta[0], meta[1], meta[2]

    def clear(i, _):
        slot_ref[i] = 0
        fill_ref[i] = 0
        return 0

    lax.fori_loop(0, GROUPS * GROUPS, clear, 0)
    for d in range(GROUPS):
        count_ref[d] = 0

    def source(s, _):
        high, low = s // SIDE, s % SIDE
        own_head = jnp.where(core == 0, high, low)
        own_line = jnp.where(core == 0, low, high)
        base = (((line - own_line) & 3) * SIDE + ((head - own_head) & 3)) * SB
        for b in range(SB):
            home = hf_ref[s, b]
            rank = count_ref[home]
            count_ref[home] = rank + 1
            rank_ref[s * SB + b] = rank
            slot_ref[home * GROUPS + rank] = base + b
            fill_ref[home * GROUPS + rank] = hf_ref[s, SB + b]
        return 0

    lax.fori_loop(0, GROUPS, source, 0)


def make_tables(meta, hf):
    ints = lambda n: jax.ShapeDtypeStruct((n,), jnp.int32)
    return pl.pallas_call(
        table_kernel,
        out_shape=[ints(GROUPS * GROUPS), ints(GROUPS * GROUPS), ints(GROUPS * SB)],
        in_specs=[SM, SM],
        out_specs=[SM, SM, SM],
        scratch_shapes=[pltpu.SMEM((GROUPS,), jnp.int32)],
        cost_estimate=pl.CostEstimate(flops=4096, bytes_accessed=4096, transcendentals=0),
    )(meta, hf)


def soften(scores, value_rows):
    row_max = jnp.max(scores, axis=-1, keepdims=True)
    weights = jnp.exp2((scores - row_max) * SCALE)
    totals = jnp.sum(weights, axis=-1, keepdims=True)
    mixture = jnp.dot(
        weights.astype(jnp.bfloat16), value_rows, preferred_element_type=jnp.float32
    )
    return mixture / totals


def inner(queries, key_rows):
    return lax.dot_general(
        queries, key_rows, (((1,), (1,)), ((), ())), preferred_element_type=jnp.float32
    )


def short_kernel(shifts, meta, hf_ref, slot_ref, fill_ref, rank_ref, *refs):
    kv_parts = refs[:SIDE]
    q_refs = refs[SIDE : SIDE + len(shifts)]
    out_refs = refs[SIDE + len(shifts) : SIDE + 2 * len(shifts)]
    kv_ref, sems = refs[-2:]
    part_rows = SIDE * ROWS
    copies = [
        pltpu.make_async_copy(
            kv_parts[j], kv_ref.at[pl.ds(j * part_rows, part_rows)], sems.at[j]
        )
        for j in range(SIDE)
    ]
    for copy in copies:
        copy.start()
    for copy in copies:
        copy.wait()
    head, line, core = meta[0], meta[1], meta[2]
    width = CHUNK * BLOCK
    lane = lax.broadcasted_iota(jnp.int32, (1, width), 1)
    lane_block = lane // BLOCK
    lane_row = lane % BLOCK
    row = lax.broadcasted_iota(jnp.int32, (BLOCK, width), 0)

    for position, k in enumerate(shifts):
        q_ref, out_ref = q_refs[position], out_refs[position]
        own_head = (head - k) & 3
        own = jnp.where(core == 0, own_head * SIDE + line, line * SIDE + own_head)

        def one_block(b, _, q_ref=q_ref, out_ref=out_ref, own=own):
            home = hf_ref[own, b]
            own_fill = hf_ref[own, SB + b]
            rank = rank_ref[own * SB + b]
            first = home * GROUPS
            rows = pl.ds(pl.multiple_of(b * BLOCK, BLOCK), BLOCK)

            def attend(chunks):
                q = q_ref[rows, :]
                q = jnp.concatenate(
                    [q[:, h * HD : (h + 1) * HD] for h in range(GROUP)], axis=0
                )
                key_parts, value_parts, biases = [], [], []
                for c in range(chunks):
                    limits = []
                    for j in range(CHUNK):
                        n = c * CHUNK + j
                        start = pl.multiple_of(slot_ref[first + n] * BLOCK, BLOCK)
                        kv = kv_ref[pl.ds(start, BLOCK), :]
                        key_parts.append(kv[:, :HD])
                        value_parts.append(kv[:, HD:])
                        limits.append(jnp.where(n <= rank, fill_ref[first + n], 0))
                    limit = jnp.where(
                        lane_block < 2,
                        jnp.where(lane_block == 0, limits[0], limits[1]),
                        jnp.where(lane_block == 2, limits[2], limits[3]),
                    )
                    if c < chunks - 1:
                        bias = jnp.where(lane_row < limit, 0.0, MASKED)
                        biases.append(jnp.broadcast_to(bias, (BLOCK, width)))
                    else:
                        causal = jnp.where(
                            lane_block == rank - c * CHUNK, row + 1, BLOCK
                        )
                        limit = jnp.minimum(limit, causal)
                        biases.append(jnp.where(lane_row < limit, 0.0, MASKED))
                keys = jnp.concatenate(key_parts, axis=0)
                values = jnp.concatenate(value_parts, axis=0)
                bias = jnp.concatenate(biases, axis=1)
                scores = inner(q, keys) + jnp.concatenate([bias] * GROUP, axis=0)
                mixed = soften(scores, values)
                used = lax.broadcasted_iota(jnp.int32, (BLOCK, HD), 0) < own_fill
                for h in range(GROUP):
                    part = jnp.where(used, mixed[h * BLOCK : (h + 1) * BLOCK], 0.0)
                    out_ref[rows, h * HD : (h + 1) * HD] = part.astype(jnp.bfloat16)

            for chunks in range(1, GROUPS // CHUNK + 1):
                pl.when(rank // CHUNK == chunks - 1)(functools.partial(attend, chunks))
            return 0

        lax.fori_loop(0, SB, one_block, 0)


def short_attention(shifts, meta, hf, tables, kv_parts, q_parts):
    count = len(shifts)
    return pl.pallas_call(
        functools.partial(short_kernel, shifts),
        out_shape=[jax.ShapeDtypeStruct((ROWS, GROUP * HD), jnp.bfloat16)] * count,
        in_specs=[SM] * 5 + [HB] * SIDE + [VM] * count,
        out_specs=[VM] * count,
        scratch_shapes=[
            pltpu.VMEM((GROUPS * ROWS, 2 * HD), jnp.bfloat16),
            pltpu.SemaphoreType.DMA((SIDE,)),
        ],
        compiler_params=pltpu.CompilerParams(vmem_limit_bytes=32 * MIB),
        cost_estimate=pl.CostEstimate(
            flops=count * 700_000_000, bytes_accessed=4 * MIB, transcendentals=count * 1_300_000
        ),
    )(meta, hf, *tables, *kv_parts, *q_parts)


def long_kernel(doc_ref, q_ref, *refs):
    parts = refs[:5]
    out_ref, bias_ref = refs[5:]
    own_doc = doc_ref[...]
    lane = lax.broadcasted_iota(jnp.int32, (LROWS, LROWS), 1)
    row = lax.broadcasted_iota(jnp.int32, (LROWS, LROWS), 0)
    for n in range(5):
        key_doc = parts[n][LROWS : LROWS + 16, :LROWS].astype(jnp.float32)[:1]
        allowed = own_doc == key_doc
        if n == 0:
            allowed = allowed & (lane <= row)
        bias_ref[:, n * LROWS : (n + 1) * LROWS] = jnp.where(allowed, 0.0, MASKED)

    def one_head(h, _):
        col = pl.multiple_of(h * HD, HD)
        vcol = pl.multiple_of((KVH + h) * HD, HD)
        keys = jnp.concatenate([p[:LROWS, pl.ds(col, HD)] for p in parts], axis=0)
        values = jnp.concatenate([p[:LROWS, pl.ds(vcol, HD)] for p in parts], axis=0)
        for i in range(GROUP):
            qcol = pl.multiple_of((h * GROUP + i) * HD, HD)
            scores = inner(q_ref[:, pl.ds(qcol, HD)], keys) + bias_ref[...]
            out_ref[:, pl.ds(qcol, HD)] = soften(scores, values).astype(jnp.bfloat16)
        return 0

    lax.fori_loop(0, KVH, one_head, 0)


def long_attention(docs, queries, parts):
    return pl.pallas_call(
        long_kernel,
        out_shape=jax.ShapeDtypeStruct((LROWS, QH * HD), jnp.bfloat16),
        in_specs=[VM] * 7,
        out_specs=VM,
        scratch_shapes=[pltpu.VMEM((LROWS, 5 * LROWS), jnp.float32)],
        compiler_params=pltpu.CompilerParams(vmem_limit_bytes=32 * MIB),
        cost_estimate=pl.CostEstimate(
            flops=2_700_000_000, bytes_accessed=5 * MIB, transcendentals=5_200_000
        ),
    )(docs, queries, *parts)


def shards(
    short_queries,
    short_keys,
    short_values,
    block_fill,
    block_home,
    long_queries,
    long_keys,
    long_values,
    long_docs,
):
    place, rank = lax.axis_index("dp"), lax.axis_index("ctx")
    core = rank % 2
    head = jnp.where(core == 0, place // SIDE, place % SIDE)
    line = jnp.where(core == 0, place % SIDE, place // SIDE)
    meta = jnp.stack([head, line, core]).astype(jnp.int32)

    kv_own = split_kv(meta, short_keys.reshape(ROWS, KVH * HD), short_values.reshape(ROWS, KVH * HD))
    kv_line = [kv_own[0]] + [send(kv_own[k], along_head(k)) for k in (1, 2, 3)]
    kv_line = jnp.concatenate(kv_line, axis=0)

    q_own = split_q(meta, short_queries.reshape(ROWS, QH * HD))
    q_parts = [q_own[0]] + [send(q_own[k], along_head(k)) for k in (1, 2, 3)]
    kv_parts = [kv_line] + [send(kv_line, along_rows(k)) for k in (1, 2, 3)]

    hf = jnp.concatenate([block_home.reshape(1, SB), block_fill.reshape(1, SB)], axis=1)
    hf = lax.all_gather(hf, "dp", axis=0, tiled=True)
    tables = make_tables(meta, hf)

    docs = long_docs.reshape(1, LROWS).astype(jnp.float32) + 1.0
    doc_rows = jnp.pad(docs.astype(jnp.bfloat16), ((0, 15), (0, 2 * KVH * HD - LROWS)))
    long_own = jnp.concatenate(
        [
            jnp.concatenate(
                [long_keys.reshape(LROWS, KVH * HD), long_values.reshape(LROWS, KVH * HD)], axis=1
            ),
            doc_rows,
        ],
        axis=0,
    )
    long_one = send(long_own, up_chips(1))
    long_two = send(long_own, up_chips(2))
    long_side = send(long_one, other_core)
    long_cross = send(jnp.where(core == 0, long_own, long_two), other_core)
    long_out = long_attention(
        docs.reshape(LROWS, 1),
        long_queries.reshape(LROWS, QH * HD),
        [long_own, long_one, long_two, long_side, long_cross],
    )

    mixed = short_attention((0, 1, 2, 3), meta, hf, tables, kv_parts, q_parts)
    back = [mixed[0]] + [send(mixed[k], along_head(-k)) for k in (1, 2, 3)]
    short_out = join(meta, back)
    return short_out.reshape(short_queries.shape), long_out.reshape(long_queries.shape)


def solution(mesh):
    return jax.shard_map(
        shards,
        mesh=mesh,
        in_specs=(
            P("dp", "ctx", None, None),
            P("dp", "ctx", None, None),
            P("dp", "ctx", None, None),
            P("dp", "ctx", None),
            P("dp", "ctx", None),
            P("dp", "ctx", None),
            P("dp", "ctx", None),
            P("dp", "ctx", None),
            P("dp", "ctx"),
        ),
        out_specs=(P("dp", "ctx", None, None), P("dp", "ctx", None)),
        check_vma=False,
    )
```

profile of v0, /device:TPU:0, one launch (start us, length us, event | category | flops | bytes accessed | tf_op | source)
XLA Modules:
  0.0 132.7 jit_solution(12032570387894037075)
XLA Ops:
  0.7 0.7 pad_add_fusion.meta
  1.3 2.4 %shard_map.105 = (bf16[512,256]{1,0:T(8,128)(2,1)}, bf16[512,256]{1,0:T(8,128)(2,1)}, bf16[512,256]{1,0:T(8,128)(2,1)}, bf16[512,256]{1,0:T(8,128)(2,1)}) custom-call(s32[3]{0:T(128)} %pad_add_fusion.meta, bf16[512,512]{1,0:T(8,128)(2,1)} %bitcast.27, bf16[512,512]{1,0:T(8,128)(2,1)} %bitcast.28), custom_call_target="tpu_custom_call" | custom-call | bytes 2097152 | tf_op jit(solution)/shard_map/pallas_call | solution.py:90
  3.7 1.6 %collective-permute-start = (bf16[512,256]{1,0:T(8,128)(2,1)}, bf16[512,256]{1,0:T(8,128)(2,1)S(1)}, u32[]{:S(2)}, u32[]{:S(2)}) collective-permute-start(bf16[512,256]{1,0:T(8,128)(2,1)} %get-tuple-element.21), channel_id=1, source_target_pairs={{0,32},{1,9},{2,34},{3,11},{4,36},{5,13},{6,38},{7,15},{8,40},{9,1... | collective-permute-start | bytes 786440 | tf_op jit(solution)/shard_map/ppermute | solution.py:50
  5.3 2.7 %collective-permute-start.1 = (bf16[512,256]{1,0:T(8,128)(2,1)}, bf16[512,256]{1,0:T(8,128)(2,1)S(1)}, u32[]{:S(2)}, u32[]{:S(2)}) collective-permute-start(bf16[512,256]{1,0:T(8,128)(2,1)} %get-tuple-element.22), channel_id=1, source_target_pairs={{0,64},{1,17},{2,66},{3,19},{4,68},{5,21},{6,70},{7,23},{8,72},{9,... | collective-permute-start | bytes 786440 | tf_op jit(solution)/shard_map/ppermute | solution.py:50
  8.1 1.4 %collective-permute-start.2 = (bf16[512,256]{1,0:T(8,128)(2,1)}, bf16[512,256]{1,0:T(8,128)(2,1)S(1)}, u32[]{:S(2)}, u32[]{:S(2)}) collective-permute-start(bf16[512,256]{1,0:T(8,128)(2,1)} %get-tuple-element.23), channel_id=1, source_target_pairs={{0,96},{1,25},{2,98},{3,27},{4,100},{5,29},{6,102},{7,31},{8,104},... | collective-permute-start | bytes 786440 | tf_op jit(solution)/shard_map/ppermute | solution.py:50
  9.5 3.8 %shard_map.106 = (bf16[512,512]{1,0:T(8,128)(2,1)}, bf16[512,512]{1,0:T(8,128)(2,1)}, bf16[512,512]{1,0:T(8,128)(2,1)}, bf16[512,512]{1,0:T(8,128)(2,1)}) custom-call(s32[3]{0:T(128)} %pad_add_fusion.meta, bf16[512,2048]{1,0:T(8,128)(2,1)} %bitcast.21), custom_call_target="tpu_custom_call" | custom-call | bytes 4194304 | tf_op jit(solution)/shard_map/pallas_call | solution.py:107
  13.3 0.6 collective-permute-start.6
  13.9 0.9 collective-permute-start.7
  14.8 0.1 fusion.1.refs_0_
  14.9 0.0 copy-start.18
  15.0 0.0 collective-permute-done
  15.0 5.9 %collective-permute-start.13 = (bf16[272,1024]{1,0:T(8,128)(2,1)S(1)}, bf16[272,1024]{1,0:T(8,128)(2,1)S(1)}, u32[]{:S(2)}, u32[]{:S(2)}) collective-permute-start(bf16[272,1024]{1,0:T(8,128)(2,1)S(1)} %fusion.1.refs_0_), channel_id=1, source_target_pairs={{0,4},{1,5},{2,6},{3,7},{8,12},{9,13},{10,14},{11,15},{16,20},{17,... | collective-permute-start | bytes 1671176 | tf_op jit(solution)/shard_map/ppermute | solution.py:50
  21.0 0.0 copy-start.23
  21.0 0.0 copy-start.24
  21.1 1.6 %collective-permute-start.3 = (bf16[2048,256]{1,0:T(8,128)(2,1)S(1)}, bf16[2048,256]{1,0:T(8,128)(2,1)S(1)}, u32[]{:S(2)}, u32[]{:S(2)}) collective-permute-start(bf16[2048,256]{1,0:T(8,128)(2,1)S(1)} %constant_dynamic-update-slice_fusion.refs_0_), channel_id=1, source_target_pairs={{0,8},{1,33},{2,10},{3,35},{4,12},{5,37},{6,14},{7,39},{8,16},{9,4... | collective-permute-start | bytes 3145736 | tf_op jit(solution)/shard_map/ppermute | solution.py:50
  22.7 2.9 %collective-permute-start.4 = (bf16[2048,256]{1,0:T(8,128)(2,1)S(1)}, bf16[2048,256]{1,0:T(8,128)(2,1)}, u32[]{:S(2)}, u32[]{:S(2)}) collective-permute-start(bf16[2048,256]{1,0:T(8,128)(2,1)S(1)} %constant_dynamic-update-slice_fusion.refs_0_), channel_id=1, source_target_pairs={{0,16},{1,65},{2,18},{3,67},{4,20},{5,69},{6,22},{7,71},{8,24},{9,... | collective-permute-start | bytes 3145736 | tf_op jit(solution)/shard_map/ppermute | solution.py:50
  25.6 5.5 %collective-permute-done.6.refs_5_ = bf16[512,512]{1,0:T(8,128)(2,1)S(1)} collective-permute-done((bf16[512,512]{1,0:T(8,128)(2,1)}, bf16[512,512]{1,0:T(8,128)(2,1)S(1)}, u32[]{:S(2)}, u32[]{:S(2)}) %collective-permute-start.6) | collective-permute-done | bytes 524320 | tf_op jit(solution)/shard_map/ppermute | solution.py:50
  31.2 0.8 copy-done.7
  31.9 2.0 %collective-permute-start.5 = (bf16[2048,256]{1,0:T(8,128)(2,1)S(1)}, bf16[2048,256]{1,0:T(8,128)(2,1)}, u32[]{:S(2)}, u32[]{:S(2)}) collective-permute-start(bf16[2048,256]{1,0:T(8,128)(2,1)S(1)} %constant_dynamic-update-slice_fusion.refs_0_), channel_id=1, source_target_pairs={{0,24},{1,97},{2,26},{3,99},{4,28},{5,101},{6,30},{7,103},{8,0},{9... | collective-permute-start | bytes 3145736 | tf_op jit(solution)/shard_map/ppermute | solution.py:50
  34.0 0.8 copy-done.9
  34.8 5.2 %collective-permute-start.12 = (bf16[272,1024]{1,0:T(8,128)(2,1)S(1)}, bf16[272,1024]{1,0:T(8,128)(2,1)}, u32[]{:S(2)}, u32[]{:S(2)}) collective-permute-start(bf16[272,1024]{1,0:T(8,128)(2,1)S(1)} %fusion.1.refs_0_), channel_id=1, source_target_pairs={{0,2},{1,3},{2,4},{3,5},{4,6},{5,7},{8,10},{9,11},{10,12},{11,13},... | collective-permute-start | bytes 1671176 | tf_op jit(solution)/shard_map/ppermute | solution.py:50
  40.1 1.0 broadcast_select_fusion
  41.0 11.9 %collective-permute-done.8.refs_7_ = bf16[512,512]{1,0:T(8,128)(2,1)S(1)} collective-permute-done((bf16[512,512]{1,0:T(8,128)(2,1)S(1)}, bf16[512,512]{1,0:T(8,128)(2,1)S(1)}, u32[]{:S(2)}, u32[]{:S(2)}) %collective-permute-start.8) | collective-permute-done | bytes 524320 | tf_op jit(solution)/shard_map/ppermute | solution.py:50
  52.9 0.8 copy-done.11
  53.7 0.5 collective-permute-start.14
  54.2 0.1 add_bitcast_fusion
  54.3 22.3 %all-gather = s32[16,1,16]{2,1,0:T(1,128)} all-gather(s32[1,1,16]{2,1,0:T(1,128)S(1)} %add_bitcast_fusion), channel_id=1, replica_groups=mesh['dp'=16,'ctx'=8] {'dp'}, dimensions={0}, use_global_device_ids=true | all-gather | bytes 1088 | tf_op jit(solution)/shard_map/all_gather | solution.py:359
  76.6 3.9 %shard_map.104 = (s32[256]{0:T(256)}, s32[256]{0:T(256)}, s32[128]{0:T(128)}) custom-call(s32[3]{0:T(128)} %pad_add_fusion.meta, s32[16,16]{1,0:T(8,128)} %bitcast.18), custom_call_target="tpu_custom_call" | custom-call | flops 4096 | bytes 4096 | tf_op jit(solution)/shard_map/pallas_call | solution.py:167
  80.5 0.0 copy-start.4
  80.5 1.0 copy-done.4
  81.5 0.7 copy-done.1
  82.2 1.2 copy-done.5
  83.4 1.0 copy-done.6
  84.5 1.0 copy-done.8
  85.5 1.0 copy-done.10
  86.6 1.0 copy-done.12
  87.6 0.6 copy-done.13
  88.2 0.7 copy-done.14
  88.9 0.7 copy-done.15
  89.6 19.6 %shard_map.107 = (bf16[512,512]{1,0:T(8,128)(2,1)S(1)}, bf16[512,512]{1,0:T(8,128)(2,1)}, bf16[512,512]{1,0:T(8,128)(2,1)}, bf16[512,512]{1,0:T(8,128)(2,1)}) custom-call(s32[3]{0:T(128)S(1)} %copy-done.2, s32[16,16]{1,0:T(8,128)S(1)} %bitcast.19, s32[256]{0:T(256)S(1)} %copy-done.13, s32[256]{0:T(256)S(1)} %copy-done.14, s32[128]{0:T(128)S(1)} %copy-done.15, ...), custom_call_target="tpu_custom_call" | custom-call | flops 2800000000 | bytes 4194304 | tf_op jit(solution)/shard_map/pallas_call | solution.py:276
  109.3 0.8 copy-done
  110.0 1.6 %collective-permute-start.10 = (bf16[512,512]{1,0:T(8,128)(2,1)}, bf16[512,512]{1,0:T(8,128)(2,1)S(1)}, u32[]{:S(2)}, u32[]{:S(2)}) collective-permute-start(bf16[512,512]{1,0:T(8,128)(2,1)} %get-tuple-element.30), channel_id=1, source_target_pairs={{0,64},{1,17},{2,66},{3,19},{4,68},{5,21},{6,70},{7,23},{8,72},{9,... | collective-permute-start | bytes 1572872 | tf_op jit(solution)/shard_map/ppermute | solution.py:50
  111.7 0.4 collective-permute-start.11
  112.1 2.8 %collective-permute-start.9 = (bf16[512,512]{1,0:T(8,128)(2,1)}, bf16[512,512]{1,0:T(8,128)(2,1)}, u32[]{:S(2)}, u32[]{:S(2)}) collective-permute-start(bf16[512,512]{1,0:T(8,128)(2,1)} %get-tuple-element.29), channel_id=1, source_target_pairs={{0,96},{1,25},{2,98},{3,27},{4,100},{5,29},{6,102},{7,31},{8,104},... | collective-permute-start | bytes 1572872 | tf_op jit(solution)/shard_map/ppermute | solution.py:50
  114.9 0.1 copy.14.doc_ref
  115.1 13.0 %shard_map.109 = bf16[256,2048]{1,0:T(8,128)(2,1)} custom-call(f32[256,1]{1,0:T(8,128)S(1)} %copy.14.doc_ref, bf16[256,2048]{1,0:T(8,128)(2,1)S(1)} %bitcast.20, bf16[272,1024]{1,0:T(8,128)(2,1)S(1)} %fusion.1.refs_0_, bf16[272,1024]{1,0:T(8,128)(2,1)} %collective-permute-done.12.refs_1_, bf16[272,1024]{1,0:T(8,128)(2,1)S(1)} %collective-permute-done.13.refs_2_, ...), custom_call_target="tpu_custom_call" | custom-call | flops 2700000000 | bytes 5242880 | tf_op jit(solution)/shard_map/pallas_call | solution.py:320
  128.1 0.8 copy-done.19
  128.8 3.8 %shard_map.108 = bf16[512,2048]{1,0:T(8,128)(2,1)} custom-call(s32[3]{0:T(128)} %pad_add_fusion.meta, bf16[512,512]{1,0:T(8,128)(2,1)} %copy-done, bf16[512,512]{1,0:T(8,128)(2,1)} %collective-permute-done.9.refs_1_, bf16[512,512]{1,0:T(8,128)(2,1)} %copy-done.19, bf16[512,512]{1,0:T(8,128)(2,1)} %collective-permute-done.11.refs_3_), custom_call_target="tpu_custom_call" | custom-call | bytes 4194304 | tf_op jit(solution)/shard_map/pallas_call | solution.py:126
  (51 shorter events, 0.2 us)
Async XLA Ops:
  3.7 11.1 %copy-start.21 = (s32[1,256]{1,0:T(1,128)S(1)}, s32[1,256]{1,0:T(1,128)}, u32[]{:S(2)}) copy-start(s32[1,256]{1,0:T(1,128)} %param.17) | copy-start | bytes 3076
  3.7 11.1 %copy-start.16 = (bf16[1,256,512]{2,1,0:T(8,128)(2,1)S(1)}, bf16[1,256,512]{2,1,0:T(8,128)(2,1)}, u32[]{:S(2)}) copy-start(bf16[1,256,512]{2,1,0:T(8,128)(2,1)} %param.16) | copy-start | bytes 786436
  3.7 11.1 %copy-start.17 = (bf16[1,256,512]{2,1,0:T(8,128)(2,1)S(1)}, bf16[1,256,512]{2,1,0:T(8,128)(2,1)}, u32[]{:S(2)}) copy-start(bf16[1,256,512]{2,1,0:T(8,128)(2,1)} %param.15) | copy-start | bytes 786436
  3.7 11.3 %collective-permute-start = (bf16[512,256]{1,0:T(8,128)(2,1)}, bf16[512,256]{1,0:T(8,128)(2,1)S(1)}, u32[]{:S(2)}, u32[]{:S(2)}) collective-permute-start(bf16[512,256]{1,0:T(8,128)(2,1)} %get-tuple-element.21), channel_id=1, source_target_pairs={{0,32},{1,9},{2,34},{3,11},{4,36},{5,13},{6,38},{7,15},{8,40},{9,1... | collective-permute-start | bytes 786440 | tf_op jit(solution)/shard_map/ppermute | solution.py:50
  5.3 15.6 %collective-permute-start.1 = (bf16[512,256]{1,0:T(8,128)(2,1)}, bf16[512,256]{1,0:T(8,128)(2,1)S(1)}, u32[]{:S(2)}, u32[]{:S(2)}) collective-permute-start(bf16[512,256]{1,0:T(8,128)(2,1)} %get-tuple-element.22), channel_id=1, source_target_pairs={{0,64},{1,17},{2,66},{3,19},{4,68},{5,21},{6,70},{7,23},{8,72},{9,... | collective-permute-start | bytes 786440 | tf_op jit(solution)/shard_map/ppermute | solution.py:50
  8.1 13.0 %collective-permute-start.2 = (bf16[512,256]{1,0:T(8,128)(2,1)}, bf16[512,256]{1,0:T(8,128)(2,1)S(1)}, u32[]{:S(2)}, u32[]{:S(2)}) collective-permute-start(bf16[512,256]{1,0:T(8,128)(2,1)} %get-tuple-element.23), channel_id=1, source_target_pairs={{0,96},{1,25},{2,98},{3,27},{4,100},{5,29},{6,102},{7,31},{8,104},... | collective-permute-start | bytes 786440 | tf_op jit(solution)/shard_map/ppermute | solution.py:50
  9.5 5.4 %copy-start.20 = (bf16[512,256]{1,0:T(8,128)(2,1)S(1)}, bf16[512,256]{1,0:T(8,128)(2,1)}, u32[]{:S(2)}) copy-start(bf16[512,256]{1,0:T(8,128)(2,1)} %get-tuple-element.20) | copy-start | bytes 786436
  13.3 17.8 %collective-permute-start.6 = (bf16[512,512]{1,0:T(8,128)(2,1)}, bf16[512,512]{1,0:T(8,128)(2,1)S(1)}, u32[]{:S(2)}, u32[]{:S(2)}) collective-permute-start(bf16[512,512]{1,0:T(8,128)(2,1)} %get-tuple-element.25), channel_id=1, source_target_pairs={{0,32},{1,9},{2,34},{3,11},{4,36},{5,13},{6,38},{7,15},{8,40},{9,1... | collective-permute-start | bytes 1572872 | tf_op jit(solution)/shard_map/ppermute | solution.py:50
  13.9 20.0 %collective-permute-start.7 = (bf16[512,512]{1,0:T(8,128)(2,1)}, bf16[512,512]{1,0:T(8,128)(2,1)S(1)}, u32[]{:S(2)}, u32[]{:S(2)}) collective-permute-start(bf16[512,512]{1,0:T(8,128)(2,1)} %get-tuple-element.26), channel_id=1, source_target_pairs={{0,64},{1,17},{2,66},{3,19},{4,68},{5,21},{6,70},{7,23},{8,72},{9,... | collective-permute-start | bytes 1572872 | tf_op jit(solution)/shard_map/ppermute | solution.py:50
  14.9 25.1 %copy-start.22 = (bf16[512,512]{1,0:T(8,128)(2,1)S(1)}, bf16[512,512]{1,0:T(8,128)(2,1)}, u32[]{:S(2)}) copy-start(bf16[512,512]{1,0:T(8,128)(2,1)} %get-tuple-element.27) | copy-start | bytes 1572868
  14.9 25.1 %copy-start.18 = (bf16[1,256,512]{2,1,0:T(8,128)(2,1)S(1)}, bf16[1,256,512]{2,1,0:T(8,128)(2,1)}, u32[]{:S(2)}) copy-start(bf16[1,256,512]{2,1,0:T(8,128)(2,1)} %param.15) | copy-start | bytes 786436
  15.0 25.1 %collective-permute-start.13 = (bf16[272,1024]{1,0:T(8,128)(2,1)S(1)}, bf16[272,1024]{1,0:T(8,128)(2,1)S(1)}, u32[]{:S(2)}, u32[]{:S(2)}) collective-permute-start(bf16[272,1024]{1,0:T(8,128)(2,1)S(1)} %fusion.1.refs_0_), channel_id=1, source_target_pairs={{0,4},{1,5},{2,6},{3,7},{8,12},{9,13},{10,14},{11,15},{16,20},{17,... | collective-permute-start | bytes 1671176 | tf_op jit(solution)/shard_map/ppermute | solution.py:50
  21.0 33.3 %copy-start.23 = (s32[1,1,8]{2,1,0:T(1,128)S(1)}, s32[1,1,8]{2,1,0:T(1,128)}, u32[]{:S(2)}) copy-start(s32[1,1,8]{2,1,0:T(1,128)} %param.12) | copy-start | bytes 100
  21.0 33.3 %copy-start.24 = (s32[1,1,8]{2,1,0:T(1,128)S(1)}, s32[1,1,8]{2,1,0:T(1,128)}, u32[]{:S(2)}) copy-start(s32[1,1,8]{2,1,0:T(1,128)} %param.13) | copy-start | bytes 100
  21.0 60.5 %copy-start.2 = (s32[3]{0:T(128)S(1)}, s32[3]{0:T(128)}, u32[]{:S(2)}) copy-start(s32[3]{0:T(128)} %pad_add_fusion.meta) | copy-start | bytes 40
  21.1 59.5 %collective-permute-start.3 = (bf16[2048,256]{1,0:T(8,128)(2,1)S(1)}, bf16[2048,256]{1,0:T(8,128)(2,1)S(1)}, u32[]{:S(2)}, u32[]{:S(2)}) collective-permute-start(bf16[2048,256]{1,0:T(8,128)(2,1)S(1)} %constant_dynamic-update-slice_fusion.refs_0_), channel_id=1, source_target_pairs={{0,8},{1,33},{2,10},{3,35},{4,12},{5,37},{6,14},{7,39},{8,16},{9,4... | collective-permute-start | bytes 3145736 | tf_op jit(solution)/shard_map/ppermute | solution.py:50
  22.7 58.8 %collective-permute-start.4 = (bf16[2048,256]{1,0:T(8,128)(2,1)S(1)}, bf16[2048,256]{1,0:T(8,128)(2,1)}, u32[]{:S(2)}, u32[]{:S(2)}) collective-permute-start(bf16[2048,256]{1,0:T(8,128)(2,1)S(1)} %constant_dynamic-update-slice_fusion.refs_0_), channel_id=1, source_target_pairs={{0,16},{1,65},{2,18},{3,67},{4,20},{5,69},{6,22},{7,71},{8,24},{9,... | collective-permute-start | bytes 3145736 | tf_op jit(solution)/shard_map/ppermute | solution.py:50
  31.1 0.8 copy-start.7
  31.9 49.6 %collective-permute-start.5 = (bf16[2048,256]{1,0:T(8,128)(2,1)S(1)}, bf16[2048,256]{1,0:T(8,128)(2,1)}, u32[]{:S(2)}, u32[]{:S(2)}) collective-permute-start(bf16[2048,256]{1,0:T(8,128)(2,1)S(1)} %constant_dynamic-update-slice_fusion.refs_0_), channel_id=1, source_target_pairs={{0,24},{1,97},{2,26},{3,99},{4,28},{5,101},{6,30},{7,103},{8,0},{9... | collective-permute-start | bytes 3145736 | tf_op jit(solution)/shard_map/ppermute | solution.py:50
  34.0 0.8 copy-start.9
  34.8 18.9 %collective-permute-start.12 = (bf16[272,1024]{1,0:T(8,128)(2,1)S(1)}, bf16[272,1024]{1,0:T(8,128)(2,1)}, u32[]{:S(2)}, u32[]{:S(2)}) collective-permute-start(bf16[272,1024]{1,0:T(8,128)(2,1)S(1)} %fusion.1.refs_0_), channel_id=1, source_target_pairs={{0,2},{1,3},{2,4},{3,5},{4,6},{5,7},{8,10},{9,11},{10,12},{11,13},... | collective-permute-start | bytes 1671176 | tf_op jit(solution)/shard_map/ppermute | solution.py:50
  40.0 12.9 %collective-permute-start.8 = (bf16[512,512]{1,0:T(8,128)(2,1)S(1)}, bf16[512,512]{1,0:T(8,128)(2,1)S(1)}, u32[]{:S(2)}, u32[]{:S(2)}) collective-permute-start(bf16[512,512]{1,0:T(8,128)(2,1)S(1)} %copy-done.22), channel_id=1, source_target_pairs={{0,96},{1,25},{2,98},{3,27},{4,100},{5,29},{6,102},{7,31},{8,104},... | collective-permute-start | bytes 1572872 | tf_op jit(solution)/shard_map/ppermute | solution.py:50
  52.9 0.8 copy-start.11
  53.7 61.3 %collective-permute-start.15 = (bf16[272,1024]{1,0:T(8,128)(2,1)}, bf16[272,1024]{1,0:T(8,128)(2,1)}, u32[]{:S(2)}, u32[]{:S(2)}) collective-permute-start(bf16[272,1024]{1,0:T(8,128)(2,1)} %broadcast_select_fusion), channel_id=1, source_target_pairs={{0,1},{1,0},{2,3},{3,2},{4,5},{5,4},{6,7},{7,6},{8,9},{9,8},{10,11... | collective-permute-start | bytes 1671176 | tf_op jit(solution)/shard_map/ppermute | solution.py:50
  53.7 61.3 %collective-permute-start.14 = (bf16[272,1024]{1,0:T(8,128)(2,1)}, bf16[272,1024]{1,0:T(8,128)(2,1)}, u32[]{:S(2)}, u32[]{:S(2)}) collective-permute-start(bf16[272,1024]{1,0:T(8,128)(2,1)} %collective-permute-done.12.refs_1_), channel_id=1, source_target_pairs={{0,1},{1,0},{2,3},{3,2},{4,5},{5,4},{6,7},{7,6},{8,9},{9,8},{10,11... | collective-permute-start | bytes 1671176 | tf_op jit(solution)/shard_map/ppermute | solution.py:50
  80.5 1.0 copy-start.4
  81.5 0.7 copy-start.1
  82.2 1.2 copy-start.5
  83.4 1.0 copy-start.6
  84.5 1.0 copy-start.8
  85.5 1.0 copy-start.10
  86.6 1.0 copy-start.12
  87.6 0.6 copy-start.13
  88.2 0.7 copy-start.14
  88.9 0.7 copy-start.15
  89.6 25.5 %copy-start.3 = (bf16[1,256,2048]{2,1,0:T(8,128)(2,1)S(1)}, bf16[1,256,2048]{2,1,0:T(8,128)(2,1)}, u32[]{:S(2)}) copy-start(bf16[1,256,2048]{2,1,0:T(8,128)(2,1)} %param.14) | copy-start | bytes 3145732
  109.2 0.8 copy-start
  110.0 18.0 %collective-permute-start.10 = (bf16[512,512]{1,0:T(8,128)(2,1)}, bf16[512,512]{1,0:T(8,128)(2,1)S(1)}, u32[]{:S(2)}, u32[]{:S(2)}) collective-permute-start(bf16[512,512]{1,0:T(8,128)(2,1)} %get-tuple-element.30), channel_id=1, source_target_pairs={{0,64},{1,17},{2,66},{3,19},{4,68},{5,21},{6,70},{7,23},{8,72},{9,... | collective-permute-start | bytes 1572872 | tf_op jit(solution)/shard_map/ppermute | solution.py:50
  111.7 16.4 %collective-permute-start.11 = (bf16[512,512]{1,0:T(8,128)(2,1)}, bf16[512,512]{1,0:T(8,128)(2,1)}, u32[]{:S(2)}, u32[]{:S(2)}) collective-permute-start(bf16[512,512]{1,0:T(8,128)(2,1)} %get-tuple-element.31), channel_id=1, source_target_pairs={{0,32},{1,9},{2,34},{3,11},{4,36},{5,13},{6,38},{7,15},{8,40},{9,1... | collective-permute-start | bytes 1572872 | tf_op jit(solution)/shard_map/ppermute | solution.py:50
  112.1 16.0 %collective-permute-start.9 = (bf16[512,512]{1,0:T(8,128)(2,1)}, bf16[512,512]{1,0:T(8,128)(2,1)}, u32[]{:S(2)}, u32[]{:S(2)}) collective-permute-start(bf16[512,512]{1,0:T(8,128)(2,1)} %get-tuple-element.29), channel_id=1, source_target_pairs={{0,96},{1,25},{2,98},{3,27},{4,100},{5,29},{6,102},{7,31},{8,104},... | collective-permute-start | bytes 1572872 | tf_op jit(solution)/shard_map/ppermute | solution.py:50
  128.0 0.8 copy-start.19
where the time goes:
time: 134 us; the launch traced here: 133 us
  Pallas kernels  46.6 us (35%)
  starting transfers between devices  30.4 us (23%)
  blocking collectives  22.3 us (17%)
  waiting for transfers between devices  17.5 us (13%)
  local copies, waits for them, and re-layouts  13.3 us (10%)
  other arithmetic  1.77 us (1%)
    ppermute x16, starting transfers between devices, send(): return lax.ppermute(value, ('dp', 'ctx'), pairs(step))  30.4 us
    all_gather x1, blocking collectives, shards(): hf = lax.all_gather(hf, 'dp', axis=0, tiled=True)  22.3 us
    pallas_call x1, Pallas kernels, short_attention(): pl.pallas_call(functools.partial(short_kernel, shifts), out_shape=[jax.Sh...  19.6 us
    ppermute x16, waiting for transfers between devices, send(): return lax.ppermute(value, ('dp', 'ctx'), pairs(step))  17.5 us
    unnamed x53, local copies, waits for them, and re-layouts  13.1 us
    pallas_call x1, Pallas kernels, long_attention(): pl.pallas_call(long_kernel, out_shape=jax.ShapeDtypeStruct((LROWS, QH * H...  13 us
    pallas_call x1, Pallas kernels, make_tables(): pl.pallas_call(table_kernel, out_shape=[ints(GROUPS * GROUPS), ints(GROUP...  3.94 us
    pallas_call x1, Pallas kernels, join(): pl.pallas_call(join_kernel, grid=(4,), out_shape=jax.ShapeDtypeStruct((RO...  3.85 us
  transfers between devices with their start and end apart: 16, of which 2 were waited for; matrix products, arithmetic and copies ran while one was open for 1% of the time, Pallas kernels for 30%

commit v1 on v0

--- a/solution.py
+++ b/solution.py
@@ -25,7 +25,7 @@
 
 VM = pl.BlockSpec(memory_space=pltpu.VMEM)
 SM = pl.BlockSpec(memory_space=pltpu.SMEM)
-HB = pl.BlockSpec(memory_space=pl.ANY)
+HB = pl.BlockSpec(memory_space=pltpu.HBM)
 
 
 def pairs(step):
@@ -79,56 +79,70 @@
     return (x, y, z, 1 - core)
 
 
-def split_kv_kernel(meta, k_ref, v_ref, *outs):
+def other_place(bit):
+    def step(x, y, z, core):
+        place = (x * SIDE + y) ^ bit
+        return (place // SIDE, place % SIDE, z, core)
+
+    return step
+
+
+def split_kernel(width, meta, *refs):
+    sources, outs, sems = refs[:-SIDE - 1], refs[-SIDE - 1 : -1], refs[-1]
+    copies = []
     for k in range(SIDE):
-        col = pl.multiple_of(((meta[0] + k) % SIDE) * HD, HD)
-        outs[k][:, :HD] = k_ref[:, pl.ds(col, HD)]
-        outs[k][:, HD:] = v_ref[:, pl.ds(col, HD)]
-
-
-def split_kv(meta, keys, values):
+        col = pl.multiple_of(((meta[0] + k) & 3) * width, width)
+        for n, source in enumerate(sources):
+            copies.append(
+                pltpu.make_async_copy(
+                    source.at[:, pl.ds(col, width)],
+                    outs[k].at[:, pl.ds(n * width, width)],
+                    sems.at[k, n],
+                )
+            )
+    for copy in copies:
+        copy.start()
+    for copy in copies:
+        copy.wait()
+
+
+def split_heads(meta, *sources):
+    width = sources[0].shape[1] // KVH
+    total = len(sources) * width
     return pl.pallas_call(
-        split_kv_kernel,
-        out_shape=[jax.ShapeDtypeStruct((ROWS, 2 * HD), jnp.bfloat16)] * SIDE,
-        in_specs=[SM, VM, VM],
-        out_specs=[VM] * SIDE,
-        cost_estimate=pl.CostEstimate(flops=0, bytes_accessed=2 * MIB, transcendentals=0),
-    )(meta, keys, values)
-
-
-def split_q_kernel(meta, q_ref, *outs):
+        functools.partial(split_kernel, width),
+        out_shape=[jax.ShapeDtypeStruct((ROWS, total), jnp.bfloat16)] * SIDE,
+        in_specs=[SM] + [HB] * len(sources),
+        out_specs=[HB] * SIDE,
+        scratch_shapes=[pltpu.SemaphoreType.DMA((SIDE, len(sources)))],
+        cost_estimate=pl.CostEstimate(
+            flops=0, bytes_accessed=SIDE * ROWS * total * 4, transcendentals=0
+        ),
+    )(meta, *sources)
+
+
+def join_kernel(meta, *refs):
+    pieces, out_ref, sems = refs[:SIDE], refs[SIDE], refs[SIDE + 1]
+    width = GROUP * HD
+    copies = []
     for k in range(SIDE):
-        col = pl.multiple_of(((meta[0] + k) % SIDE) * GROUP * HD, GROUP * HD)
-        outs[k][...] = q_ref[:, pl.ds(col, GROUP * HD)]
-
-
-def split_q(meta, queries):
-    width = GROUP * HD
-    return pl.pallas_call(
-        split_q_kernel,
-        grid=(4,),
-        out_shape=[jax.ShapeDtypeStruct((ROWS, width), jnp.bfloat16)] * SIDE,
-        in_specs=[SM, pl.BlockSpec((ROWS // 4, QH * HD), lambda i: (i, 0))],
-        out_specs=[pl.BlockSpec((ROWS // 4, width), lambda i: (i, 0))] * SIDE,
-        cost_estimate=pl.CostEstimate(flops=0, bytes_accessed=4 * MIB, transcendentals=0),
-    )(meta, queries)
-
-
-def join_kernel(meta, *refs):
-    out_ref = refs[-1]
-    for k in range(SIDE):
-        col = pl.multiple_of(((meta[0] + k) % SIDE) * GROUP * HD, GROUP * HD)
-        out_ref[:, pl.ds(col, GROUP * HD)] = refs[k][...]
+        col = pl.multiple_of(((meta[0] + k) & 3) * width, width)
+        copies.append(
+            pltpu.make_async_copy(pieces[k], out_ref.at[:, pl.ds(col, width)], sems.at[k])
+        )
+    for copy in copies:
+        copy.start()
+    for copy in copies:
+        copy.wait()
 
 
 def join(meta, pieces):
-    width = GROUP * HD
     return pl.pallas_call(
         join_kernel,
-        grid=(4,),
         out_shape=jax.ShapeDtypeStruct((ROWS, QH * HD), jnp.bfloat16),
-        in_specs=[SM] + [pl.BlockSpec((ROWS // 4, width), lambda i: (i, 0))] * SIDE,
-        out_specs=pl.BlockSpec((ROWS // 4, QH * HD), lambda i: (i, 0)),
+        in_specs=[SM] + [HB] * SIDE,
+        out_specs=HB,
+        scratch_shapes=[pltpu.SemaphoreType.DMA((SIDE,))],
         cost_estimate=pl.CostEstimate(flops=0, bytes_accessed=4 * MIB, transcendentals=0),
     )(meta, *pieces)
 
@@ -150,13 +164,14 @@
         own_head = jnp.where(core == 0, high, low)
         own_line = jnp.where(core == 0, low, high)
         base = (((line - own_line) & 3) * SIDE + ((head - own_head) & 3)) * SB
+        at = s ^ meta[3]
         for b in range(SB):
-            home = hf_ref[s, b]
+            home = hf_ref[at, b]
             rank = count_ref[home]
             count_ref[home] = rank + 1
-            rank_ref[s * SB + b] = rank
+            rank_ref[at * SB + b] = rank
             slot_ref[home * GROUPS + rank] = base + b
-            fill_ref[home * GROUPS + rank] = hf_ref[s, SB + b]
+            fill_ref[home * GROUPS + rank] = hf_ref[at, SB + b]
         return 0
 
     lax.fori_loop(0, GROUPS, source, 0)
@@ -191,20 +206,27 @@
 
 
 def short_kernel(shifts, meta, hf_ref, slot_ref, fill_ref, rank_ref, *refs):
-    kv_parts = refs[:SIDE]
-    q_refs = refs[SIDE : SIDE + len(shifts)]
-    out_refs = refs[SIDE + len(shifts) : SIDE + 2 * len(shifts)]
-    kv_ref, sems = refs[-2:]
+    count = len(shifts)
+    kv_parts = refs[1 : 1 + SIDE]
+    q_parts = refs[1 + SIDE : 1 + SIDE + count]
+    out_parts = refs[1 + SIDE + count : 1 + SIDE + 2 * count]
+    kv_ref, q_refs, out_refs, kv_sems, q_sems, out_sems = refs[-6:]
     part_rows = SIDE * ROWS
-    copies = [
+    kv_copies = [
         pltpu.make_async_copy(
-            kv_parts[j], kv_ref.at[pl.ds(j * part_rows, part_rows)], sems.at[j]
+            kv_parts[j], kv_ref.at[pl.ds(j * part_rows, part_rows)], kv_sems.at[j]
         )
         for j in range(SIDE)
     ]
-    for copy in copies:
+    q_copies = [
+        pltpu.make_async_copy(q_parts[n], q_refs.at[n], q_sems.at[n]) for n in range(count)
+    ]
+    out_copies = [
+        pltpu.make_async_copy(out_refs.at[n], out_parts[n], out_sems.at[n]) for n in range(count)
+    ]
+    for copy in kv_copies + q_copies:
         copy.start()
-    for copy in copies:
+    for copy in kv_copies:
         copy.wait()
     head, line, core = meta[0], meta[1], meta[2]
     width = CHUNK * BLOCK
@@ -214,9 +236,10 @@
     row = lax.broadcasted_iota(jnp.int32, (BLOCK, width), 0)
 
     for position, k in enumerate(shifts):
-        q_ref, out_ref = q_refs[position], out_refs[position]
+        q_ref, out_ref = q_refs.at[position], out_refs.at[position]
+        q_copies[position].wait()
         own_head = (head - k) & 3
-        own = jnp.where(core == 0, own_head * SIDE + line, line * SIDE + own_head)
+        own = jnp.where(core == 0, own_head * SIDE + line, line * SIDE + own_head) ^ meta[3]
 
         def one_block(b, _, q_ref=q_ref, out_ref=out_ref, own=own):
             home = hf_ref[own, b]
@@ -269,29 +292,42 @@
             return 0
 
         lax.fori_loop(0, SB, one_block, 0)
-
-
-def short_attention(shifts, meta, hf, tables, kv_parts, q_parts):
+        out_copies[position].start()
+    for copy in out_copies:
+        copy.wait()
+
+
+def short_attention(shifts, after, meta, hf, tables, kv_parts, q_parts):
     count = len(shifts)
     return pl.pallas_call(
         functools.partial(short_kernel, shifts),
         out_shape=[jax.ShapeDtypeStruct((ROWS, GROUP * HD), jnp.bfloat16)] * count,
-        in_specs=[SM] * 5 + [HB] * SIDE + [VM] * count,
-        out_specs=[VM] * count,
+        in_specs=[SM] * 5 + [HB] * (1 + SIDE + count),
+        out_specs=[HB] * count,
         scratch_shapes=[
             pltpu.VMEM((GROUPS * ROWS, 2 * HD), jnp.bfloat16),
+            pltpu.VMEM((count, ROWS, GROUP * HD), jnp.bfloat16),
+            pltpu.VMEM((count, ROWS, GROUP * HD), jnp.bfloat16),
             pltpu.SemaphoreType.DMA((SIDE,)),
+            pltpu.SemaphoreType.DMA((count,)),
+            pltpu.SemaphoreType.DMA((count,)),
         ],
         compiler_params=pltpu.CompilerParams(vmem_limit_bytes=32 * MIB),
         cost_estimate=pl.CostEstimate(
             flops=count * 700_000_000, bytes_accessed=4 * MIB, transcendentals=count * 1_300_000
         ),
-    )(meta, hf, *tables, *kv_parts, *q_parts)
+    )(meta, hf, *tables, after, *kv_parts, *q_parts)
 
 
 def long_kernel(doc_ref, q_ref, *refs):
-    parts = refs[:5]
-    out_ref, bias_ref = refs[5:]
+    out_hbm, kv_ref, query_ref, out_ref, bias_ref, sems = refs[5:]
+    copies = [pltpu.make_async_copy(refs[n], kv_ref.at[n], sems.at[n]) for n in range(5)]
+    copies.append(pltpu.make_async_copy(q_ref, query_ref, sems.at[5]))
+    for copy in copies:
+        copy.start()
+    for copy in copies:
+        copy.wait()
+    parts = [kv_ref.at[n] for n in range(5)]
     own_doc = doc_ref[...]
     lane = lax.broadcasted_iota(jnp.int32, (LROWS, LROWS), 1)
     row = lax.broadcasted_iota(jnp.int32, (LROWS, LROWS), 0)
@@ -309,20 +345,29 @@
         values = jnp.concatenate([p[:LROWS, pl.ds(vcol, HD)] for p in parts], axis=0)
         for i in range(GROUP):
             qcol = pl.multiple_of((h * GROUP + i) * HD, HD)
-            scores = inner(q_ref[:, pl.ds(qcol, HD)], keys) + bias_ref[...]
+            scores = inner(query_ref[:, pl.ds(qcol, HD)], keys) + bias_ref[...]
             out_ref[:, pl.ds(qcol, HD)] = soften(scores, values).astype(jnp.bfloat16)
         return 0
 
     lax.fori_loop(0, KVH, one_head, 0)
+    done = pltpu.make_async_copy(out_ref, out_hbm, sems.at[6])
+    done.start()
+    done.wait()
 
 
 def long_attention(docs, queries, parts):
     return pl.pallas_call(
         long_kernel,
         out_shape=jax.ShapeDtypeStruct((LROWS, QH * HD), jnp.bfloat16),
-        in_specs=[VM] * 7,
-        out_specs=VM,
-        scratch_shapes=[pltpu.VMEM((LROWS, 5 * LROWS), jnp.float32)],
+        in_specs=[VM] + [HB] * 6,
+        out_specs=HB,
+        scratch_shapes=[
+            pltpu.VMEM((5, LROWS + 16, 2 * KVH * HD), jnp.bfloat16),
+            pltpu.VMEM((LROWS, QH * HD), jnp.bfloat16),
+            pltpu.VMEM((LROWS, QH * HD), jnp.bfloat16),
+            pltpu.VMEM((LROWS, 5 * LROWS), jnp.float32),
+            pltpu.SemaphoreType.DMA((7,)),
+        ],
         compiler_params=pltpu.CompilerParams(vmem_limit_bytes=32 * MIB),
         cost_estimate=pl.CostEstimate(
             flops=2_700_000_000, bytes_accessed=5 * MIB, transcendentals=5_200_000
@@ -345,18 +390,19 @@
     core = rank % 2
     head = jnp.where(core == 0, place // SIDE, place % SIDE)
     line = jnp.where(core == 0, place % SIDE, place // SIDE)
-    meta = jnp.stack([head, line, core]).astype(jnp.int32)
-
-    kv_own = split_kv(meta, short_keys.reshape(ROWS, KVH * HD), short_values.reshape(ROWS, KVH * HD))
+    meta = jnp.stack([head, line, core, place]).astype(jnp.int32)
+
+    kv_own = split_heads(meta, short_keys.reshape(ROWS, KVH * HD), short_values.reshape(ROWS, KVH * HD))
     kv_line = [kv_own[0]] + [send(kv_own[k], along_head(k)) for k in (1, 2, 3)]
     kv_line = jnp.concatenate(kv_line, axis=0)
 
-    q_own = split_q(meta, short_queries.reshape(ROWS, QH * HD))
+    q_own = split_heads(meta, short_queries.reshape(ROWS, QH * HD))
     q_parts = [q_own[0]] + [send(q_own[k], along_head(k)) for k in (1, 2, 3)]
     kv_parts = [kv_line] + [send(kv_line, along_rows(k)) for k in (1, 2, 3)]
 
     hf = jnp.concatenate([block_home.reshape(1, SB), block_fill.reshape(1, SB)], axis=1)
-    hf = lax.all_gather(hf, "dp", axis=0, tiled=True)
+    for bit in (1, 2, 4, 8):
+        hf = jnp.concatenate([hf, send(hf, other_place(bit))], axis=0)
     tables = make_tables(meta, hf)
 
     docs = long_docs.reshape(1, LROWS).astype(jnp.float32) + 1.0
@@ -380,8 +426,13 @@
         [long_own, long_one, long_two, long_side, long_cross],
     )
 
-    mixed = short_attention((0, 1, 2, 3), meta, hf, tables, kv_parts, q_parts)
-    back = [mixed[0]] + [send(mixed[k], along_head(-k)) for k in (1, 2, 3)]
+    back = [None] * SIDE
+    for shifts in ((1, 3), (2, 0)):
+        mixed = short_attention(
+            shifts, long_out, meta, hf, tables, kv_parts, [q_parts[k] for k in shifts]
+        )
+        for k, piece in zip(shifts, mixed):
+            back[k] = send(piece, along_head(-k)) if k else piece
     short_out = join(meta, back)
     return short_out.reshape(short_queries.shape), long_out.reshape(long_queries.shape)
 

time: 134 us -> 280 us (2.09)
  Pallas kernels: 46.6 us -> 202 us
  blocking collectives: 22.3 us -> 0 us
  starting transfers between devices: 30.4 us -> 41.5 us
    pallas_call x3, Pallas kernels: 10 us -> 164 us  [the longest x2 99.1 us: split_heads(): pl.pallas_call(functools.partial(split_kernel, width), out_shape=[jax.Sha...]
    all_gather x1 -> x0, blocking collectives: 22.3 us -> none  [shards(): hf = lax.all_gather(hf, 'dp', axis=0, tiled=True)]
    ppermute x16 -> x20, starting transfers between devices: 30.4 us -> 41.5 us  [send(): return lax.ppermute(value, ('dp', 'ctx'), pairs(step))]
    unnamed x53 -> x49, local copies, waits for them, and re-layouts: 13.1 us -> 9.66 us
    ppermute x16 -> x20, waiting for transfers between devices: 17.5 us -> 19.8 us  [send(): return lax.ppermute(value, ('dp', 'ctx'), pairs(step))]
    pallas_call x1 -> x2, Pallas kernels: 19.6 us -> 20.1 us  [short_attention(): pl.pallas_call(functools.partial(short_kernel, shifts), out_shape=[jax.Sh...]
  transfers between devices with their start and end apart: 16 -> 20, of which waited for: 2 -> 5; matrix products, arithmetic and copies ran while one was open for 1% -> 1% of each run, Pallas kernels for 30% -> 49%
where the time goes in v1:
time: 280 us; the launch traced here: 279 us
  Pallas kernels  202 us (72%)
  starting transfers between devices  41.5 us (15%)
  waiting for transfers between devices  19.8 us (7%)
  local copies, waits for them, and re-layouts  11 us (4%)
  other arithmetic  4.39 us (2%)
    pallas_call x2, Pallas kernels, split_heads(): pl.pallas_call(functools.partial(split_kernel, width), out_shape=[jax.Sha...  99.1 us
    pallas_call x1, Pallas kernels, join(): pl.pallas_call(join_kernel, out_shape=jax.ShapeDtypeStruct((ROWS, QH * HD...  65.3 us
    ppermute x20, starting transfers between devices, send(): return lax.ppermute(value, ('dp', 'ctx'), pairs(step))  41.5 us
    pallas_call x2, Pallas kernels, short_attention(): pl.pallas_call(functools.partial(short_kernel, shifts), out_shape=[jax.Sh...  20.1 us
    ppermute x20, waiting for transfers between devices, send(): return lax.ppermute(value, ('dp', 'ctx'), pairs(step))  19.8 us
    pallas_call x1, Pallas kernels, long_attention(): pl.pallas_call(long_kernel, out_shape=jax.ShapeDtypeStruct((LROWS, QH * H...  13.1 us
    unnamed x49, local copies, waits for them, and re-layouts  9.66 us
  transfers between devices with their start and end apart: 20, of which 5 were waited for; matrix products, arithmetic and copies ran while one was open for 1% of the time, Pallas kernels for 49%

profile of v1, /device:TPU:0, one launch (start us, length us, event | category | flops | bytes accessed | tf_op | source)
XLA Modules:
  0.0 279.3 jit_solution(10492362531106251472)
XLA Ops:
  0.6 0.7 fusion.2
  1.3 1.9 fusion.1.refs_0_
  3.2 6.7 %collective-permute-start.5 = (bf16[272,1024]{1,0:T(8,128)(2,1)}, bf16[272,1024]{1,0:T(8,128)(2,1)}, u32[]{:S(2)}, u32[]{:S(2)}) collective-permute-start(bf16[272,1024]{1,0:T(8,128)(2,1)} %fusion.1.refs_0_), channel_id=1, source_target_pairs={{0,4},{1,5},{2,6},{3,7},{8,12},{9,13},{10,14},{11,15},{16,20},{17,... | collective-permute-start | bytes 1671176 | tf_op jit(solution)/shard_map/ppermute | solution.py:50
  9.9 3.7 %collective-permute-start.4 = (bf16[272,1024]{1,0:T(8,128)(2,1)}, bf16[272,1024]{1,0:T(8,128)(2,1)}, u32[]{:S(2)}, u32[]{:S(2)}) collective-permute-start(bf16[272,1024]{1,0:T(8,128)(2,1)} %fusion.1.refs_0_), channel_id=1, source_target_pairs={{0,2},{1,3},{2,4},{3,5},{4,6},{5,7},{8,10},{9,11},{10,12},{11,13},... | collective-permute-start | bytes 1671176 | tf_op jit(solution)/shard_map/ppermute | solution.py:50
  13.6 0.7 pad_add_fusion.4
  14.4 1.6 collective-permute-start
  16.0 0.6 pad_add_fusion.3.meta
  16.6 33.6 %shard_map.106 = (bf16[512,256]{1,0:T(8,128)(2,1)}, bf16[512,256]{1,0:T(8,128)(2,1)}, bf16[512,256]{1,0:T(8,128)(2,1)}, bf16[512,256]{1,0:T(8,128)(2,1)}) custom-call(s32[4]{0:T(128)} %pad_add_fusion.3.meta, bf16[512,512]{1,0:T(8,128)(2,1)} %bitcast.24, bf16[512,512]{1,0:T(8,128)(2,1)} %bitcast.25), custom_call_target="tpu_custom_call" | custom-call | bytes 2097152 | tf_op jit(solution)/shard_map/pallas_call | solution.py:112
  50.2 1.6 collective-permute-start.8
  51.9 2.9 %collective-permute-start.1 = (s32[2,16]{1,0:T(2,128)S(1)}, s32[2,16]{1,0:T(2,128)S(1)}, u32[]{:S(2)}, u32[]{:S(2)}) collective-permute-start(s32[2,16]{1,0:T(2,128)S(1)} %pad_add_fusion.2), channel_id=1, source_target_pairs={{0,16},{1,17},{2,18},{3,19},{4,20},{5,21},{6,22},{7,23},{8,24},{9,... | collective-permute-start | bytes 392 | tf_op jit(solution)/shard_map/ppermute | solution.py:50
  54.8 2.7 collective-permute-start.9
  57.6 1.0 collective-permute-start.2
  58.5 1.0 constant_dynamic-update-slice_fusion.3
  59.5 65.5 %shard_map.107 = (bf16[512,512]{1,0:T(8,128)(2,1)}, bf16[512,512]{1,0:T(8,128)(2,1)}, bf16[512,512]{1,0:T(8,128)(2,1)}, bf16[512,512]{1,0:T(8,128)(2,1)}) custom-call(s32[4]{0:T(128)} %pad_add_fusion.3.meta, bf16[512,2048]{1,0:T(8,128)(2,1)} %bitcast.18), custom_call_target="tpu_custom_call" | custom-call | bytes 4194304 | tf_op jit(solution)/shard_map/pallas_call | solution.py:112
  125.0 1.9 collective-permute-start.10
  126.9 0.1 pad_add_fusion
  127.0 1.4 collective-permute-start.14
  128.4 2.2 collective-permute-start.3
  130.7 1.3 collective-permute-done.10
  132.0 1.8 collective-permute-start.13
  133.8 6.4 %collective-permute-done.3 = s32[8,16]{1,0:T(8,128)S(1)} collective-permute-done((s32[8,16]{1,0:T(8,128)S(1)}, s32[8,16]{1,0:T(8,128)S(1)}, u32[]{:S(2)}, u32[]{:S(2)}) %collective-permute-start.3) | collective-permute-done | bytes 544 | tf_op jit(solution)/shard_map/ppermute | solution.py:50
  140.2 6.1 %collective-permute-start.12 = (bf16[2048,256]{1,0:T(8,128)(2,1)S(1)}, bf16[2048,256]{1,0:T(8,128)(2,1)S(1)}, u32[]{:S(2)}, u32[]{:S(2)}) collective-permute-start(bf16[2048,256]{1,0:T(8,128)(2,1)S(1)} %constant_dynamic-update-slice_fusion.refs_1_), channel_id=1, source_target_pairs={{0,16},{1,65},{2,18},{3,67},{4,20},{5,69},{6,22},{7,71},{8,24},{9,... | collective-permute-start | bytes 3145736 | tf_op jit(solution)/shard_map/ppermute | solution.py:50
  146.4 0.2 broadcast_select_fusion
  146.6 0.8 copy-done.2
  147.4 0.5 collective-permute-start.6
  147.9 2.2 collective-permute-done.7.refs_4_
  150.1 0.8 copy-done.11
  150.9 1.6 collective-permute-start.15
  152.4 0.8 copy-done.13
  153.2 2.2 collective-permute-start.16
  155.5 1.2 concatenate.31.hf_ref
  156.6 0.1 copy.11.doc_ref
  156.8 3.9 %shard_map.104 = (s32[256]{0:T(256)}, s32[256]{0:T(256)}, s32[128]{0:T(128)}) custom-call(s32[4]{0:T(128)} %pad_add_fusion.3.meta, s32[16,16]{1,0:T(8,128)} %concatenate.31.hf_ref), custom_call_target="tpu_custom_call" | custom-call | flops 4096 | bytes 4096 | tf_op jit(solution)/shard_map/pallas_call | solution.py:182
  160.8 1.2 copy-done.10
  162.0 1.1 copy-done.12
  163.0 1.1 copy-done.14
  164.1 13.1 %shard_map.105.refs_0_ = bf16[256,2048]{1,0:T(8,128)(2,1)} custom-call(f32[256,1]{1,0:T(8,128)S(1)} %copy.11.doc_ref, bf16[256,2048]{1,0:T(8,128)(2,1)S(1)} %bitcast.17, bf16[272,1024]{1,0:T(8,128)(2,1)} %fusion.1.refs_0_, bf16[272,1024]{1,0:T(8,128)(2,1)} %collective-permute-done.4.refs_1_, bf16[272,1024]{1,0:T(8,128)(2,1)} %collective-permute-done.5.refs_2_, ...), custom_call_target="tpu_custom_call" | custom-call | flops 2700000000 | bytes 5242880 | tf_op jit(solution)/shard_map/pallas_call | solution.py:359
  177.3 1.2 copy-done
  178.6 9.8 %shard_map.108 = (bf16[512,512]{1,0:T(8,128)(2,1)S(1)}, bf16[512,512]{1,0:T(8,128)(2,1)S(1)}) custom-call(s32[4]{0:T(128)S(1)} %copy-done.6, s32[16,16]{1,0:T(8,128)S(1)} %copy-done.5, s32[256]{0:T(256)S(1)} %copy-done.7, s32[256]{0:T(256)S(1)} %copy-done.8, s32[128]{0:T(128)S(1)} %copy-done.9, bf16[256,2048]{1,0:T(8,128)(2,1)S(1)} %copy-done, ...), custom_call_target="tpu_custom_call" | custom-call | flops 1400000000 | bytes 4194304 | tf_op jit(solution)/shard_map/pallas_call | solution.py:302
  188.4 0.8 copy-done.4
  189.2 1.5 collective-permute-start.18
  190.7 10.3 %shard_map.109 = (bf16[512,512]{1,0:T(8,128)(2,1)S(1)}, bf16[512,512]{1,0:T(8,128)(2,1)S(1)}) custom-call(s32[4]{0:T(128)S(1)} %copy-done.6, s32[16,16]{1,0:T(8,128)S(1)} %copy-done.5, s32[256]{0:T(256)S(1)} %copy-done.7, s32[256]{0:T(256)S(1)} %copy-done.8, s32[128]{0:T(128)S(1)} %copy-done.9, bf16[256,2048]{1,0:T(8,128)(2,1)S(1)} %copy-done, ...), custom_call_target="tpu_custom_call" | custom-call | flops 1400000000 | bytes 4194304 | tf_op jit(solution)/shard_map/pallas_call | solution.py:302
  201.0 1.6 collective-permute-start.17
  202.6 0.5 collective-permute-start.19
  203.1 7.1 %collective-permute-done.17.refs_1_ = bf16[512,512]{1,0:T(8,128)(2,1)S(1)} collective-permute-done((bf16[512,512]{1,0:T(8,128)(2,1)S(1)}, bf16[512,512]{1,0:T(8,128)(2,1)S(1)}, u32[]{:S(2)}, u32[]{:S(2)}) %collective-permute-start.17) | collective-permute-done | bytes 524320 | tf_op jit(solution)/shard_map/ppermute | solution.py:50
  210.2 2.8 collective-permute-done.19.refs_3_
  213.0 0.8 copy-done.19
  213.8 65.3 %shard_map.110 = bf16[512,2048]{1,0:T(8,128)(2,1)} custom-call(s32[4]{0:T(128)} %pad_add_fusion.3.meta, bf16[512,512]{1,0:T(8,128)(2,1)} %copy-done.4, bf16[512,512]{1,0:T(8,128)(2,1)} %copy-done.18, bf16[512,512]{1,0:T(8,128)(2,1)} %copy-done.17, bf16[512,512]{1,0:T(8,128)(2,1)} %copy-done.19), custom_call_target="tpu_custom_call" | custom-call | bytes 4194304 | tf_op jit(solution)/shard_map/pallas_call | solution.py:140
  (59 shorter events, 0.3 us)
Async XLA Ops:
  1.3 50.5 %copy-start.20 = (s32[1,1,8]{2,1,0:T(1,128)S(1)}, s32[1,1,8]{2,1,0:T(1,128)}, u32[]{:S(2)}) copy-start(s32[1,1,8]{2,1,0:T(1,128)} %param.12) | copy-start | bytes 100
  1.3 50.5 %copy-start.21 = (s32[1,1,8]{2,1,0:T(1,128)S(1)}, s32[1,1,8]{2,1,0:T(1,128)}, u32[]{:S(2)}) copy-start(s32[1,1,8]{2,1,0:T(1,128)} %param.13) | copy-start | bytes 100
  3.2 143.1 %collective-permute-start.5 = (bf16[272,1024]{1,0:T(8,128)(2,1)}, bf16[272,1024]{1,0:T(8,128)(2,1)}, u32[]{:S(2)}, u32[]{:S(2)}) collective-permute-start(bf16[272,1024]{1,0:T(8,128)(2,1)} %fusion.1.refs_0_), channel_id=1, source_target_pairs={{0,4},{1,5},{2,6},{3,7},{8,12},{9,13},{10,14},{11,15},{16,20},{17,... | collective-permute-start | bytes 1671176 | tf_op jit(solution)/shard_map/ppermute | solution.py:50
  9.9 137.5 %collective-permute-start.4 = (bf16[272,1024]{1,0:T(8,128)(2,1)}, bf16[272,1024]{1,0:T(8,128)(2,1)}, u32[]{:S(2)}, u32[]{:S(2)}) collective-permute-start(bf16[272,1024]{1,0:T(8,128)(2,1)} %fusion.1.refs_0_), channel_id=1, source_target_pairs={{0,2},{1,3},{2,4},{3,5},{4,6},{5,7},{8,10},{9,11},{10,12},{11,13},... | collective-permute-start | bytes 1671176 | tf_op jit(solution)/shard_map/ppermute | solution.py:50
  14.4 37.4 %collective-permute-start = (s32[1,16]{1,0:T(1,128)S(1)}, s32[1,16]{1,0:T(1,128)S(1)}, u32[]{:S(2)}, u32[]{:S(2)}) collective-permute-start(s32[1,16]{1,0:T(1,128)S(1)} %pad_add_fusion.4), channel_id=1, source_target_pairs={{0,8},{1,9},{2,10},{3,11},{4,12},{5,13},{6,14},{7,15},{8,0},{9,1},... | collective-permute-start | bytes 200 | tf_op jit(solution)/shard_map/ppermute | solution.py:50
  50.2 76.8 %collective-permute-start.8 = (bf16[512,256]{1,0:T(8,128)(2,1)}, bf16[512,256]{1,0:T(8,128)(2,1)S(1)}, u32[]{:S(2)}, u32[]{:S(2)}) collective-permute-start(bf16[512,256]{1,0:T(8,128)(2,1)} %get-tuple-element.21), channel_id=1, source_target_pairs={{0,32},{1,9},{2,34},{3,11},{4,36},{5,13},{6,38},{7,15},{8,40},{9,1... | collective-permute-start | bytes 786440 | tf_op jit(solution)/shard_map/ppermute | solution.py:50
  51.9 5.7 %collective-permute-start.1 = (s32[2,16]{1,0:T(2,128)S(1)}, s32[2,16]{1,0:T(2,128)S(1)}, u32[]{:S(2)}, u32[]{:S(2)}) collective-permute-start(s32[2,16]{1,0:T(2,128)S(1)} %pad_add_fusion.2), channel_id=1, source_target_pairs={{0,16},{1,17},{2,18},{3,19},{4,20},{5,21},{6,22},{7,23},{8,24},{9,... | collective-permute-start | bytes 392 | tf_op jit(solution)/shard_map/ppermute | solution.py:50
  54.8 73.6 %collective-permute-start.9 = (bf16[512,256]{1,0:T(8,128)(2,1)}, bf16[512,256]{1,0:T(8,128)(2,1)S(1)}, u32[]{:S(2)}, u32[]{:S(2)}) collective-permute-start(bf16[512,256]{1,0:T(8,128)(2,1)} %get-tuple-element.22), channel_id=1, source_target_pairs={{0,64},{1,17},{2,66},{3,19},{4,68},{5,21},{6,70},{7,23},{8,72},{9,... | collective-permute-start | bytes 786440 | tf_op jit(solution)/shard_map/ppermute | solution.py:50
  57.6 67.4 %collective-permute-start.2 = (s32[4,16]{1,0:T(4,128)S(1)}, s32[4,16]{1,0:T(4,128)S(1)}, u32[]{:S(2)}, u32[]{:S(2)}) collective-permute-start(s32[4,16]{1,0:T(4,128)S(1)} %pad_add_fusion.1), channel_id=1, source_target_pairs={{0,32},{1,33},{2,34},{3,35},{4,36},{5,37},{6,38},{7,39},{8,40},{9,... | collective-permute-start | bytes 776 | tf_op jit(solution)/shard_map/ppermute | solution.py:50
  59.5 65.5 %copy-start.22 = (bf16[512,256]{1,0:T(8,128)(2,1)S(1)}, bf16[512,256]{1,0:T(8,128)(2,1)}, u32[]{:S(2)}) copy-start(bf16[512,256]{1,0:T(8,128)(2,1)} %get-tuple-element.23) | copy-start | bytes 786436
  125.0 21.4 %copy-start.15 = (bf16[1,256,512]{2,1,0:T(8,128)(2,1)S(1)}, bf16[1,256,512]{2,1,0:T(8,128)(2,1)}, u32[]{:S(2)}) copy-start(bf16[1,256,512]{2,1,0:T(8,128)(2,1)} %param.16) | copy-start | bytes 786436
  125.0 21.4 %copy-start.16 = (bf16[1,256,512]{2,1,0:T(8,128)(2,1)S(1)}, bf16[1,256,512]{2,1,0:T(8,128)(2,1)}, u32[]{:S(2)}) copy-start(bf16[1,256,512]{2,1,0:T(8,128)(2,1)} %param.15) | copy-start | bytes 786436
  125.0 6.9 %collective-permute-start.10 = (bf16[512,256]{1,0:T(8,128)(2,1)S(1)}, bf16[512,256]{1,0:T(8,128)(2,1)S(1)}, u32[]{:S(2)}, u32[]{:S(2)}) collective-permute-start(bf16[512,256]{1,0:T(8,128)(2,1)S(1)} %copy-done.22), channel_id=1, source_target_pairs={{0,96},{1,25},{2,98},{3,27},{4,100},{5,29},{6,102},{7,31},{8,104},... | collective-permute-start | bytes 786440 | tf_op jit(solution)/shard_map/ppermute | solution.py:50
  127.0 19.6 %collective-permute-start.14 = (bf16[512,512]{1,0:T(8,128)(2,1)}, bf16[512,512]{1,0:T(8,128)(2,1)S(1)}, u32[]{:S(2)}, u32[]{:S(2)}) collective-permute-start(bf16[512,512]{1,0:T(8,128)(2,1)} %get-tuple-element.24), channel_id=1, source_target_pairs={{0,64},{1,17},{2,66},{3,19},{4,68},{5,21},{6,70},{7,23},{8,72},{9,... | collective-permute-start | bytes 1572872 | tf_op jit(solution)/shard_map/ppermute | solution.py:50
  128.4 11.8 %collective-permute-start.3 = (s32[8,16]{1,0:T(8,128)S(1)}, s32[8,16]{1,0:T(8,128)S(1)}, u32[]{:S(2)}, u32[]{:S(2)}) collective-permute-start(s32[8,16]{1,0:T(8,128)S(1)} %pad_add_fusion), channel_id=1, source_target_pairs={{0,64},{1,65},{2,66},{3,67},{4,68},{5,69},{6,70},{7,71},{8,72},{9,... | collective-permute-start | bytes 1544 | tf_op jit(solution)/shard_map/ppermute | solution.py:50
  132.0 45.3 %collective-permute-start.13 = (bf16[2048,256]{1,0:T(8,128)(2,1)S(1)}, bf16[2048,256]{1,0:T(8,128)(2,1)S(1)}, u32[]{:S(2)}, u32[]{:S(2)}) collective-permute-start(bf16[2048,256]{1,0:T(8,128)(2,1)S(1)} %constant_dynamic-update-slice_fusion.refs_1_), channel_id=1, source_target_pairs={{0,24},{1,97},{2,26},{3,99},{4,28},{5,101},{6,30},{7,103},{8,0},{9... | collective-permute-start | bytes 3145736 | tf_op jit(solution)/shard_map/ppermute | solution.py:50
  140.2 37.0 %collective-permute-start.12 = (bf16[2048,256]{1,0:T(8,128)(2,1)S(1)}, bf16[2048,256]{1,0:T(8,128)(2,1)S(1)}, u32[]{:S(2)}, u32[]{:S(2)}) collective-permute-start(bf16[2048,256]{1,0:T(8,128)(2,1)S(1)} %constant_dynamic-update-slice_fusion.refs_1_), channel_id=1, source_target_pairs={{0,16},{1,65},{2,18},{3,67},{4,20},{5,69},{6,22},{7,71},{8,24},{9,... | collective-permute-start | bytes 3145736 | tf_op jit(solution)/shard_map/ppermute | solution.py:50
  146.4 30.9 %collective-permute-start.11 = (bf16[2048,256]{1,0:T(8,128)(2,1)S(1)}, bf16[2048,256]{1,0:T(8,128)(2,1)}, u32[]{:S(2)}, u32[]{:S(2)}) collective-permute-start(bf16[2048,256]{1,0:T(8,128)(2,1)S(1)} %constant_dynamic-update-slice_fusion.refs_1_), channel_id=1, source_target_pairs={{0,8},{1,33},{2,10},{3,35},{4,12},{5,37},{6,14},{7,39},{8,16},{9,4... | collective-permute-start | bytes 3145736 | tf_op jit(solution)/shard_map/ppermute | solution.py:50
  146.6 0.8 copy-start.2
  147.4 2.7 collective-permute-start.7
  147.4 5.1 %collective-permute-start.6 = (bf16[272,1024]{1,0:T(8,128)(2,1)}, bf16[272,1024]{1,0:T(8,128)(2,1)S(1)}, u32[]{:S(2)}, u32[]{:S(2)}) collective-permute-start(bf16[272,1024]{1,0:T(8,128)(2,1)} %collective-permute-done.4.refs_1_), channel_id=1, source_target_pairs={{0,1},{1,0},{2,3},{3,2},{4,5},{5,4},{6,7},{7,6},{8,9},{9,8},{10,11... | collective-permute-start | bytes 1671176 | tf_op jit(solution)/shard_map/ppermute | solution.py:50
  150.1 0.8 copy-start.11
  150.9 39.8 %collective-permute-start.15 = (bf16[512,512]{1,0:T(8,128)(2,1)}, bf16[512,512]{1,0:T(8,128)(2,1)}, u32[]{:S(2)}, u32[]{:S(2)}) collective-permute-start(bf16[512,512]{1,0:T(8,128)(2,1)} %get-tuple-element.27), channel_id=1, source_target_pairs={{0,32},{1,9},{2,34},{3,11},{4,36},{5,13},{6,38},{7,15},{8,40},{9,1... | collective-permute-start | bytes 1572872 | tf_op jit(solution)/shard_map/ppermute | solution.py:50
  152.4 0.8 copy-start.13
  153.2 37.4 %collective-permute-start.16 = (bf16[512,512]{1,0:T(8,128)(2,1)}, bf16[512,512]{1,0:T(8,128)(2,1)}, u32[]{:S(2)}, u32[]{:S(2)}) collective-permute-start(bf16[512,512]{1,0:T(8,128)(2,1)} %get-tuple-element.28), channel_id=1, source_target_pairs={{0,96},{1,25},{2,98},{3,27},{4,100},{5,29},{6,102},{7,31},{8,104},... | collective-permute-start | bytes 1572872 | tf_op jit(solution)/shard_map/ppermute | solution.py:50
  160.7 1.2 copy-start.10
  162.0 1.1 copy-start.12
  163.0 1.1 copy-start.14
  164.1 13.2 %copy-start.1 = (bf16[512,512]{1,0:T(8,128)(2,1)S(1)}, bf16[512,512]{1,0:T(8,128)(2,1)}, u32[]{:S(2)}) copy-start(bf16[512,512]{1,0:T(8,128)(2,1)} %get-tuple-element.25.refs_6_) | copy-start | bytes 1572868
  164.1 13.2 %copy-start.3 = (bf16[512,512]{1,0:T(8,128)(2,1)S(1)}, bf16[512,512]{1,0:T(8,128)(2,1)}, u32[]{:S(2)}) copy-start(bf16[512,512]{1,0:T(8,128)(2,1)} %copy-done.2) | copy-start | bytes 1572868
  164.1 13.2 %copy-start.5 = (s32[16,16]{1,0:T(8,128)S(1)}, s32[16,16]{1,0:T(8,128)}, u32[]{:S(2)}) copy-start(s32[16,16]{1,0:T(8,128)} %concatenate.31.hf_ref) | copy-start | bytes 3076
  164.1 13.2 %copy-start.6 = (s32[4]{0:T(128)S(1)}, s32[4]{0:T(128)}, u32[]{:S(2)}) copy-start(s32[4]{0:T(128)} %pad_add_fusion.3.meta) | copy-start | bytes 52
  164.1 13.2 %copy-start.7 = (s32[256]{0:T(256)S(1)}, s32[256]{0:T(256)}, u32[]{:S(2)}) copy-start(s32[256]{0:T(256)} %get-tuple-element.17.slot_ref) | copy-start | bytes 3076
  164.1 13.2 %copy-start.8 = (s32[256]{0:T(256)S(1)}, s32[256]{0:T(256)}, u32[]{:S(2)}) copy-start(s32[256]{0:T(256)} %get-tuple-element.18.fill_ref) | copy-start | bytes 3076
  164.1 13.2 %copy-start.9 = (s32[128]{0:T(128)S(1)}, s32[128]{0:T(128)}, u32[]{:S(2)}) copy-start(s32[128]{0:T(128)} %get-tuple-element.19.rank_ref) | copy-start | bytes 1540
  177.3 1.2 copy-start
  188.4 0.8 copy-start.4
  189.2 13.9 %collective-permute-start.18 = (bf16[512,512]{1,0:T(8,128)(2,1)S(1)}, bf16[512,512]{1,0:T(8,128)(2,1)S(1)}, u32[]{:S(2)}, u32[]{:S(2)}) collective-permute-start(bf16[512,512]{1,0:T(8,128)(2,1)S(1)} %get-tuple-element.30), channel_id=1, source_target_pairs={{0,64},{1,17},{2,66},{3,19},{4,68},{5,21},{6,70},{7,23},{8,72},{9,... | collective-permute-start | bytes 1572872 | tf_op jit(solution)/shard_map/ppermute | solution.py:50
  201.0 9.2 %collective-permute-start.17 = (bf16[512,512]{1,0:T(8,128)(2,1)S(1)}, bf16[512,512]{1,0:T(8,128)(2,1)S(1)}, u32[]{:S(2)}, u32[]{:S(2)}) collective-permute-start(bf16[512,512]{1,0:T(8,128)(2,1)S(1)} %get-tuple-element.29), channel_id=1, source_target_pairs={{0,96},{1,25},{2,98},{3,27},{4,100},{5,29},{6,102},{7,31},{8,104},... | collective-permute-start | bytes 1572872 | tf_op jit(solution)/shard_map/ppermute | solution.py:50
  202.6 10.4 %collective-permute-start.19 = (bf16[512,512]{1,0:T(8,128)(2,1)S(1)}, bf16[512,512]{1,0:T(8,128)(2,1)S(1)}, u32[]{:S(2)}, u32[]{:S(2)}) collective-permute-start(bf16[512,512]{1,0:T(8,128)(2,1)S(1)} %get-tuple-element.31), channel_id=1, source_target_pairs={{0,32},{1,9},{2,34},{3,11},{4,36},{5,13},{6,38},{7,15},{8,40},{9,1... | collective-permute-start | bytes 1572872 | tf_op jit(solution)/shard_map/ppermute | solution.py:50
  203.1 9.9 %copy-start.17 = (bf16[512,512]{1,0:T(8,128)(2,1)}, bf16[512,512]{1,0:T(8,128)(2,1)S(1)}, u32[]{:S(2)}) copy-start(bf16[512,512]{1,0:T(8,128)(2,1)S(1)} %collective-permute-done.18.refs_2_) | copy-start | bytes 1572868
  210.2 2.8 copy-start.18
  213.0 0.8 copy-start.19

commit v2 on v0

v2 whole, which is shorter than its diff:
```python
import functools

import jax
import jax.numpy as jnp
from jax import lax
from jax.experimental import pallas as pl
from jax.experimental.pallas import tpu as pltpu
from jax.sharding import PartitionSpec as P

QH = 16
KVH = 4
HD = 128
BLOCK = 64
SB = 8
GROUP = QH // KVH
SIDE = 4
GROUPS = SIDE * SIDE
RANKS = 8
ROWS = SB * BLOCK
LROWS = 256
EXTRA = 16
PIECE = ROWS + EXTRA
KVW = 2 * HD
QW = GROUP * HD
CHUNK = 4
SET = 4
MASKED = -1e30
SCALE = HD**-0.5 * 1.4426950408889634
MIB = 1024 * 1024

VM = pl.BlockSpec(memory_space=pltpu.VMEM)
SM = pl.BlockSpec(memory_space=pltpu.SMEM)
HB = pl.BlockSpec(memory_space=pl.ANY)
FAR = pl.BlockSpec(memory_space=pltpu.HBM)


def pairs(step):
    found = []
    for x in range(SIDE):
        for y in range(SIDE):
            for z in range(RANKS // 2):
                for core in range(2):
                    target = step(x, y, z, core)
                    if target is not None:
                        tx, ty, tz, tcore = target
                        found.append(
                            (
                                (x * SIDE + y) * RANKS + z * 2 + core,
                                (tx * SIDE + ty) * RANKS + tz * 2 + tcore,
                            )
                        )
    return found


def send(value, step):
    return lax.ppermute(value, ("dp", "ctx"), pairs(step))


def along_head(k):
    def step(x, y, z, core):
        if core == 0:
            return (x + k) % SIDE, y, z, core
        return x, (y + k) % SIDE, z, core

    return step


def along_rows(k):
    def step(x, y, z, core):
        if core == 0:
            return x, (y + k) % SIDE, z, core
        return (x + k) % SIDE, y, z, core

    return step


def up_chips(k):
    def step(x, y, z, core):
        return (x, y, z + k, core) if z + k < RANKS // 2 else None

    return step


def other_core(x, y, z, core):
    return x, y, z, 1 - core


def where_am_i():
    place, rank = lax.axis_index("dp"), lax.axis_index("ctx")
    x, y, core = lax.shift_right_logical(place, 2), place & 3, rank & 1
    return jnp.where(core == 0, x, y), jnp.where(core == 0, y, x), core


def busy(us):
    return pl.CostEstimate(flops=int(us * 1e9), bytes_accessed=MIB, transcendentals=0)


def split_kernel(home_in, fill_in, doc_in, k_ref, v_ref, q_ref, lk_ref, lv_ref, *refs):
    outs, own, packed = refs[: SIDE - 1], refs[SIDE - 1], refs[SIDE]
    home, fill, docs, sems, few_sems = refs[SIDE + 1 :]
    mine = where_am_i()[0]
    few = [
        pltpu.make_async_copy(source, to, few_sems.at[n])
        for n, (source, to) in enumerate(((home_in, home), (fill_in, fill), (doc_in, docs)))
    ]
    copies = []
    for k in range(SIDE):
        head = (mine + k) & 3
        col = pl.multiple_of(head * HD, HD)
        out = own if k == 0 else outs[k - 1]
        moves = [(k_ref, col, HD, 0), (v_ref, col, HD, HD)]
        if k > 0:
            moves.append((q_ref, pl.multiple_of(head * QW, QW), QW, KVW))
        for n, (source, at, wide, to) in enumerate(moves):
            copies.append(
                pltpu.make_async_copy(
                    source.at[:, pl.ds(at, wide)],
                    out.at[pl.ds(0, ROWS), pl.ds(to, wide)],
                    sems.at[k, n],
                )
            )
    wide = KVH * HD
    for n, source in enumerate((lk_ref, lv_ref)):
        to = packed.at[pl.ds(0, LROWS), pl.ds(n * wide, wide)]
        copies.append(pltpu.make_async_copy(source, to, sems.at[SIDE, n]))
    for copy in few + copies:
        copy.start()
    for copy in few:
        copy.wait()
    row = lax.broadcasted_iota(jnp.int32, (EXTRA, KVW), 0)
    facts = jnp.zeros((EXTRA, KVW), jnp.int32)
    for b in range(SB):
        facts = jnp.where(row == b, home[b], facts)
        facts = jnp.where(row == SB + b, fill[b], facts)
    facts = facts.astype(jnp.float32).astype(jnp.bfloat16)
    own[ROWS:, :] = facts
    for out in outs:
        out[ROWS:, :KVW] = facts
        out[ROWS:, KVW:] = jnp.zeros((EXTRA, QW), jnp.bfloat16)
    doc_row = docs[...].astype(jnp.float32) + 1.0
    packed[LROWS:, :LROWS] = jnp.broadcast_to(doc_row, (EXTRA, LROWS)).astype(jnp.bfloat16)
    packed[LROWS:, LROWS:] = jnp.zeros((EXTRA, 2 * wide - LROWS), jnp.bfloat16)
    for copy in copies:
        copy.wait()


def split(home, fill, docs, keys, values, queries, long_keys, long_values):
    shapes = [jax.ShapeDtypeStruct((PIECE, KVW + QW), jnp.bfloat16)] * (SIDE - 1)
    shapes += [
        jax.ShapeDtypeStruct((PIECE, KVW), jnp.bfloat16),
        jax.ShapeDtypeStruct((LROWS + EXTRA, 2 * KVH * HD), jnp.bfloat16),
    ]
    return pl.pallas_call(
        split_kernel,
        out_shape=shapes,
        in_specs=[FAR] * 8,
        out_specs=[VM] * (SIDE + 1),
        scratch_shapes=[
            pltpu.SMEM((SB,), jnp.int32),
            pltpu.SMEM((SB,), jnp.int32),
            pltpu.VMEM((1, LROWS), jnp.int32),
            pltpu.SemaphoreType.DMA((SIDE + 1, 3)),
            pltpu.SemaphoreType.DMA((3,)),
        ],
        compiler_params=pltpu.CompilerParams(vmem_limit_bytes=60 * MIB),
        cost_estimate=busy(2),
    )(home, fill, docs, keys, values, queries, long_keys, long_values)


def stack_kernel(*refs):
    for n in range(SIDE):
        refs[-1][n * PIECE : (n + 1) * PIECE] = refs[n][:, :KVW]


def stack(pieces):
    return pl.pallas_call(
        stack_kernel,
        out_shape=jax.ShapeDtypeStruct((SIDE * PIECE, KVW), jnp.bfloat16),
        in_specs=[VM] * SIDE,
        out_specs=VM,
        compiler_params=pltpu.CompilerParams(vmem_limit_bytes=2 * MIB),
        cost_estimate=busy(1),
    )(*pieces)


def join_kernel(*refs):
    pieces, out_ref, sems = refs[:SIDE], refs[SIDE], refs[SIDE + 1]
    mine = where_am_i()[0]
    copies = []
    for k in range(SIDE):
        col = pl.multiple_of(((mine + k) & 3) * QW, QW)
        copies.append(
            pltpu.make_async_copy(pieces[k], out_ref.at[:, pl.ds(col, QW)], sems.at[k])
        )
    for copy in copies:
        copy.start()
    for copy in copies:
        copy.wait()


def join(pieces):
    return pl.pallas_call(
        join_kernel,
        out_shape=jax.ShapeDtypeStruct((ROWS, QH * HD), jnp.bfloat16),
        in_specs=[VM] * SIDE,
        out_specs=FAR,
        scratch_shapes=[pltpu.SemaphoreType.DMA((SIDE,))],
        compiler_params=pltpu.CompilerParams(vmem_limit_bytes=MIB),
        cost_estimate=busy(2),
    )(*pieces)


def fill_table(kv_ref, table_ref):
    head, line, core = where_am_i()
    shape = (GROUPS, HD)
    lane = lax.broadcasted_iota(jnp.int32, shape, 1)
    row = lax.broadcasted_iota(jnp.int32, shape, 0)
    facts = jnp.full(shape, -1.0, jnp.float32)
    for p in range(GROUPS):
        piece = kv_ref[p * PIECE + ROWS : (p + 1) * PIECE, :HD].astype(jnp.float32)
        facts = jnp.where(lane == p, piece, facts)
    facts = facts.astype(jnp.int32)

    def order(p):
        own_head = (head - p) & 3
        own_line = (line - lax.shift_right_logical(p, 2)) & 3
        return jnp.where(core == 0, own_head * SIDE + own_line, own_line * SIDE + own_head)

    one = lax.broadcasted_iota(jnp.int32, (HD, HD), 0)
    two = lax.broadcasted_iota(jnp.int32, (HD, HD), 1)
    earlier = jnp.where((order(one) < order(two)) & (one < GROUPS), 1.0, 0.0)
    here = jnp.zeros(shape, jnp.float32)
    slots = jnp.zeros(shape, jnp.int32)
    fills = jnp.zeros(shape, jnp.int32)
    for b in range(SB):
        same = facts[b : b + 1] == row
        here = jnp.where(same, 1.0, here)
        slots = jnp.where(same, lane * (PIECE // EXTRA) + b * (BLOCK // EXTRA), slots)
        fills = jnp.where(same, facts[SB + b : SB + b + 1], fills)
    ranks = jnp.dot(here, earlier, preferred_element_type=jnp.float32).astype(jnp.int32)
    own_rows = lax.broadcasted_iota(jnp.int32, (SB, HD), 0)
    own_ranks = jnp.zeros((SB, HD), jnp.int32)
    for d in range(GROUPS):
        own_ranks = jnp.where(facts[:SB] == d, ranks[d : d + 1], own_ranks)
    place = jnp.zeros((SB, HD), jnp.int32)
    for b in range(SB):
        other = own_ranks[b : b + 1]
        ahead = (other > own_ranks) | ((other == own_ranks) & (own_rows > b))
        place = place + jnp.where(ahead, 1, 0)
    listed = [jnp.zeros((SB, HD), jnp.int32) for _ in range(4)]
    for b in range(SB):
        chosen = place[b : b + 1] == own_rows
        found = (b, facts[b : b + 1], facts[SB + b : SB + b + 1], own_ranks[b : b + 1])
        listed = [jnp.where(chosen, new, old) for new, old in zip(found, listed)]
    for n in range(4):
        table_ref[n * SB : (n + 1) * SB] = listed[n]
    ranks = jnp.where(here > 0.0, ranks, -1)
    slot_list = jnp.zeros(shape, jnp.int32)
    fill_list = jnp.zeros(shape, jnp.int32)
    for r in range(GROUPS):
        chosen = ranks == r
        slot = jnp.sum(jnp.where(chosen, slots, 0), axis=1, keepdims=True)
        fill = jnp.sum(jnp.where(chosen, fills, 0), axis=1, keepdims=True)
        slot_list = jnp.where(lane == r, slot, slot_list)
        fill_list = jnp.where(lane == r, fill, fill_list)
    table_ref[4 * SB : 4 * SB + GROUPS] = slot_list
    table_ref[4 * SB + GROUPS :] = fill_list


def soften(scores, value_rows):
    row_max = jnp.max(scores, axis=-1, keepdims=True)
    weights = jnp.exp2((scores - row_max) * SCALE)
    totals = jnp.sum(weights, axis=-1, keepdims=True)
    mixture = jnp.dot(
        weights.astype(jnp.bfloat16), value_rows, preferred_element_type=jnp.float32
    )
    return mixture / totals


def inner(queries, key_rows):
    return lax.dot_general(
        queries, key_rows, (((1,), (1,)), ((), ())), preferred_element_type=jnp.float32
    )


def short_kernel(shifts, first, waits, q_all, *refs):
    count = len(shifts)
    line_parts, kv_parts = refs[: SIDE - 1], refs[SIDE - 1 : 2 * SIDE - 1]
    refs = refs[2 * SIDE - 1 + waits :]
    if first:
        out_parts, table = refs[:count], refs[count]
        table_ref, table_sem = refs[-2:]
        refs = refs[count + 1 :]
    else:
        table, out_parts = refs[0], refs[1 : 1 + count]
        refs = refs[1 + count :]
    kv_ref, q_ref, out_ref, mix_ref, top_ref, kv_sems, q_sems = refs[:7]
    col = pl.multiple_of(where_am_i()[0] * QW, QW)
    wanted = [
        line_parts[k - 1].at[pl.ds(0, ROWS), pl.ds(KVW, QW)] if k else q_all.at[:, pl.ds(col, QW)]
        for k in shifts
    ]
    part_rows = SIDE * PIECE
    copies = [
        pltpu.make_async_copy(
            kv_parts[n], kv_ref.at[pl.ds(n * part_rows, part_rows)], kv_sems.at[n]
        )
        for n in range(SIDE)
    ]
    copies += [
        pltpu.make_async_copy(source, q_ref.at[pl.ds(n * ROWS, ROWS)], q_sems.at[n])
        for n, source in enumerate(wanted)
    ]
    for copy in copies:
        copy.start()
    for copy in copies:
        copy.wait()
    if first:
        fill_table(kv_ref, table_ref)
        table_copy = pltpu.make_async_copy(table_ref, table, table_sem)
        table_copy.start()
        table_copy.wait()
    width = CHUNK * BLOCK
    lane = lax.broadcasted_iota(jnp.int32, (BLOCK, width), 1)
    lane_block = lane // BLOCK
    lane_row = lane % BLOCK
    row = lax.broadcasted_iota(jnp.int32, (BLOCK, width), 0)
    ones = jnp.ones((width, HD), jnp.bfloat16)

    def one_set(t, _):
        piece = t // (SB // SET)
        k = piece + shifts[0]
        base = (t % (SB // SET)) * SET

        def fact(n, u):
            return table[n * SB + base + u, k]

        def rows_of(u):
            return pl.ds(pl.multiple_of(piece * ROWS + fact(0, u) * BLOCK, BLOCK), BLOCK)

        def scores_of(u, c):
            home, rank = fact(1, u), fact(3, u)
            q = q_ref[rows_of(u), :]
            q = jnp.concatenate([q[:, h * HD : (h + 1) * HD] for h in range(GROUP)], axis=0)
            limits, keys, values = [], [], []
            for j in range(CHUNK):
                n = c * CHUNK + j
                start = pl.multiple_of(table[4 * SB + home, n] * EXTRA, EXTRA)
                kv = kv_ref[pl.ds(start, BLOCK), :]
                keys.append(kv[:, :HD])
                values.append(kv[:, HD:])
                limits.append(jnp.where(n <= rank, table[4 * SB + GROUPS + home, n], 0))
            limit = jnp.where(
                lane_block < 2,
                jnp.where(lane_block == 0, limits[0], limits[1]),
                jnp.where(lane_block == 2, limits[2], limits[3]),
            )
            causal = jnp.where(lane_block == rank - c * CHUNK, row + 1, BLOCK)
            bias = jnp.where(lane_row < jnp.minimum(limit, causal), 0.0, MASKED)
            scores = inner(q, jnp.concatenate(keys, axis=0))
            scores = scores + jnp.concatenate([bias] * GROUP, axis=0)
            values = jnp.concatenate([jnp.concatenate(values, axis=0), ones], axis=1)
            return scores, values

        def weigh(scores, top, values):
            weights = jnp.exp2((scores - top) * SCALE).astype(jnp.bfloat16)
            return jnp.dot(weights, values, preferred_element_type=jnp.float32)

        for u in range(SET):
            scores, values = scores_of(u, 0)
            top = jnp.max(scores, axis=-1, keepdims=True)
            top_ref[u] = jnp.broadcast_to(top, (GROUP * BLOCK, HD))
            mix_ref[u] = weigh(scores, top, values)

        def later(c, _):
            for u in range(SET):
                scores, values = scores_of(u, c)
                old = top_ref[u]
                top = jnp.broadcast_to(jnp.max(scores, axis=-1, keepdims=True), old.shape)
                top = jnp.maximum(old, top)
                top_ref[u] = top
                shrink = jnp.exp2((old - top) * SCALE)
                shrink = jnp.concatenate([shrink, shrink], axis=1)
                mix_ref[u] = mix_ref[u] * shrink + weigh(scores, jnp.concatenate([top, top], axis=1), values)
            return 0

        lax.fori_loop(1, fact(3, 0) // CHUNK + 1, later, 0)
        for u in range(SET):
            mixed = mix_ref[u]
            mixed = mixed[:, :HD] / mixed[:, HD:]
            used = row[:, :HD] < fact(2, u)
            for h in range(GROUP):
                part = jnp.where(used, mixed[h * BLOCK : (h + 1) * BLOCK], 0.0)
                out_ref[rows_of(u), h * HD : (h + 1) * HD] = part.astype(jnp.bfloat16)
        return 0

    lax.fori_loop(0, count * (SB // SET), one_set, 0)
    for n in range(count):
        out_parts[n][...] = out_ref[n * ROWS : (n + 1) * ROWS]


def short_attention(shifts, table, after, queries, line_parts, kv_parts):
    count = len(shifts)
    first = table is None
    outs = [jax.ShapeDtypeStruct((ROWS, QW), jnp.bfloat16)] * count
    scratch = [
        pltpu.VMEM((GROUPS * PIECE, KVW), jnp.bfloat16),
        pltpu.VMEM((count * ROWS, QW), jnp.bfloat16),
        pltpu.VMEM((count * ROWS, QW), jnp.bfloat16),
        pltpu.VMEM((SET, GROUP * BLOCK, 2 * HD), jnp.float32),
        pltpu.VMEM((SET, GROUP * BLOCK, HD), jnp.float32),
        pltpu.SemaphoreType.DMA((SIDE,)),
        pltpu.SemaphoreType.DMA((count,)),
    ]
    if first:
        outs = outs + [jax.ShapeDtypeStruct((4 * GROUPS, HD), jnp.int32)]
        scratch += [pltpu.VMEM((4 * GROUPS, HD), jnp.int32), pltpu.SemaphoreType.DMA(())]
    found = pl.pallas_call(
        functools.partial(short_kernel, shifts, first, len(after)),
        out_shape=outs,
        in_specs=[FAR]
        + [HB] * (2 * SIDE - 1)
        + [SM if first else HB] * len(after)
        + ([] if first else [SM]),
        out_specs=[VM] * count + ([SM] if first else []),
        scratch_shapes=scratch,
        compiler_params=pltpu.CompilerParams(vmem_limit_bytes=24 * MIB),
        cost_estimate=busy(4 * count),
    )(queries, *line_parts, *kv_parts, *after, *([] if first else [table]))
    return (found[:count], found[count]) if first else (found, table)


def long_kernel(q_in, *refs):
    parts = refs[:5]
    out_ref, token, q_ref, bias_ref, sem = refs[5:]
    copy = pltpu.make_async_copy(q_in, q_ref, sem)
    copy.start()
    token[0] = 0
    square = (LROWS, LROWS)
    lane = lax.broadcasted_iota(jnp.int32, square, 1)
    row = lax.broadcasted_iota(jnp.int32, square, 0)
    docs = [p[LROWS : LROWS + EXTRA, :LROWS].astype(jnp.float32)[:1] for p in parts]
    own_doc = jnp.transpose(jnp.broadcast_to(docs[0], square))
    for n in range(5):
        allowed = own_doc == docs[n]
        if n == 0:
            allowed = allowed & (lane <= row)
        bias_ref[:, n * LROWS : (n + 1) * LROWS] = jnp.where(allowed, 0.0, MASKED)
    copy.wait()

    def one_head(h, _):
        col = pl.multiple_of(h * HD, HD)
        vcol = pl.multiple_of((KVH + h) * HD, HD)
        keys = jnp.concatenate([p[:LROWS, pl.ds(col, HD)] for p in parts], axis=0)
        values = jnp.concatenate([p[:LROWS, pl.ds(vcol, HD)] for p in parts], axis=0)
        for i in range(GROUP):
            qcol = pl.multiple_of((h * GROUP + i) * HD, HD)
            scores = inner(q_ref[:, pl.ds(qcol, HD)], keys) + bias_ref[...]
            out_ref[:, pl.ds(qcol, HD)] = soften(scores, values).astype(jnp.bfloat16)
        return 0

    lax.fori_loop(0, KVH, one_head, 0)


def long_attention(queries, parts):
    return pl.pallas_call(
        long_kernel,
        out_shape=[
            jax.ShapeDtypeStruct((LROWS, QH * HD), jnp.bfloat16),
            jax.ShapeDtypeStruct((1,), jnp.int32),
        ],
        in_specs=[FAR] + [VM] * 5,
        out_specs=[VM, SM],
        scratch_shapes=[
            pltpu.VMEM((LROWS, QH * HD), jnp.bfloat16),
            pltpu.VMEM((LROWS, 5 * LROWS), jnp.float32),
            pltpu.SemaphoreType.DMA(()),
        ],
        compiler_params=pltpu.CompilerParams(vmem_limit_bytes=20 * MIB),
        cost_estimate=busy(0.1),
    )(queries, *parts)


def shards(
    short_queries,
    short_keys,
    short_values,
    block_fill,
    block_home,
    long_queries,
    long_keys,
    long_values,
    long_docs,
):
    queries = short_queries.reshape(ROWS, QH * HD)
    *own, own_kv, packed = split(
        block_home.reshape(SB),
        block_fill.reshape(SB),
        long_docs.reshape(1, LROWS),
        short_keys.reshape(ROWS, KVH * HD),
        short_values.reshape(ROWS, KVH * HD),
        queries,
        long_keys.reshape(LROWS, KVH * HD),
        long_values.reshape(LROWS, KVH * HD),
    )
    line_parts = [send(own[k - 1], along_head(k)) for k in (1, 2, 3)]
    long_one = send(packed, up_chips(1))
    long_two = send(packed, up_chips(2))
    stacked = stack([own_kv] + line_parts)
    kv_parts = [stacked] + [send(stacked, along_rows(k)) for k in (1, 2, 3)]
    long_side = send(long_one, other_core)
    core = lax.axis_index("ctx") % 2
    long_cross = send(jnp.where(core == 0, packed, long_two), other_core)
    long_out, token = long_attention(
        long_queries.reshape(LROWS, QH * HD),
        [packed, long_one, long_two, long_side, long_cross],
    )

    mixed, table = short_attention((1, 2, 3), None, [token], queries, line_parts, kv_parts)
    back = [send(piece, along_head(-k)) for k, piece in zip((1, 2, 3), mixed)]
    kept, _ = short_attention((0,), table, [], queries, line_parts, kv_parts)
    short_out = join([kept[0]] + back)
    return short_out.reshape(short_queries.shape), long_out.reshape(long_queries.shape)


def solution(mesh):
    return jax.shard_map(
        shards,
        mesh=mesh,
        in_specs=(
            P("dp", "ctx", None, None),
            P("dp", "ctx", None, None),
            P("dp", "ctx", None, None),
            P("dp", "ctx", None),
            P("dp", "ctx", None),
            P("dp", "ctx", None),
            P("dp", "ctx", None),
            P("dp", "ctx", None),
            P("dp", "ctx"),
        ),
        out_specs=(P("dp", "ctx", None, None), P("dp", "ctx", None)),
        check_vma=False,
    )
```

time: 134 us -> 95.5 us (0.71)
  blocking collectives: 22.3 us -> 0 us
  waiting for transfers between devices: 17.5 us -> 30.3 us
  local copies, waits for them, and re-layouts: 13.3 us -> 2.76 us
  Pallas kernels: 46.6 us -> 37.7 us
  starting transfers between devices: 30.4 us -> 23.5 us
  other arithmetic: 1.77 us -> 0.06 us
    all_gather x1 -> x0, blocking collectives: 22.3 us -> none  [shards(): hf = lax.all_gather(hf, 'dp', axis=0, tiled=True)]
    ppermute x16 -> x13, waiting for transfers between devices: 17.5 us -> 30.3 us  [send(): return lax.ppermute(value, ('dp', 'ctx'), pairs(step))]
    unnamed x53 -> x20, local copies, waits for them, and re-layouts: 13.1 us -> 2.76 us
    pallas_call x6, Pallas kernels: 46.6 us -> 37.7 us  [the longest x2 19.6 us: short_attention(): pl.pallas_call(functools.partial(short_kernel, shifts, first, len(after))...]
    ppermute x16 -> x13, starting transfers between devices: 30.4 us -> 23.5 us  [send(): return lax.ppermute(value, ('dp', 'ctx'), pairs(step))]
  transfers between devices with their start and end apart: 16 -> 13, of which waited for: 2 -> 8; matrix products, arithmetic and copies ran while one was open for 1% -> 0% of each run, Pallas kernels for 30% -> 18%
where the time goes in v2:
time: 95.5 us; the launch traced here: 95.1 us
  Pallas kernels  37.7 us (39%)
  waiting for transfers between devices  30.3 us (32%)
  starting transfers between devices  23.5 us (25%)
  local copies, waits for them, and re-layouts  2.76 us (3%)
    ppermute x13, waiting for transfers between devices, send(): return lax.ppermute(value, ('dp', 'ctx'), pairs(step))  30.3 us
    ppermute x13, starting transfers between devices, send(): return lax.ppermute(value, ('dp', 'ctx'), pairs(step))  23.5 us
    pallas_call x2, Pallas kernels, short_attention(): pl.pallas_call(functools.partial(short_kernel, shifts, first, len(after))...  19.6 us
    pallas_call x1, Pallas kernels, long_attention(): pl.pallas_call(long_kernel, out_shape=[jax.ShapeDtypeStruct((LROWS, QH *...  12.9 us
    pallas_call x1, Pallas kernels, split(): pl.pallas_call(split_kernel, out_shape=shapes, in_specs=[FAR] * 8, out_sp...  3.85 us
    unnamed x20, local copies, waits for them, and re-layouts  2.76 us
  transfers between devices with their start and end apart: 13, of which 8 were waited for; matrix products, arithmetic and copies ran while one was open for 0% of the time, Pallas kernels for 18%

profile of v2, /device:TPU:0, one launch (start us, length us, event | category | flops | bytes accessed | tf_op | source)
XLA Modules:
  0.0 95.1 jit_solution(4222574048439157608)
XLA Ops:
  0.6 3.8 %shard_map.104 = (bf16[528,768]{1,0:T(8,128)(2,1)}, bf16[528,768]{1,0:T(8,128)(2,1)}, bf16[528,768]{1,0:T(8,128)(2,1)}, bf16[528,256]{1,0:T(8,128)(2,1)}, bf16[272,1024]{1,0:T(8,128)(2,1)}) custom-call(s32[8]{0:T(128)} %bitcast.19, s32[8]{0:T(128)} %bitcast.20, s32[1,256]{1,0:T(1,128)} %doc_in.1, bf16[512,512]{1,0:T(8,128)(2,1)} %bitcast.15, ...), custom_call_target="tpu_custom_call" | custom-call | flops 2000000000 | bytes 1048576 | tf_op jit(solution)/shard_map/pallas_call | solution.py:153
  4.5 1.6 %collective-permute-start = (bf16[528,768]{1,0:T(8,128)(2,1)}, bf16[528,768]{1,0:T(8,128)(2,1)S(1)}, u32[]{:S(2)}, u32[]{:S(2)}) collective-permute-start(bf16[528,768]{1,0:T(8,128)(2,1)} %get-tuple-element.13), channel_id=1, source_target_pairs={{0,32},{1,9},{2,34},{3,11},{4,36},{5,13},{6,38},{7,15},{8,40},{9,1... | collective-permute-start | bytes 2433032 | tf_op jit(solution)/shard_map/ppermute | solution.py:56
  6.1 2.7 %collective-permute-start.1 = (bf16[528,768]{1,0:T(8,128)(2,1)}, bf16[528,768]{1,0:T(8,128)(2,1)S(1)}, u32[]{:S(2)}, u32[]{:S(2)}) collective-permute-start(bf16[528,768]{1,0:T(8,128)(2,1)} %get-tuple-element.14), channel_id=1, source_target_pairs={{0,64},{1,17},{2,66},{3,19},{4,68},{5,21},{6,70},{7,23},{8,72},{9,... | collective-permute-start | bytes 2433032 | tf_op jit(solution)/shard_map/ppermute | solution.py:56
  8.9 1.4 %collective-permute-start.2 = (bf16[528,768]{1,0:T(8,128)(2,1)}, bf16[528,768]{1,0:T(8,128)(2,1)S(1)}, u32[]{:S(2)}, u32[]{:S(2)}) collective-permute-start(bf16[528,768]{1,0:T(8,128)(2,1)} %get-tuple-element.15), channel_id=1, source_target_pairs={{0,96},{1,25},{2,98},{3,27},{4,100},{5,29},{6,102},{7,31},{8,104},... | collective-permute-start | bytes 2433032 | tf_op jit(solution)/shard_map/ppermute | solution.py:56
  10.3 5.8 %collective-permute-start.7 = (bf16[272,1024]{1,0:T(8,128)(2,1)}, bf16[272,1024]{1,0:T(8,128)(2,1)S(1)}, u32[]{:S(2)}, u32[]{:S(2)}) collective-permute-start(bf16[272,1024]{1,0:T(8,128)(2,1)} %get-tuple-element.17.refs_0_), channel_id=1, source_target_pairs={{0,4},{1,5},{2,6},{3,7},{8,12},{9,13},{10,14},{11,15},{16,20},{17,... | collective-permute-start | bytes 1671176 | tf_op jit(solution)/shard_map/ppermute | solution.py:56
  16.1 3.8 %collective-permute-start.6 = (bf16[272,1024]{1,0:T(8,128)(2,1)}, bf16[272,1024]{1,0:T(8,128)(2,1)}, u32[]{:S(2)}, u32[]{:S(2)}) collective-permute-start(bf16[272,1024]{1,0:T(8,128)(2,1)} %get-tuple-element.17.refs_0_), channel_id=1, source_target_pairs={{0,2},{1,3},{2,4},{3,5},{4,6},{5,7},{8,10},{9,11},{10,12},{11,13},... | collective-permute-start | bytes 1671176 | tf_op jit(solution)/shard_map/ppermute | solution.py:56
  19.9 0.0 collective-permute-done.refs_1_.refs_0_
  19.9 0.0 copy-start.2
  19.9 8.1 %collective-permute-done.1.refs_2_.refs_1_ = bf16[528,768]{1,0:T(8,128)(2,1)S(1)} collective-permute-done((bf16[528,768]{1,0:T(8,128)(2,1)}, bf16[528,768]{1,0:T(8,128)(2,1)S(1)}, u32[]{:S(2)}, u32[]{:S(2)}) %collective-permute-start.1) | collective-permute-done | bytes 811040 | tf_op jit(solution)/shard_map/ppermute | solution.py:56
  28.0 0.0 copy-start.4
  28.0 0.0 collective-permute-done.2.refs_3_.refs_2_
  28.0 0.0 copy-start.6
  28.0 1.1 %copy-done.8 = bf16[528,256]{1,0:T(8,128)(2,1)S(1)} copy-done((bf16[528,256]{1,0:T(8,128)(2,1)S(1)}, bf16[528,256]{1,0:T(8,128)(2,1)}, u32[]{:S(2)}) %copy-start.8) | copy-done | bytes 270360
  29.1 0.1 shard_map.105.refs_3_
  29.2 0.0 copy-done.2
  29.2 0.0 copy-done.4
  29.2 0.0 copy-done.6
  29.2 0.0 copy-start.1
  29.3 3.1 %collective-permute-start.5 = (bf16[2112,256]{1,0:T(8,128)(2,1)S(1)}, bf16[2112,256]{1,0:T(8,128)(2,1)}, u32[]{:S(2)}, u32[]{:S(2)}) collective-permute-start(bf16[2112,256]{1,0:T(8,128)(2,1)S(1)} %shard_map.105.refs_3_), channel_id=1, source_target_pairs={{0,24},{1,97},{2,26},{3,99},{4,28},{5,101},{6,30},{7,103},{8,0},{9... | collective-permute-start | bytes 3244040 | tf_op jit(solution)/shard_map/ppermute | solution.py:56
  32.3 0.6 collective-permute-start.4
  33.0 1.0 %collective-permute-start.3 = (bf16[2112,256]{1,0:T(8,128)(2,1)S(1)}, bf16[2112,256]{1,0:T(8,128)(2,1)}, u32[]{:S(2)}, u32[]{:S(2)}) collective-permute-start(bf16[2112,256]{1,0:T(8,128)(2,1)S(1)} %shard_map.105.refs_3_), channel_id=1, source_target_pairs={{0,8},{1,33},{2,10},{3,35},{4,12},{5,37},{6,14},{7,39},{8,16},{9,4... | collective-permute-start | bytes 3244040 | tf_op jit(solution)/shard_map/ppermute | solution.py:56
  33.9 0.0 collective-permute-done.7.refs_2_
  33.9 0.0 copy-done
  33.9 0.1 broadcast_select_fusion
  34.0 0.1 collective-permute-start.9
  34.1 5.5 %collective-permute-done.6.refs_1_ = bf16[272,1024]{1,0:T(8,128)(2,1)} collective-permute-done((bf16[272,1024]{1,0:T(8,128)(2,1)}, bf16[272,1024]{1,0:T(8,128)(2,1)}, u32[]{:S(2)}, u32[]{:S(2)}) %collective-permute-start.6) | collective-permute-done | bytes 557088 | tf_op jit(solution)/shard_map/ppermute | solution.py:56
  39.6 0.0 collective-permute-start.8
  39.6 0.0 collective-permute-done.9.refs_4_
  39.6 2.2 %collective-permute-done.8.refs_3_ = bf16[272,1024]{1,0:T(8,128)(2,1)S(1)} collective-permute-done((bf16[272,1024]{1,0:T(8,128)(2,1)}, bf16[272,1024]{1,0:T(8,128)(2,1)S(1)}, u32[]{:S(2)}, u32[]{:S(2)}) %collective-permute-start.8) | collective-permute-done | bytes 557088 | tf_op jit(solution)/shard_map/ppermute | solution.py:56
  41.7 0.0 copy-done.1
  41.7 12.9 %shard_map.106 = (bf16[256,2048]{1,0:T(8,128)(2,1)}, s32[1]{0:T(128)}) custom-call(bf16[256,2048]{1,0:T(8,128)(2,1)S(1)} %bitcast.10, bf16[272,1024]{1,0:T(8,128)(2,1)S(1)} %copy-done, bf16[272,1024]{1,0:T(8,128)(2,1)} %collective-permute-done.6.refs_1_, bf16[272,1024]{1,0:T(8,128)(2,1)S(1)} %collective-permute-done.7.refs_2_, ...), custom_call_target="tpu_custom_call" | custom-call | flops 100000000 | bytes 1048576 | tf_op jit(solution)/shard_map/pallas_call | solution.py:466
  54.6 2.0 %collective-permute-done.5.refs_6_ = bf16[2112,256]{1,0:T(8,128)(2,1)} collective-permute-done((bf16[2112,256]{1,0:T(8,128)(2,1)S(1)}, bf16[2112,256]{1,0:T(8,128)(2,1)}, u32[]{:S(2)}, u32[]{:S(2)}) %collective-permute-start.5) | collective-permute-done | bytes 1081376 | tf_op jit(solution)/shard_map/ppermute | solution.py:56
  56.6 0.0 collective-permute-done.4.refs_5_
  56.6 4.1 %collective-permute-done.3.refs_4_ = bf16[2112,256]{1,0:T(8,128)(2,1)} collective-permute-done((bf16[2112,256]{1,0:T(8,128)(2,1)S(1)}, bf16[2112,256]{1,0:T(8,128)(2,1)}, u32[]{:S(2)}, u32[]{:S(2)}) %collective-permute-start.3) | collective-permute-done | bytes 1081376 | tf_op jit(solution)/shard_map/ppermute | solution.py:56
  60.7 0.0 copy-done.3
  60.7 0.0 copy-done.5
  60.7 0.0 copy-done.7
  60.7 0.0 copy-start.9
  60.7 1.6 %copy-done.9 = bf16[1,1,512,2048]{3,2,1,0:T(8,128)(2,1)S(1)} copy-done((bf16[1,1,512,2048]{3,2,1,0:T(8,128)(2,1)S(1)}, bf16[1,1,512,2048]{3,2,1,0:T(8,128)(2,1)}, u32[]{:S(2)}) %copy-start.9) | copy-done | bytes 2097176
  62.3 15.0 %shard_map.107 = (bf16[512,512]{1,0:T(8,128)(2,1)S(1)}, bf16[512,512]{1,0:T(8,128)(2,1)S(1)}, bf16[512,512]{1,0:T(8,128)(2,1)S(1)}, s32[64,128]{1,0:T(8,128)S(1)}) custom-call(bf16[512,2048]{1,0:T(8,128)(2,1)S(1)} %bitcast.12, bf16[528,768]{1,0:T(8,128)(2,1)S(1)} %copy-done.3, bf16[528,768]{1,0:T(8,128)(2,1)S(1)} %copy-done.5, ...), custom_call_target="tpu_custom_call" | custom-call | flops 12000000000 | bytes 1048576 | tf_op jit(solution)/shard_map/pallas_call | solution.py:418
  77.3 0.1 collective-permute-start.10
  77.4 3.3 %collective-permute-start.11 = (bf16[512,512]{1,0:T(8,128)(2,1)S(1)}, bf16[512,512]{1,0:T(8,128)(2,1)S(1)}, u32[]{:S(2)}, u32[]{:S(2)}) collective-permute-start(bf16[512,512]{1,0:T(8,128)(2,1)S(1)} %get-tuple-element.21), channel_id=1, source_target_pairs={{0,64},{1,17},{2,66},{3,19},{4,68},{5,21},{6,70},{7,23},{8,72},{9,... | collective-permute-start | bytes 1572872 | tf_op jit(solution)/shard_map/ppermute | solution.py:56
  80.6 0.0 collective-permute-start.12
  80.6 4.6 %shard_map.108.refs_0_ = bf16[512,512]{1,0:T(8,128)(2,1)S(1)} custom-call(bf16[512,2048]{1,0:T(8,128)(2,1)S(1)} %bitcast.13, bf16[528,768]{1,0:T(8,128)(2,1)S(1)} %copy-done.3, bf16[528,768]{1,0:T(8,128)(2,1)S(1)} %copy-done.5, bf16[528,768]{1,0:T(8,128)(2,1)S(1)} %copy-done.7, bf16[2112,256]{1,0:T(8,128)(2,1)S(1)} %shard_map.105.refs_3_, ...), custom_call_target="tpu_custom_call" | custom-call | flops 4000000000 | bytes 1048576 | tf_op jit(solution)/shard_map/pallas_call | solution.py:418
  85.3 1.2 %collective-permute-done.10.refs_1_ = bf16[512,512]{1,0:T(8,128)(2,1)S(1)} collective-permute-done((bf16[512,512]{1,0:T(8,128)(2,1)S(1)}, bf16[512,512]{1,0:T(8,128)(2,1)S(1)}, u32[]{:S(2)}, u32[]{:S(2)}) %collective-permute-start.10) | collective-permute-done | bytes 524320 | tf_op jit(solution)/shard_map/ppermute | solution.py:56
  86.5 1.7 %collective-permute-done.11.refs_2_ = bf16[512,512]{1,0:T(8,128)(2,1)S(1)} collective-permute-done((bf16[512,512]{1,0:T(8,128)(2,1)S(1)}, bf16[512,512]{1,0:T(8,128)(2,1)S(1)}, u32[]{:S(2)}, u32[]{:S(2)}) %collective-permute-start.11) | collective-permute-done | bytes 524320 | tf_op jit(solution)/shard_map/ppermute | solution.py:56
  88.2 5.5 %collective-permute-done.12.refs_3_ = bf16[512,512]{1,0:T(8,128)(2,1)S(1)} collective-permute-done((bf16[512,512]{1,0:T(8,128)(2,1)S(1)}, bf16[512,512]{1,0:T(8,128)(2,1)S(1)}, u32[]{:S(2)}, u32[]{:S(2)}) %collective-permute-start.12) | collective-permute-done | bytes 524320 | tf_op jit(solution)/shard_map/ppermute | solution.py:56
  93.7 1.3 %shard_map.109 = bf16[512,2048]{1,0:T(8,128)(2,1)} custom-call(bf16[512,512]{1,0:T(8,128)(2,1)S(1)} %shard_map.108.refs_0_, bf16[512,512]{1,0:T(8,128)(2,1)S(1)} %collective-permute-done.10.refs_1_, bf16[512,512]{1,0:T(8,128)(2,1)S(1)} %collective-permute-done.11.refs_2_, bf16[512,512]{1,0:T(8,128)(2,1)S(1)} %collective-permute-done.12.refs_3_), custom_call_target="tpu_custom_call" | custom-call | flops 2000000000 | bytes 1048576 | tf_op jit(solution)/shard_map/pallas_call | solution.py:202
  (5 shorter events, 0.0 us)
Async XLA Ops:
  4.5 15.4 %collective-permute-start = (bf16[528,768]{1,0:T(8,128)(2,1)}, bf16[528,768]{1,0:T(8,128)(2,1)S(1)}, u32[]{:S(2)}, u32[]{:S(2)}) collective-permute-start(bf16[528,768]{1,0:T(8,128)(2,1)} %get-tuple-element.13), channel_id=1, source_target_pairs={{0,32},{1,9},{2,34},{3,11},{4,36},{5,13},{6,38},{7,15},{8,40},{9,1... | collective-permute-start | bytes 2433032 | tf_op jit(solution)/shard_map/ppermute | solution.py:56
  6.1 21.9 %collective-permute-start.1 = (bf16[528,768]{1,0:T(8,128)(2,1)}, bf16[528,768]{1,0:T(8,128)(2,1)S(1)}, u32[]{:S(2)}, u32[]{:S(2)}) collective-permute-start(bf16[528,768]{1,0:T(8,128)(2,1)} %get-tuple-element.14), channel_id=1, source_target_pairs={{0,64},{1,17},{2,66},{3,19},{4,68},{5,21},{6,70},{7,23},{8,72},{9,... | collective-permute-start | bytes 2433032 | tf_op jit(solution)/shard_map/ppermute | solution.py:56
  8.9 19.1 %collective-permute-start.2 = (bf16[528,768]{1,0:T(8,128)(2,1)}, bf16[528,768]{1,0:T(8,128)(2,1)S(1)}, u32[]{:S(2)}, u32[]{:S(2)}) collective-permute-start(bf16[528,768]{1,0:T(8,128)(2,1)} %get-tuple-element.15), channel_id=1, source_target_pairs={{0,96},{1,25},{2,98},{3,27},{4,100},{5,29},{6,102},{7,31},{8,104},... | collective-permute-start | bytes 2433032 | tf_op jit(solution)/shard_map/ppermute | solution.py:56
  10.3 23.7 %collective-permute-start.7 = (bf16[272,1024]{1,0:T(8,128)(2,1)}, bf16[272,1024]{1,0:T(8,128)(2,1)S(1)}, u32[]{:S(2)}, u32[]{:S(2)}) collective-permute-start(bf16[272,1024]{1,0:T(8,128)(2,1)} %get-tuple-element.17.refs_0_), channel_id=1, source_target_pairs={{0,4},{1,5},{2,6},{3,7},{8,12},{9,13},{10,14},{11,15},{16,20},{17,... | collective-permute-start | bytes 1671176 | tf_op jit(solution)/shard_map/ppermute | solution.py:56
  16.1 23.5 %collective-permute-start.6 = (bf16[272,1024]{1,0:T(8,128)(2,1)}, bf16[272,1024]{1,0:T(8,128)(2,1)}, u32[]{:S(2)}, u32[]{:S(2)}) collective-permute-start(bf16[272,1024]{1,0:T(8,128)(2,1)} %get-tuple-element.17.refs_0_), channel_id=1, source_target_pairs={{0,2},{1,3},{2,4},{3,5},{4,6},{5,7},{8,10},{9,11},{10,12},{11,13},... | collective-permute-start | bytes 1671176 | tf_op jit(solution)/shard_map/ppermute | solution.py:56
  19.9 9.4 %copy-start.2 = (bf16[528,768]{1,0:T(8,128)(2,1)}, bf16[528,768]{1,0:T(8,128)(2,1)S(1)}, u32[]{:S(2)}) copy-start(bf16[528,768]{1,0:T(8,128)(2,1)S(1)} %collective-permute-done.refs_1_.refs_0_) | copy-start | bytes 2433028
  28.0 1.2 %copy-start.4 = (bf16[528,768]{1,0:T(8,128)(2,1)}, bf16[528,768]{1,0:T(8,128)(2,1)S(1)}, u32[]{:S(2)}) copy-start(bf16[528,768]{1,0:T(8,128)(2,1)S(1)} %collective-permute-done.1.refs_2_.refs_1_) | copy-start | bytes 2433028
  28.0 1.2 %copy-start.6 = (bf16[528,768]{1,0:T(8,128)(2,1)}, bf16[528,768]{1,0:T(8,128)(2,1)S(1)}, u32[]{:S(2)}) copy-start(bf16[528,768]{1,0:T(8,128)(2,1)S(1)} %collective-permute-done.2.refs_3_.refs_2_) | copy-start | bytes 2433028
  28.0 1.1 %copy-start.8 = (bf16[528,256]{1,0:T(8,128)(2,1)S(1)}, bf16[528,256]{1,0:T(8,128)(2,1)}, u32[]{:S(2)}) copy-start(bf16[528,256]{1,0:T(8,128)(2,1)} %get-tuple-element.16.refs_0_) | copy-start | bytes 811012
  29.1 4.8 %copy-start = (bf16[272,1024]{1,0:T(8,128)(2,1)S(1)}, bf16[272,1024]{1,0:T(8,128)(2,1)}, u32[]{:S(2)}) copy-start(bf16[272,1024]{1,0:T(8,128)(2,1)} %get-tuple-element.17.refs_0_) | copy-start | bytes 1671172
  29.2 12.5 %copy-start.1 = (bf16[1,256,2048]{2,1,0:T(8,128)(2,1)S(1)}, bf16[1,256,2048]{2,1,0:T(8,128)(2,1)}, u32[]{:S(2)}) copy-start(bf16[1,256,2048]{2,1,0:T(8,128)(2,1)} %param.14) | copy-start | bytes 3145732
  29.3 27.3 %collective-permute-start.5 = (bf16[2112,256]{1,0:T(8,128)(2,1)S(1)}, bf16[2112,256]{1,0:T(8,128)(2,1)}, u32[]{:S(2)}, u32[]{:S(2)}) collective-permute-start(bf16[2112,256]{1,0:T(8,128)(2,1)S(1)} %shard_map.105.refs_3_), channel_id=1, source_target_pairs={{0,24},{1,97},{2,26},{3,99},{4,28},{5,101},{6,30},{7,103},{8,0},{9... | collective-permute-start | bytes 3244040 | tf_op jit(solution)/shard_map/ppermute | solution.py:56
  32.3 24.3 %collective-permute-start.4 = (bf16[2112,256]{1,0:T(8,128)(2,1)S(1)}, bf16[2112,256]{1,0:T(8,128)(2,1)}, u32[]{:S(2)}, u32[]{:S(2)}) collective-permute-start(bf16[2112,256]{1,0:T(8,128)(2,1)S(1)} %shard_map.105.refs_3_), channel_id=1, source_target_pairs={{0,16},{1,65},{2,18},{3,67},{4,20},{5,69},{6,22},{7,71},{8,24},{9,... | collective-permute-start | bytes 3244040 | tf_op jit(solution)/shard_map/ppermute | solution.py:56
  33.0 27.7 %collective-permute-start.3 = (bf16[2112,256]{1,0:T(8,128)(2,1)S(1)}, bf16[2112,256]{1,0:T(8,128)(2,1)}, u32[]{:S(2)}, u32[]{:S(2)}) collective-permute-start(bf16[2112,256]{1,0:T(8,128)(2,1)S(1)} %shard_map.105.refs_3_), channel_id=1, source_target_pairs={{0,8},{1,33},{2,10},{3,35},{4,12},{5,37},{6,14},{7,39},{8,16},{9,4... | collective-permute-start | bytes 3244040 | tf_op jit(solution)/shard_map/ppermute | solution.py:56
  34.0 5.6 %collective-permute-start.9 = (bf16[272,1024]{1,0:T(8,128)(2,1)S(1)}, bf16[272,1024]{1,0:T(8,128)(2,1)S(1)}, u32[]{:S(2)}, u32[]{:S(2)}) collective-permute-start(bf16[272,1024]{1,0:T(8,128)(2,1)S(1)} %broadcast_select_fusion), channel_id=1, source_target_pairs={{0,1},{1,0},{2,3},{3,2},{4,5},{5,4},{6,7},{7,6},{8,9},{9,8},{10,11... | collective-permute-start | bytes 1671176 | tf_op jit(solution)/shard_map/ppermute | solution.py:56
  39.6 2.2 %collective-permute-start.8 = (bf16[272,1024]{1,0:T(8,128)(2,1)}, bf16[272,1024]{1,0:T(8,128)(2,1)S(1)}, u32[]{:S(2)}, u32[]{:S(2)}) collective-permute-start(bf16[272,1024]{1,0:T(8,128)(2,1)} %collective-permute-done.6.refs_1_), channel_id=1, source_target_pairs={{0,1},{1,0},{2,3},{3,2},{4,5},{5,4},{6,7},{7,6},{8,9},{9,8},{10,11... | collective-permute-start | bytes 1671176 | tf_op jit(solution)/shard_map/ppermute | solution.py:56
  41.7 19.0 %copy-start.3 = (bf16[528,768]{1,0:T(8,128)(2,1)S(1)}, bf16[528,768]{1,0:T(8,128)(2,1)}, u32[]{:S(2)}) copy-start(bf16[528,768]{1,0:T(8,128)(2,1)} %copy-done.2) | copy-start | bytes 2433028
  41.7 19.0 %copy-start.5 = (bf16[528,768]{1,0:T(8,128)(2,1)S(1)}, bf16[528,768]{1,0:T(8,128)(2,1)}, u32[]{:S(2)}) copy-start(bf16[528,768]{1,0:T(8,128)(2,1)} %copy-done.4) | copy-start | bytes 2433028
  41.7 19.0 %copy-start.7 = (bf16[528,768]{1,0:T(8,128)(2,1)S(1)}, bf16[528,768]{1,0:T(8,128)(2,1)}, u32[]{:S(2)}) copy-start(bf16[528,768]{1,0:T(8,128)(2,1)} %copy-done.6) | copy-start | bytes 2433028
  60.7 1.6 %copy-start.9 = (bf16[1,1,512,2048]{3,2,1,0:T(8,128)(2,1)S(1)}, bf16[1,1,512,2048]{3,2,1,0:T(8,128)(2,1)}, u32[]{:S(2)}) copy-start(bf16[1,1,512,2048]{3,2,1,0:T(8,128)(2,1)} %param.9) | copy-start | bytes 6291460
  77.3 9.2 %collective-permute-start.10 = (bf16[512,512]{1,0:T(8,128)(2,1)S(1)}, bf16[512,512]{1,0:T(8,128)(2,1)S(1)}, u32[]{:S(2)}, u32[]{:S(2)}) collective-permute-start(bf16[512,512]{1,0:T(8,128)(2,1)S(1)} %get-tuple-element.20), channel_id=1, source_target_pairs={{0,96},{1,25},{2,98},{3,27},{4,100},{5,29},{6,102},{7,31},{8,104},... | collective-permute-start | bytes 1572872 | tf_op jit(solution)/shard_map/ppermute | solution.py:56
  77.4 10.9 %collective-permute-start.11 = (bf16[512,512]{1,0:T(8,128)(2,1)S(1)}, bf16[512,512]{1,0:T(8,128)(2,1)S(1)}, u32[]{:S(2)}, u32[]{:S(2)}) collective-permute-start(bf16[512,512]{1,0:T(8,128)(2,1)S(1)} %get-tuple-element.21), channel_id=1, source_target_pairs={{0,64},{1,17},{2,66},{3,19},{4,68},{5,21},{6,70},{7,23},{8,72},{9,... | collective-permute-start | bytes 1572872 | tf_op jit(solution)/shard_map/ppermute | solution.py:56
  80.6 13.1 %collective-permute-start.12 = (bf16[512,512]{1,0:T(8,128)(2,1)S(1)}, bf16[512,512]{1,0:T(8,128)(2,1)S(1)}, u32[]{:S(2)}, u32[]{:S(2)}) collective-permute-start(bf16[512,512]{1,0:T(8,128)(2,1)S(1)} %get-tuple-element.22), channel_id=1, source_target_pairs={{0,32},{1,9},{2,34},{3,11},{4,36},{5,13},{6,38},{7,15},{8,40},{9,1... | collective-permute-start | bytes 1572872 | tf_op jit(solution)/shard_map/ppermute | solution.py:56

commit v3 on v2

--- a/solution.py
+++ b/solution.py
@@ -24,6 +24,8 @@
 QW = GROUP * HD
 CHUNK = 4
 SET = 4
+ORDER = (2, 1, 3)
+WIDE = 2 * CHUNK
 MASKED = -1e30
 SCALE = HD**-0.5 * 1.4426950408889634
 MIB = 1024 * 1024
@@ -96,34 +98,43 @@
 
 
 def split_kernel(home_in, fill_in, doc_in, k_ref, v_ref, q_ref, lk_ref, lv_ref, *refs):
-    outs, own, packed = refs[: SIDE - 1], refs[SIDE - 1], refs[SIDE]
-    home, fill, docs, sems, few_sems = refs[SIDE + 1 :]
+    outs, packed_out = refs[: SIDE + 1], refs[SIDE + 1]
+    refs = refs[SIDE + 2 :]
+    home, fill, docs, pieces, own_q, packed, sems, few_sems, out_sems = refs
     mine = where_am_i()[0]
     few = [
         pltpu.make_async_copy(source, to, few_sems.at[n])
         for n, (source, to) in enumerate(((home_in, home), (fill_in, fill), (doc_in, docs)))
     ]
-    copies = []
-    for k in range(SIDE):
+    for copy in few:
+        copy.start()
+    copies = {}
+    for k in ORDER + (0,):
         head = (mine + k) & 3
         col = pl.multiple_of(head * HD, HD)
-        out = own if k == 0 else outs[k - 1]
-        moves = [(k_ref, col, HD, 0), (v_ref, col, HD, HD)]
-        if k > 0:
-            moves.append((q_ref, pl.multiple_of(head * QW, QW), QW, KVW))
-        for n, (source, at, wide, to) in enumerate(moves):
-            copies.append(
-                pltpu.make_async_copy(
-                    source.at[:, pl.ds(at, wide)],
-                    out.at[pl.ds(0, ROWS), pl.ds(to, wide)],
-                    sems.at[k, n],
-                )
-            )
+        qcol = pl.multiple_of(head * QW, QW)
+        piece = pieces.at[k]
+        goals = [
+            (k_ref.at[:, pl.ds(col, HD)], piece.at[pl.ds(0, ROWS), pl.ds(0, HD)]),
+            (v_ref.at[:, pl.ds(col, HD)], piece.at[pl.ds(0, ROWS), pl.ds(HD, HD)]),
+            (
+                q_ref.at[:, pl.ds(qcol, QW)],
+                piece.at[pl.ds(0, ROWS), pl.ds(KVW, QW)] if k else own_q,
+            ),
+        ]
+        copies[k] = [
+            pltpu.make_async_copy(source, to, sems.at[k, n]) for n, (source, to) in enumerate(goals)
+        ]
+        for copy in copies[k]:
+            copy.start()
     wide = KVH * HD
-    for n, source in enumerate((lk_ref, lv_ref)):
-        to = packed.at[pl.ds(0, LROWS), pl.ds(n * wide, wide)]
-        copies.append(pltpu.make_async_copy(source, to, sems.at[SIDE, n]))
-    for copy in few + copies:
+    long_copies = [
+        pltpu.make_async_copy(
+            source, packed.at[pl.ds(0, LROWS), pl.ds(n * wide, wide)], sems.at[SIDE, n]
+        )
+        for n, source in enumerate((lk_ref, lv_ref))
+    ]
+    for copy in long_copies:
         copy.start()
     for copy in few:
         copy.wait()
@@ -133,34 +144,48 @@
         facts = jnp.where(row == b, home[b], facts)
         facts = jnp.where(row == SB + b, fill[b], facts)
     facts = facts.astype(jnp.float32).astype(jnp.bfloat16)
-    own[ROWS:, :] = facts
-    for out in outs:
-        out[ROWS:, :KVW] = facts
-        out[ROWS:, KVW:] = jnp.zeros((EXTRA, QW), jnp.bfloat16)
+    for k in range(SIDE):
+        pieces[k, ROWS:, :KVW] = facts
+        if k:
+            pieces[k, ROWS:, KVW:] = jnp.zeros((EXTRA, QW), jnp.bfloat16)
     doc_row = docs[...].astype(jnp.float32) + 1.0
     packed[LROWS:, :LROWS] = jnp.broadcast_to(doc_row, (EXTRA, LROWS)).astype(jnp.bfloat16)
     packed[LROWS:, LROWS:] = jnp.zeros((EXTRA, 2 * wide - LROWS), jnp.bfloat16)
-    for copy in copies:
+    done = []
+    for k in ORDER + (0,):
+        for copy in copies[k]:
+            copy.wait()
+        source = pieces.at[k] if k else pieces.at[0, :, pl.ds(0, KVW)]
+        done.append(pltpu.make_async_copy(source, outs[k], out_sems.at[k]))
+        done[-1].start()
+    done.append(pltpu.make_async_copy(own_q, outs[SIDE], out_sems.at[SIDE]))
+    done[-1].start()
+    for copy in long_copies:
         copy.wait()
+    done.append(pltpu.make_async_copy(packed, packed_out, out_sems.at[SIDE + 1]))
+    done[-1].start()
+    for copy in done:
+        copy.wait()
 
 
 def split(home, fill, docs, keys, values, queries, long_keys, long_values):
-    shapes = [jax.ShapeDtypeStruct((PIECE, KVW + QW), jnp.bfloat16)] * (SIDE - 1)
-    shapes += [
-        jax.ShapeDtypeStruct((PIECE, KVW), jnp.bfloat16),
-        jax.ShapeDtypeStruct((LROWS + EXTRA, 2 * KVH * HD), jnp.bfloat16),
-    ]
+    shapes = [(PIECE, KVW)] + [(PIECE, KVW + QW)] * (SIDE - 1)
+    shapes += [(ROWS, QW), (LROWS + EXTRA, 2 * KVH * HD)]
     return pl.pallas_call(
         split_kernel,
-        out_shape=shapes,
+        out_shape=[jax.ShapeDtypeStruct(shape, jnp.bfloat16) for shape in shapes],
         in_specs=[FAR] * 8,
-        out_specs=[VM] * (SIDE + 1),
+        out_specs=[FAR] * (SIDE + 2),
         scratch_shapes=[
             pltpu.SMEM((SB,), jnp.int32),
             pltpu.SMEM((SB,), jnp.int32),
             pltpu.VMEM((1, LROWS), jnp.int32),
+            pltpu.VMEM((SIDE, PIECE, KVW + QW), jnp.bfloat16),
+            pltpu.VMEM((ROWS, QW), jnp.bfloat16),
+            pltpu.VMEM((LROWS + EXTRA, 2 * KVH * HD), jnp.bfloat16),
             pltpu.SemaphoreType.DMA((SIDE + 1, 3)),
             pltpu.SemaphoreType.DMA((3,)),
+            pltpu.SemaphoreType.DMA((SIDE + 2,)),
         ],
         compiler_params=pltpu.CompilerParams(vmem_limit_bytes=60 * MIB),
         cost_estimate=busy(2),
@@ -238,22 +263,12 @@
         slots = jnp.where(same, lane * (PIECE // EXTRA) + b * (BLOCK // EXTRA), slots)
         fills = jnp.where(same, facts[SB + b : SB + b + 1], fills)
     ranks = jnp.dot(here, earlier, preferred_element_type=jnp.float32).astype(jnp.int32)
-    own_rows = lax.broadcasted_iota(jnp.int32, (SB, HD), 0)
     own_ranks = jnp.zeros((SB, HD), jnp.int32)
     for d in range(GROUPS):
         own_ranks = jnp.where(facts[:SB] == d, ranks[d : d + 1], own_ranks)
-    place = jnp.zeros((SB, HD), jnp.int32)
-    for b in range(SB):
-        other = own_ranks[b : b + 1]
-        ahead = (other > own_ranks) | ((other == own_ranks) & (own_rows > b))
-        place = place + jnp.where(ahead, 1, 0)
-    listed = [jnp.zeros((SB, HD), jnp.int32) for _ in range(4)]
-    for b in range(SB):
-        chosen = place[b : b + 1] == own_rows
-        found = (b, facts[b : b + 1], facts[SB + b : SB + b + 1], own_ranks[b : b + 1])
-        listed = [jnp.where(chosen, new, old) for new, old in zip(found, listed)]
-    for n in range(4):
-        table_ref[n * SB : (n + 1) * SB] = listed[n]
+    table_ref[: 2 * SB] = facts
+    table_ref[2 * SB : 3 * SB] = own_ranks
+    table_ref[3 * SB : 4 * SB] = own_ranks
     ranks = jnp.where(here > 0.0, ranks, -1)
     slot_list = jnp.zeros(shape, jnp.int32)
     fill_list = jnp.zeros(shape, jnp.int32)
@@ -283,10 +298,10 @@
     )
 
 
-def short_kernel(shifts, first, waits, q_all, *refs):
+def short_kernel(shifts, first, waits, *refs):
     count = len(shifts)
-    line_parts, kv_parts = refs[: SIDE - 1], refs[SIDE - 1 : 2 * SIDE - 1]
-    refs = refs[2 * SIDE - 1 + waits :]
+    q_parts, kv_parts = refs[:count], refs[count : count + SIDE]
+    refs = refs[count + SIDE + waits :]
     if first:
         out_parts, table = refs[:count], refs[count]
         table_ref, table_sem = refs[-2:]
@@ -294,12 +309,7 @@
     else:
         table, out_parts = refs[0], refs[1 : 1 + count]
         refs = refs[1 + count :]
-    kv_ref, q_ref, out_ref, mix_ref, top_ref, kv_sems, q_sems = refs[:7]
-    col = pl.multiple_of(where_am_i()[0] * QW, QW)
-    wanted = [
-        line_parts[k - 1].at[pl.ds(0, ROWS), pl.ds(KVW, QW)] if k else q_all.at[:, pl.ds(col, QW)]
-        for k in shifts
-    ]
+    kv_ref, q_ref, out_ref, mix_ref, top_ref, list_ref, kv_sems, q_sems = refs[:8]
     part_rows = SIDE * PIECE
     copies = [
         pltpu.make_async_copy(
@@ -308,8 +318,12 @@
         for n in range(SIDE)
     ]
     copies += [
-        pltpu.make_async_copy(source, q_ref.at[pl.ds(n * ROWS, ROWS)], q_sems.at[n])
-        for n, source in enumerate(wanted)
+        pltpu.make_async_copy(
+            q_parts[n].at[pl.ds(0, ROWS), pl.ds(KVW if k else 0, QW)],
+            q_ref.at[pl.ds(n * ROWS, ROWS)],
+            q_sems.at[n],
+        )
+        for n, k in enumerate(shifts)
     ]
     for copy in copies:
         copy.start()
@@ -320,86 +334,108 @@
         table_copy = pltpu.make_async_copy(table_ref, table, table_sem)
         table_copy.start()
         table_copy.wait()
-    width = CHUNK * BLOCK
-    lane = lax.broadcasted_iota(jnp.int32, (BLOCK, width), 1)
-    lane_block = lane // BLOCK
-    lane_row = lane % BLOCK
-    row = lax.broadcasted_iota(jnp.int32, (BLOCK, width), 0)
-    ones = jnp.ones((width, HD), jnp.bfloat16)
-
-    def one_set(t, _):
-        piece = t // (SB // SET)
-        k = piece + shifts[0]
-        base = (t % (SB // SET)) * SET
-
-        def fact(n, u):
-            return table[n * SB + base + u, k]
-
-        def rows_of(u):
-            return pl.ds(pl.multiple_of(piece * ROWS + fact(0, u) * BLOCK, BLOCK), BLOCK)
-
-        def scores_of(u, c):
-            home, rank = fact(1, u), fact(3, u)
-            q = q_ref[rows_of(u), :]
-            q = jnp.concatenate([q[:, h * HD : (h + 1) * HD] for h in range(GROUP)], axis=0)
-            limits, keys, values = [], [], []
-            for j in range(CHUNK):
-                n = c * CHUNK + j
-                start = pl.multiple_of(table[4 * SB + home, n] * EXTRA, EXTRA)
-                kv = kv_ref[pl.ds(start, BLOCK), :]
-                keys.append(kv[:, :HD])
-                values.append(kv[:, HD:])
-                limits.append(jnp.where(n <= rank, table[4 * SB + GROUPS + home, n], 0))
-            limit = jnp.where(
-                lane_block < 2,
-                jnp.where(lane_block == 0, limits[0], limits[1]),
-                jnp.where(lane_block == 2, limits[2], limits[3]),
+    low = lax.broadcasted_iota(jnp.int32, (BLOCK, HD), 1) < BLOCK
+    lane_row = lax.broadcasted_iota(jnp.int32, (BLOCK, HD), 1) % BLOCK
+    row = lax.broadcasted_iota(jnp.int32, (BLOCK, HD), 0)
+
+    total = count * SB
+    over = [0, 0, 0]
+    ranks = []
+    for n in range(total):
+        rank = table[2 * SB + n % SB, shifts[0] + n // SB]
+        ranks.append(rank)
+        over = [old + jnp.where(rank >= 4 * (i + 1), 1, 0) for i, old in enumerate(over)]
+    spots = [over[0], over[1], over[2], 0]
+    for n in range(total):
+        b, k = n % SB, shifts[0] + n // SB
+        level = lax.shift_right_logical(ranks[n], 2)
+        spot = jnp.where(
+            level < 2,
+            jnp.where(level == 0, spots[0], spots[1]),
+            jnp.where(level == 2, spots[2], spots[3]),
+        )
+        list_ref[0, spot] = n
+        list_ref[1, spot] = table[b, k]
+        list_ref[2, spot] = ranks[n]
+        list_ref[3, spot] = table[SB + b, k]
+        spots = [old + jnp.where(level == i, 1, 0) for i, old in enumerate(spots)]
+
+    def rows_of(at):
+        return pl.ds(pl.multiple_of(list_ref[0, at] * BLOCK, BLOCK), BLOCK)
+
+    def scores_of(at, first_key, blocks):
+        home, rank = list_ref[1, at], list_ref[2, at]
+        q = q_ref[rows_of(at), :]
+        q = jnp.concatenate([q[:, h * HD : (h + 1) * HD] for h in range(GROUP)], axis=0)
+        fills, shifts_in, keys, values, biases = [], [], [], [], []
+        for j in range(blocks):
+            n = first_key + j
+            start = pl.multiple_of(table[4 * SB + home, n] * EXTRA, EXTRA)
+            kv = kv_ref[pl.ds(start, BLOCK), :]
+            keys.append(kv[:, :HD])
+            values.append(kv[:, HD:])
+            fills.append(jnp.where(n <= rank, table[4 * SB + GROUPS + home, n], 0))
+            shifts_in.append(jnp.where(n == rank, 1, BLOCK))
+        for j in range(0, blocks, 2):
+            limit = jnp.minimum(
+                jnp.where(low, fills[j], fills[j + 1]),
+                row + jnp.where(low, shifts_in[j], shifts_in[j + 1]),
             )
-            causal = jnp.where(lane_block == rank - c * CHUNK, row + 1, BLOCK)
-            bias = jnp.where(lane_row < jnp.minimum(limit, causal), 0.0, MASKED)
-            scores = inner(q, jnp.concatenate(keys, axis=0))
-            scores = scores + jnp.concatenate([bias] * GROUP, axis=0)
-            values = jnp.concatenate([jnp.concatenate(values, axis=0), ones], axis=1)
-            return scores, values
-
-        def weigh(scores, top, values):
-            weights = jnp.exp2((scores - top) * SCALE).astype(jnp.bfloat16)
-            return jnp.dot(weights, values, preferred_element_type=jnp.float32)
-
+            biases.append(jnp.where(lane_row < limit, 0.0, MASKED))
+        scores = inner(q, jnp.concatenate(keys, axis=0))
+        scores = scores + jnp.concatenate([jnp.concatenate(biases, axis=1)] * GROUP, axis=0)
+        ones = jnp.ones((blocks * BLOCK, HD), jnp.bfloat16)
+        return scores, jnp.concatenate([jnp.concatenate(values, axis=0), ones], axis=1)
+
+    def weigh(scores, top, values):
+        weights = jnp.exp2((scores - top) * SCALE).astype(jnp.bfloat16)
+        return jnp.dot(weights, values, preferred_element_type=jnp.float32)
+
+    def finish(at, mixed):
+        mixed = mixed[:, :HD] / mixed[:, HD:]
+        used = row < list_ref[3, at]
+        for h in range(GROUP):
+            part = jnp.where(used, mixed[h * BLOCK : (h + 1) * BLOCK], 0.0)
+            out_ref[rows_of(at), h * HD : (h + 1) * HD] = part.astype(jnp.bfloat16)
+
+    def in_one(blocks):
+        def body(t, _):
+            for u in range(SET):
+                at = t * SET + u
+                scores, values = scores_of(at, 0, blocks)
+                top = jnp.max(scores, axis=-1, keepdims=True)
+                finish(at, weigh(scores, top, values))
+            return 0
+
+        return body
+
+    def in_two(t, _):
         for u in range(SET):
-            scores, values = scores_of(u, 0)
+            scores, values = scores_of(t * SET + u, 0, WIDE)
             top = jnp.max(scores, axis=-1, keepdims=True)
             top_ref[u] = jnp.broadcast_to(top, (GROUP * BLOCK, HD))
             mix_ref[u] = weigh(scores, top, values)
-
-        def later(c, _):
-            for u in range(SET):
-                scores, values = scores_of(u, c)
-                old = top_ref[u]
-                top = jnp.broadcast_to(jnp.max(scores, axis=-1, keepdims=True), old.shape)
-                top = jnp.maximum(old, top)
-                top_ref[u] = top
-                shrink = jnp.exp2((old - top) * SCALE)
-                shrink = jnp.concatenate([shrink, shrink], axis=1)
-                mix_ref[u] = mix_ref[u] * shrink + weigh(scores, jnp.concatenate([top, top], axis=1), values)
-            return 0
-
-        lax.fori_loop(1, fact(3, 0) // CHUNK + 1, later, 0)
         for u in range(SET):
-            mixed = mix_ref[u]
-            mixed = mixed[:, :HD] / mixed[:, HD:]
-            used = row[:, :HD] < fact(2, u)
-            for h in range(GROUP):
-                part = jnp.where(used, mixed[h * BLOCK : (h + 1) * BLOCK], 0.0)
-                out_ref[rows_of(u), h * HD : (h + 1) * HD] = part.astype(jnp.bfloat16)
+            scores, values = scores_of(t * SET + u, WIDE, WIDE)
+            old = top_ref[u]
+            top = jnp.broadcast_to(jnp.max(scores, axis=-1, keepdims=True), old.shape)
+            top = jnp.maximum(old, top)
+            shrink = jnp.exp2((old - top) * SCALE)
+            shrink = jnp.concatenate([shrink, shrink], axis=1)
+            top = jnp.concatenate([top] * (WIDE // 2), axis=1)
+            finish(t * SET + u, mix_ref[u] * shrink + weigh(scores, top, values))
         return 0
 
-    lax.fori_loop(0, count * (SB // SET), one_set, 0)
+    twice = (over[1] + SET - 1) // SET
+    once = (over[0] + SET - 1) // SET
+    lax.fori_loop(0, twice, in_two, 0)
+    lax.fori_loop(twice, once, in_one(WIDE), 0)
+    lax.fori_loop(once, total // SET, in_one(CHUNK), 0)
     for n in range(count):
         out_parts[n][...] = out_ref[n * ROWS : (n + 1) * ROWS]
 
 
-def short_attention(shifts, table, after, queries, line_parts, kv_parts):
+def short_attention(shifts, table, after, q_parts, kv_parts):
     count = len(shifts)
     first = table is None
     outs = [jax.ShapeDtypeStruct((ROWS, QW), jnp.bfloat16)] * count
@@ -409,6 +445,7 @@
         pltpu.VMEM((count * ROWS, QW), jnp.bfloat16),
         pltpu.VMEM((SET, GROUP * BLOCK, 2 * HD), jnp.float32),
         pltpu.VMEM((SET, GROUP * BLOCK, HD), jnp.float32),
+        pltpu.SMEM((4, count * SB), jnp.int32),
         pltpu.SemaphoreType.DMA((SIDE,)),
         pltpu.SemaphoreType.DMA((count,)),
     ]
@@ -418,15 +455,14 @@
     found = pl.pallas_call(
         functools.partial(short_kernel, shifts, first, len(after)),
         out_shape=outs,
-        in_specs=[FAR]
-        + [HB] * (2 * SIDE - 1)
+        in_specs=[HB] * (count + SIDE)
         + [SM if first else HB] * len(after)
         + ([] if first else [SM]),
         out_specs=[VM] * count + ([SM] if first else []),
         scratch_shapes=scratch,
         compiler_params=pltpu.CompilerParams(vmem_limit_bytes=24 * MIB),
         cost_estimate=busy(4 * count),
-    )(queries, *line_parts, *kv_parts, *after, *([] if first else [table]))
+    )(*q_parts, *kv_parts, *after, *([] if first else [table]))
     return (found[:count], found[count]) if first else (found, table)
 
 
@@ -492,22 +528,23 @@
     long_values,
     long_docs,
 ):
-    queries = short_queries.reshape(ROWS, QH * HD)
-    *own, own_kv, packed = split(
+    *own, own_q, packed = split(
         block_home.reshape(SB),
         block_fill.reshape(SB),
         long_docs.reshape(1, LROWS),
         short_keys.reshape(ROWS, KVH * HD),
         short_values.reshape(ROWS, KVH * HD),
-        queries,
+        short_queries.reshape(ROWS, QH * HD),
         long_keys.reshape(LROWS, KVH * HD),
         long_values.reshape(LROWS, KVH * HD),
     )
-    line_parts = [send(own[k - 1], along_head(k)) for k in (1, 2, 3)]
+    sent = {k: send(own[k], along_head(k)) for k in ORDER}
+    line_parts = [sent[k] for k in (1, 2, 3)]
     long_one = send(packed, up_chips(1))
     long_two = send(packed, up_chips(2))
-    stacked = stack([own_kv] + line_parts)
-    kv_parts = [stacked] + [send(stacked, along_rows(k)) for k in (1, 2, 3)]
+    stacked = stack([own[0]] + line_parts)
+    sent = {k: send(stacked, along_rows(k)) for k in ORDER[::-1]}
+    kv_parts = [stacked] + [sent[k] for k in (1, 2, 3)]
     long_side = send(long_one, other_core)
     core = lax.axis_index("ctx") % 2
     long_cross = send(jnp.where(core == 0, packed, long_two), other_core)
@@ -516,9 +553,9 @@
         [packed, long_one, long_two, long_side, long_cross],
     )
 
-    mixed, table = short_attention((1, 2, 3), None, [token], queries, line_parts, kv_parts)
+    mixed, table = short_attention((1, 2, 3), None, [token], line_parts, kv_parts)
     back = [send(piece, along_head(-k)) for k, piece in zip((1, 2, 3), mixed)]
-    kept, _ = short_attention((0,), table, [], queries, line_parts, kv_parts)
+    kept, _ = short_attention((0,), table, [], [own_q], kv_parts)
     short_out = join([kept[0]] + back)
     return short_out.reshape(short_queries.shape), long_out.reshape(long_queries.shape)
 

time: 95.5 us -> 92.3 us (0.966)
  Pallas kernels: 37.7 us -> 34 us
  local copies, waits for them, and re-layouts: 2.76 us -> 1.18 us
  starting transfers between devices: 23.5 us -> 24.6 us
    pallas_call x2, Pallas kernels: 19.6 us -> 15.8 us  [short_attention(): pl.pallas_call(functools.partial(short_kernel, shifts, first, len(after))...]
    unnamed x20, local copies, waits for them, and re-layouts: 2.76 us -> 1.18 us
    ppermute x13, starting transfers between devices: 23.5 us -> 24.6 us  [send(): return lax.ppermute(value, ('dp', 'ctx'), pairs(step))]
  transfers between devices with their start and end apart: 13 -> 13, of which waited for: 8 -> 8; matrix products, arithmetic and copies ran while one was open for 0% -> 0% of each run, Pallas kernels for 18% -> 19%
where the time goes in v3:
time: 92.3 us; the launch traced here: 91.7 us
  Pallas kernels  34 us (37%)
  waiting for transfers between devices  31 us (34%)
  starting transfers between devices  24.6 us (27%)
  local copies, waits for them, and re-layouts  1.18 us (1%)
    ppermute x13, waiting for transfers between devices, send(): return lax.ppermute(value, ('dp', 'ctx'), pairs(step))  31 us
    ppermute x13, starting transfers between devices, send(): return lax.ppermute(value, ('dp', 'ctx'), pairs(step))  24.6 us
    pallas_call x2, Pallas kernels, short_attention(): pl.pallas_call(functools.partial(short_kernel, shifts, first, len(after))...  15.8 us
    pallas_call x1, Pallas kernels, long_attention(): pl.pallas_call(long_kernel, out_shape=[jax.ShapeDtypeStruct((LROWS, QH *...  12.9 us
    pallas_call x1, Pallas kernels, split(): pl.pallas_call(split_kernel, out_shape=[jax.ShapeDtypeStruct(shape, jnp.b...  3.91 us
  transfers between devices with their start and end apart: 13, of which 8 were waited for; matrix products, arithmetic and copies ran while one was open for 0% of the time, Pallas kernels for 19%

profile of v3, /device:TPU:0, one launch (start us, length us, event | category | flops | bytes accessed | tf_op | source)
XLA Modules:
  0.0 91.7 jit_solution(9004193780116364488)
XLA Ops:
  0.6 3.9 %shard_map.104 = (bf16[528,256]{1,0:T(8,128)(2,1)}, bf16[528,768]{1,0:T(8,128)(2,1)}, bf16[528,768]{1,0:T(8,128)(2,1)}, bf16[528,768]{1,0:T(8,128)(2,1)}, bf16[5...) custom-call(s32[8]{0:T(128)} %bitcast.17, s32[8]{0:T(128)} %bitcast.18, s32[1,256]{1,0:T(1,128)} %doc_in.1, ...), custom_call_target="tpu_custom_call" | custom-call | flops 2000000000 | bytes 1048576 | tf_op jit(solution)/shard_map/pallas_call | solution.py:174
  4.6 1.6 %collective-permute-start = (bf16[528,768]{1,0:T(8,128)(2,1)}, bf16[528,768]{1,0:T(8,128)(2,1)S(1)}, u32[]{:S(2)}, u32[]{:S(2)}) collective-permute-start(bf16[528,768]{1,0:T(8,128)(2,1)} %get-tuple-element.16), channel_id=1, source_target_pairs={{0,32},{1,9},{2,34},{3,11},{4,36},{5,13},{6,38},{7,15},{8,40},{9,1... | collective-permute-start | bytes 2433032 | tf_op jit(solution)/shard_map/ppermute | solution.py:58
  6.2 2.7 %collective-permute-start.1 = (bf16[528,768]{1,0:T(8,128)(2,1)}, bf16[528,768]{1,0:T(8,128)(2,1)S(1)}, u32[]{:S(2)}, u32[]{:S(2)}) collective-permute-start(bf16[528,768]{1,0:T(8,128)(2,1)} %get-tuple-element.17), channel_id=1, source_target_pairs={{0,64},{1,17},{2,66},{3,19},{4,68},{5,21},{6,70},{7,23},{8,72},{9,... | collective-permute-start | bytes 2433032 | tf_op jit(solution)/shard_map/ppermute | solution.py:58
  8.9 1.4 %collective-permute-start.2 = (bf16[528,768]{1,0:T(8,128)(2,1)}, bf16[528,768]{1,0:T(8,128)(2,1)S(1)}, u32[]{:S(2)}, u32[]{:S(2)}) collective-permute-start(bf16[528,768]{1,0:T(8,128)(2,1)} %get-tuple-element.18), channel_id=1, source_target_pairs={{0,96},{1,25},{2,98},{3,27},{4,100},{5,29},{6,102},{7,31},{8,104},... | collective-permute-start | bytes 2433032 | tf_op jit(solution)/shard_map/ppermute | solution.py:58
  10.4 5.8 %collective-permute-start.7 = (bf16[272,1024]{1,0:T(8,128)(2,1)}, bf16[272,1024]{1,0:T(8,128)(2,1)S(1)}, u32[]{:S(2)}, u32[]{:S(2)}) collective-permute-start(bf16[272,1024]{1,0:T(8,128)(2,1)} %get-tuple-element.19.refs_0_), channel_id=1, source_target_pairs={{0,4},{1,5},{2,6},{3,7},{8,12},{9,13},{10,14},{11,15},{16,20},{17,... | collective-permute-start | bytes 1671176 | tf_op jit(solution)/shard_map/ppermute | solution.py:58
  16.2 3.8 %collective-permute-start.6 = (bf16[272,1024]{1,0:T(8,128)(2,1)}, bf16[272,1024]{1,0:T(8,128)(2,1)}, u32[]{:S(2)}, u32[]{:S(2)}) collective-permute-start(bf16[272,1024]{1,0:T(8,128)(2,1)} %get-tuple-element.19.refs_0_), channel_id=1, source_target_pairs={{0,2},{1,3},{2,4},{3,5},{4,6},{5,7},{8,10},{9,11},{10,12},{11,13},... | collective-permute-start | bytes 1671176 | tf_op jit(solution)/shard_map/ppermute | solution.py:58
  19.9 0.0 collective-permute-done.refs_1_.refs_0_
  19.9 0.0 copy-start.2
  19.9 8.1 %collective-permute-done.1.refs_2_.refs_1_ = bf16[528,768]{1,0:T(8,128)(2,1)S(1)} collective-permute-done((bf16[528,768]{1,0:T(8,128)(2,1)}, bf16[528,768]{1,0:T(8,128)(2,1)S(1)}, u32[]{:S(2)}, u32[]{:S(2)}) %collective-permute-start.1) | collective-permute-done | bytes 811040 | tf_op jit(solution)/shard_map/ppermute | solution.py:58
  28.1 0.0 copy-start.4
  28.1 0.0 collective-permute-done.2.refs_3_.refs_2_
  28.1 0.0 copy-start.6
  28.1 1.1 %copy-done.8 = bf16[528,256]{1,0:T(8,128)(2,1)S(1)} copy-done((bf16[528,256]{1,0:T(8,128)(2,1)S(1)}, bf16[528,256]{1,0:T(8,128)(2,1)}, u32[]{:S(2)}) %copy-start.8) | copy-done | bytes 270360
  29.2 0.1 shard_map.105.refs_3_.refs_1_
  29.3 0.0 copy-done.2
  29.3 0.0 copy-done.4
  29.3 0.0 copy-done.6
  29.3 0.0 copy-start.1
  29.3 3.1 %collective-permute-start.5 = (bf16[2112,256]{1,0:T(8,128)(2,1)S(1)}, bf16[2112,256]{1,0:T(8,128)(2,1)}, u32[]{:S(2)}, u32[]{:S(2)}) collective-permute-start(bf16[2112,256]{1,0:T(8,128)(2,1)S(1)} %shard_map.105.refs_3_.refs_1_), channel_id=1, source_target_pairs={{0,24},{1,97},{2,26},{3,99},{4,28},{5,101},{6,30},{7,103},{8,0},{9... | collective-permute-start | bytes 3244040 | tf_op jit(solution)/shard_map/ppermute | solution.py:58
  32.4 0.6 collective-permute-start.4
  33.0 1.0 %collective-permute-start.3 = (bf16[2112,256]{1,0:T(8,128)(2,1)S(1)}, bf16[2112,256]{1,0:T(8,128)(2,1)}, u32[]{:S(2)}, u32[]{:S(2)}) collective-permute-start(bf16[2112,256]{1,0:T(8,128)(2,1)S(1)} %shard_map.105.refs_3_.refs_1_), channel_id=1, source_target_pairs={{0,8},{1,33},{2,10},{3,35},{4,12},{5,37},{6,14},{7,39},{8,16},{9,4... | collective-permute-start | bytes 3244040 | tf_op jit(solution)/shard_map/ppermute | solution.py:58
  34.0 0.0 collective-permute-done.7.refs_2_
  34.0 0.0 copy-done
  34.0 0.1 broadcast_select_fusion
  34.1 0.1 collective-permute-start.9
  34.2 5.5 %collective-permute-done.6.refs_1_ = bf16[272,1024]{1,0:T(8,128)(2,1)} collective-permute-done((bf16[272,1024]{1,0:T(8,128)(2,1)}, bf16[272,1024]{1,0:T(8,128)(2,1)}, u32[]{:S(2)}, u32[]{:S(2)}) %collective-permute-start.6) | collective-permute-done | bytes 557088 | tf_op jit(solution)/shard_map/ppermute | solution.py:58
  39.6 0.0 collective-permute-start.8
  39.6 0.0 collective-permute-done.9.refs_4_
  39.6 2.2 %collective-permute-done.8.refs_3_ = bf16[272,1024]{1,0:T(8,128)(2,1)S(1)} collective-permute-done((bf16[272,1024]{1,0:T(8,128)(2,1)}, bf16[272,1024]{1,0:T(8,128)(2,1)S(1)}, u32[]{:S(2)}, u32[]{:S(2)}) %collective-permute-start.8) | collective-permute-done | bytes 557088 | tf_op jit(solution)/shard_map/ppermute | solution.py:58
  41.8 0.0 copy-done.1
  41.8 12.9 %shard_map.106 = (bf16[256,2048]{1,0:T(8,128)(2,1)}, s32[1]{0:T(128)}) custom-call(bf16[256,2048]{1,0:T(8,128)(2,1)S(1)} %bitcast.10, bf16[272,1024]{1,0:T(8,128)(2,1)S(1)} %copy-done, bf16[272,1024]{1,0:T(8,128)(2,1)} %collective-permute-done.6.refs_1_, bf16[272,1024]{1,0:T(8,128)(2,1)S(1)} %collective-permute-done.7.refs_2_, ...), custom_call_target="tpu_custom_call" | custom-call | flops 100000000 | bytes 1048576 | tf_op jit(solution)/shard_map/pallas_call | solution.py:502
  54.7 2.0 %collective-permute-done.5.refs_6_.refs_4_ = bf16[2112,256]{1,0:T(8,128)(2,1)} collective-permute-done((bf16[2112,256]{1,0:T(8,128)(2,1)S(1)}, bf16[2112,256]{1,0:T(8,128)(2,1)}, u32[]{:S(2)}, u32[]{:S(2)}) %collective-permute-start.5) | collective-permute-done | bytes 1081376 | tf_op jit(solution)/shard_map/ppermute | solution.py:58
  56.7 0.0 collective-permute-done.4.refs_5_.refs_3_
  56.7 4.1 %collective-permute-done.3.refs_4_.refs_2_ = bf16[2112,256]{1,0:T(8,128)(2,1)} collective-permute-done((bf16[2112,256]{1,0:T(8,128)(2,1)S(1)}, bf16[2112,256]{1,0:T(8,128)(2,1)}, u32[]{:S(2)}, u32[]{:S(2)}) %collective-permute-start.3) | collective-permute-done | bytes 1081376 | tf_op jit(solution)/shard_map/ppermute | solution.py:58
  60.8 0.0 copy-done.3
  60.8 0.0 copy-done.5
  60.8 0.0 copy-done.7
  60.8 0.0 copy-start.9
  60.8 11.4 %shard_map.107 = (bf16[512,512]{1,0:T(8,128)(2,1)S(1)}, bf16[512,512]{1,0:T(8,128)(2,1)S(1)}, bf16[512,512]{1,0:T(8,128)(2,1)S(1)}, s32[64,128]{1,0:T(8,128)S(1)}) custom-call(bf16[528,768]{1,0:T(8,128)(2,1)S(1)} %copy-done.3, bf16[528,768]{1,0:T(8,128)(2,1)S(1)} %copy-done.5, bf16[528,768]{1,0:T(8,128)(2,1)S(1)} %copy-done.7, ...), custom_call_target="tpu_custom_call" | custom-call | flops 12000000000 | bytes 1048576 | tf_op jit(solution)/shard_map/pallas_call | solution.py:455
  72.1 1.8 %collective-permute-start.10 = (bf16[512,512]{1,0:T(8,128)(2,1)S(1)}, bf16[512,512]{1,0:T(8,128)(2,1)S(1)}, u32[]{:S(2)}, u32[]{:S(2)}) collective-permute-start(bf16[512,512]{1,0:T(8,128)(2,1)S(1)} %get-tuple-element.22), channel_id=1, source_target_pairs={{0,96},{1,25},{2,98},{3,27},{4,100},{5,29},{6,102},{7,31},{8,104},... | collective-permute-start | bytes 1572872 | tf_op jit(solution)/shard_map/ppermute | solution.py:58
  73.9 2.2 %collective-permute-start.11 = (bf16[512,512]{1,0:T(8,128)(2,1)S(1)}, bf16[512,512]{1,0:T(8,128)(2,1)S(1)}, u32[]{:S(2)}, u32[]{:S(2)}) collective-permute-start(bf16[512,512]{1,0:T(8,128)(2,1)S(1)} %get-tuple-element.23), channel_id=1, source_target_pairs={{0,64},{1,17},{2,66},{3,19},{4,68},{5,21},{6,70},{7,23},{8,72},{9,... | collective-permute-start | bytes 1572872 | tf_op jit(solution)/shard_map/ppermute | solution.py:58
  76.2 0.4 collective-permute-start.12
  76.6 0.0 copy-done.9
  76.6 4.4 %shard_map.108.refs_0_ = bf16[512,512]{1,0:T(8,128)(2,1)S(1)} custom-call(bf16[512,512]{1,0:T(8,128)(2,1)S(1)} %copy-done.9, bf16[2112,256]{1,0:T(8,128)(2,1)S(1)} %shard_map.105.refs_3_.refs_1_, bf16[2112,256]{1,0:T(8,128)(2,1)} %collective-permute-done.3.refs_4_.refs_2_, bf16[2112,256]{1,0:T(8,128)(2,1)} %collective-permute-done.4.refs_5_.refs_3_, ...), custom_call_target="tpu_custom_call" | custom-call | flops 4000000000 | bytes 1048576 | tf_op jit(solution)/shard_map/pallas_call | solution.py:455
  81.0 0.4 collective-permute-done.10.refs_1_
  81.4 3.3 %collective-permute-done.11.refs_2_ = bf16[512,512]{1,0:T(8,128)(2,1)S(1)} collective-permute-done((bf16[512,512]{1,0:T(8,128)(2,1)S(1)}, bf16[512,512]{1,0:T(8,128)(2,1)S(1)}, u32[]{:S(2)}, u32[]{:S(2)}) %collective-permute-start.11) | collective-permute-done | bytes 524320 | tf_op jit(solution)/shard_map/ppermute | solution.py:58
  84.7 5.5 %collective-permute-done.12.refs_3_ = bf16[512,512]{1,0:T(8,128)(2,1)S(1)} collective-permute-done((bf16[512,512]{1,0:T(8,128)(2,1)S(1)}, bf16[512,512]{1,0:T(8,128)(2,1)S(1)}, u32[]{:S(2)}, u32[]{:S(2)}) %collective-permute-start.12) | collective-permute-done | bytes 524320 | tf_op jit(solution)/shard_map/ppermute | solution.py:58
  90.2 1.3 %shard_map.109 = bf16[512,2048]{1,0:T(8,128)(2,1)} custom-call(bf16[512,512]{1,0:T(8,128)(2,1)S(1)} %shard_map.108.refs_0_, bf16[512,512]{1,0:T(8,128)(2,1)S(1)} %collective-permute-done.10.refs_1_, bf16[512,512]{1,0:T(8,128)(2,1)S(1)} %collective-permute-done.11.refs_2_, bf16[512,512]{1,0:T(8,128)(2,1)S(1)} %collective-permute-done.12.refs_3_), custom_call_target="tpu_custom_call" | custom-call | flops 2000000000 | bytes 1048576 | tf_op jit(solution)/shard_map/pallas_call | solution.py:227
  (5 shorter events, 0.0 us)
Async XLA Ops:
  4.6 15.4 %collective-permute-start = (bf16[528,768]{1,0:T(8,128)(2,1)}, bf16[528,768]{1,0:T(8,128)(2,1)S(1)}, u32[]{:S(2)}, u32[]{:S(2)}) collective-permute-start(bf16[528,768]{1,0:T(8,128)(2,1)} %get-tuple-element.16), channel_id=1, source_target_pairs={{0,32},{1,9},{2,34},{3,11},{4,36},{5,13},{6,38},{7,15},{8,40},{9,1... | collective-permute-start | bytes 2433032 | tf_op jit(solution)/shard_map/ppermute | solution.py:58
  6.2 21.9 %collective-permute-start.1 = (bf16[528,768]{1,0:T(8,128)(2,1)}, bf16[528,768]{1,0:T(8,128)(2,1)S(1)}, u32[]{:S(2)}, u32[]{:S(2)}) collective-permute-start(bf16[528,768]{1,0:T(8,128)(2,1)} %get-tuple-element.17), channel_id=1, source_target_pairs={{0,64},{1,17},{2,66},{3,19},{4,68},{5,21},{6,70},{7,23},{8,72},{9,... | collective-permute-start | bytes 2433032 | tf_op jit(solution)/shard_map/ppermute | solution.py:58
  8.9 19.1 %collective-permute-start.2 = (bf16[528,768]{1,0:T(8,128)(2,1)}, bf16[528,768]{1,0:T(8,128)(2,1)S(1)}, u32[]{:S(2)}, u32[]{:S(2)}) collective-permute-start(bf16[528,768]{1,0:T(8,128)(2,1)} %get-tuple-element.18), channel_id=1, source_target_pairs={{0,96},{1,25},{2,98},{3,27},{4,100},{5,29},{6,102},{7,31},{8,104},... | collective-permute-start | bytes 2433032 | tf_op jit(solution)/shard_map/ppermute | solution.py:58
  10.4 23.7 %collective-permute-start.7 = (bf16[272,1024]{1,0:T(8,128)(2,1)}, bf16[272,1024]{1,0:T(8,128)(2,1)S(1)}, u32[]{:S(2)}, u32[]{:S(2)}) collective-permute-start(bf16[272,1024]{1,0:T(8,128)(2,1)} %get-tuple-element.19.refs_0_), channel_id=1, source_target_pairs={{0,4},{1,5},{2,6},{3,7},{8,12},{9,13},{10,14},{11,15},{16,20},{17,... | collective-permute-start | bytes 1671176 | tf_op jit(solution)/shard_map/ppermute | solution.py:58
  16.2 23.5 %collective-permute-start.6 = (bf16[272,1024]{1,0:T(8,128)(2,1)}, bf16[272,1024]{1,0:T(8,128)(2,1)}, u32[]{:S(2)}, u32[]{:S(2)}) collective-permute-start(bf16[272,1024]{1,0:T(8,128)(2,1)} %get-tuple-element.19.refs_0_), channel_id=1, source_target_pairs={{0,2},{1,3},{2,4},{3,5},{4,6},{5,7},{8,10},{9,11},{10,12},{11,13},... | collective-permute-start | bytes 1671176 | tf_op jit(solution)/shard_map/ppermute | solution.py:58
  19.9 9.3 %copy-start.2 = (bf16[528,768]{1,0:T(8,128)(2,1)}, bf16[528,768]{1,0:T(8,128)(2,1)S(1)}, u32[]{:S(2)}) copy-start(bf16[528,768]{1,0:T(8,128)(2,1)S(1)} %collective-permute-done.refs_1_.refs_0_) | copy-start | bytes 2433028
  28.1 1.2 %copy-start.4 = (bf16[528,768]{1,0:T(8,128)(2,1)}, bf16[528,768]{1,0:T(8,128)(2,1)S(1)}, u32[]{:S(2)}) copy-start(bf16[528,768]{1,0:T(8,128)(2,1)S(1)} %collective-permute-done.1.refs_2_.refs_1_) | copy-start | bytes 2433028
  28.1 1.2 %copy-start.6 = (bf16[528,768]{1,0:T(8,128)(2,1)}, bf16[528,768]{1,0:T(8,128)(2,1)S(1)}, u32[]{:S(2)}) copy-start(bf16[528,768]{1,0:T(8,128)(2,1)S(1)} %collective-permute-done.2.refs_3_.refs_2_) | copy-start | bytes 2433028
  28.1 1.1 %copy-start.8 = (bf16[528,256]{1,0:T(8,128)(2,1)S(1)}, bf16[528,256]{1,0:T(8,128)(2,1)}, u32[]{:S(2)}) copy-start(bf16[528,256]{1,0:T(8,128)(2,1)} %get-tuple-element.15.refs_0_) | copy-start | bytes 811012
  29.2 4.8 %copy-start = (bf16[272,1024]{1,0:T(8,128)(2,1)S(1)}, bf16[272,1024]{1,0:T(8,128)(2,1)}, u32[]{:S(2)}) copy-start(bf16[272,1024]{1,0:T(8,128)(2,1)} %get-tuple-element.19.refs_0_) | copy-start | bytes 1671172
  29.3 12.5 %copy-start.1 = (bf16[1,256,2048]{2,1,0:T(8,128)(2,1)S(1)}, bf16[1,256,2048]{2,1,0:T(8,128)(2,1)}, u32[]{:S(2)}) copy-start(bf16[1,256,2048]{2,1,0:T(8,128)(2,1)} %param.14) | copy-start | bytes 3145732
  29.3 27.3 %collective-permute-start.5 = (bf16[2112,256]{1,0:T(8,128)(2,1)S(1)}, bf16[2112,256]{1,0:T(8,128)(2,1)}, u32[]{:S(2)}, u32[]{:S(2)}) collective-permute-start(bf16[2112,256]{1,0:T(8,128)(2,1)S(1)} %shard_map.105.refs_3_.refs_1_), channel_id=1, source_target_pairs={{0,24},{1,97},{2,26},{3,99},{4,28},{5,101},{6,30},{7,103},{8,0},{9... | collective-permute-start | bytes 3244040 | tf_op jit(solution)/shard_map/ppermute | solution.py:58
  32.4 24.3 %collective-permute-start.4 = (bf16[2112,256]{1,0:T(8,128)(2,1)S(1)}, bf16[2112,256]{1,0:T(8,128)(2,1)}, u32[]{:S(2)}, u32[]{:S(2)}) collective-permute-start(bf16[2112,256]{1,0:T(8,128)(2,1)S(1)} %shard_map.105.refs_3_.refs_1_), channel_id=1, source_target_pairs={{0,16},{1,65},{2,18},{3,67},{4,20},{5,69},{6,22},{7,71},{8,24},{9,... | collective-permute-start | bytes 3244040 | tf_op jit(solution)/shard_map/ppermute | solution.py:58
  33.0 27.7 %collective-permute-start.3 = (bf16[2112,256]{1,0:T(8,128)(2,1)S(1)}, bf16[2112,256]{1,0:T(8,128)(2,1)}, u32[]{:S(2)}, u32[]{:S(2)}) collective-permute-start(bf16[2112,256]{1,0:T(8,128)(2,1)S(1)} %shard_map.105.refs_3_.refs_1_), channel_id=1, source_target_pairs={{0,8},{1,33},{2,10},{3,35},{4,12},{5,37},{6,14},{7,39},{8,16},{9,4... | collective-permute-start | bytes 3244040 | tf_op jit(solution)/shard_map/ppermute | solution.py:58
  34.1 5.6 %collective-permute-start.9 = (bf16[272,1024]{1,0:T(8,128)(2,1)S(1)}, bf16[272,1024]{1,0:T(8,128)(2,1)S(1)}, u32[]{:S(2)}, u32[]{:S(2)}) collective-permute-start(bf16[272,1024]{1,0:T(8,128)(2,1)S(1)} %broadcast_select_fusion), channel_id=1, source_target_pairs={{0,1},{1,0},{2,3},{3,2},{4,5},{5,4},{6,7},{7,6},{8,9},{9,8},{10,11... | collective-permute-start | bytes 1671176 | tf_op jit(solution)/shard_map/ppermute | solution.py:58
  39.6 2.2 %collective-permute-start.8 = (bf16[272,1024]{1,0:T(8,128)(2,1)}, bf16[272,1024]{1,0:T(8,128)(2,1)S(1)}, u32[]{:S(2)}, u32[]{:S(2)}) collective-permute-start(bf16[272,1024]{1,0:T(8,128)(2,1)} %collective-permute-done.6.refs_1_), channel_id=1, source_target_pairs={{0,1},{1,0},{2,3},{3,2},{4,5},{5,4},{6,7},{7,6},{8,9},{9,8},{10,11... | collective-permute-start | bytes 1671176 | tf_op jit(solution)/shard_map/ppermute | solution.py:58
  41.8 19.0 %copy-start.3 = (bf16[528,768]{1,0:T(8,128)(2,1)S(1)}, bf16[528,768]{1,0:T(8,128)(2,1)}, u32[]{:S(2)}) copy-start(bf16[528,768]{1,0:T(8,128)(2,1)} %copy-done.2) | copy-start | bytes 2433028
  41.8 19.0 %copy-start.5 = (bf16[528,768]{1,0:T(8,128)(2,1)S(1)}, bf16[528,768]{1,0:T(8,128)(2,1)}, u32[]{:S(2)}) copy-start(bf16[528,768]{1,0:T(8,128)(2,1)} %copy-done.4) | copy-start | bytes 2433028
  41.8 19.0 %copy-start.7 = (bf16[528,768]{1,0:T(8,128)(2,1)S(1)}, bf16[528,768]{1,0:T(8,128)(2,1)}, u32[]{:S(2)}) copy-start(bf16[528,768]{1,0:T(8,128)(2,1)} %copy-done.6) | copy-start | bytes 2433028
  60.8 15.8 %copy-start.9 = (bf16[512,512]{1,0:T(8,128)(2,1)S(1)}, bf16[512,512]{1,0:T(8,128)(2,1)}, u32[]{:S(2)}) copy-start(bf16[512,512]{1,0:T(8,128)(2,1)} %get-tuple-element.14.refs_0_) | copy-start | bytes 1572868
  72.1 9.2 %collective-permute-start.10 = (bf16[512,512]{1,0:T(8,128)(2,1)S(1)}, bf16[512,512]{1,0:T(8,128)(2,1)S(1)}, u32[]{:S(2)}, u32[]{:S(2)}) collective-permute-start(bf16[512,512]{1,0:T(8,128)(2,1)S(1)} %get-tuple-element.22), channel_id=1, source_target_pairs={{0,96},{1,25},{2,98},{3,27},{4,100},{5,29},{6,102},{7,31},{8,104},... | collective-permute-start | bytes 1572872 | tf_op jit(solution)/shard_map/ppermute | solution.py:58
  73.9 10.8 %collective-permute-start.11 = (bf16[512,512]{1,0:T(8,128)(2,1)S(1)}, bf16[512,512]{1,0:T(8,128)(2,1)S(1)}, u32[]{:S(2)}, u32[]{:S(2)}) collective-permute-start(bf16[512,512]{1,0:T(8,128)(2,1)S(1)} %get-tuple-element.23), channel_id=1, source_target_pairs={{0,64},{1,17},{2,66},{3,19},{4,68},{5,21},{6,70},{7,23},{8,72},{9,... | collective-permute-start | bytes 1572872 | tf_op jit(solution)/shard_map/ppermute | solution.py:58
  76.2 14.1 %collective-permute-start.12 = (bf16[512,512]{1,0:T(8,128)(2,1)S(1)}, bf16[512,512]{1,0:T(8,128)(2,1)S(1)}, u32[]{:S(2)}, u32[]{:S(2)}) collective-permute-start(bf16[512,512]{1,0:T(8,128)(2,1)S(1)} %get-tuple-element.24), channel_id=1, source_target_pairs={{0,32},{1,9},{2,34},{3,11},{4,36},{5,13},{6,38},{7,15},{8,40},{9,1... | collective-permute-start | bytes 1572872 | tf_op jit(solution)/shard_map/ppermute | solution.py:58

commit v4 on v3

--- a/solution.py
+++ b/solution.py
@@ -98,8 +98,8 @@
 
 
 def split_kernel(home_in, fill_in, doc_in, k_ref, v_ref, q_ref, lk_ref, lv_ref, *refs):
-    outs, packed_out = refs[: SIDE + 1], refs[SIDE + 1]
-    refs = refs[SIDE + 2 :]
+    outs, own_q_out, far_q_out, packed_out = refs[:SIDE], *refs[SIDE : SIDE + 3]
+    refs = refs[SIDE + 3 :]
     home, fill, docs, pieces, own_q, packed, sems, few_sems, out_sems = refs
     mine = where_am_i()[0]
     few = [
@@ -155,27 +155,29 @@
     for k in ORDER + (0,):
         for copy in copies[k]:
             copy.wait()
-        source = pieces.at[k] if k else pieces.at[0, :, pl.ds(0, KVW)]
+        source = pieces.at[k] if k & 1 else pieces.at[k, :, pl.ds(0, KVW)]
         done.append(pltpu.make_async_copy(source, outs[k], out_sems.at[k]))
         done[-1].start()
-    done.append(pltpu.make_async_copy(own_q, outs[SIDE], out_sems.at[SIDE]))
-    done[-1].start()
+    far_q = pieces.at[2, pl.ds(0, ROWS), pl.ds(KVW, QW)]
+    for n, (source, to) in enumerate(((own_q, own_q_out), (far_q, far_q_out))):
+        done.append(pltpu.make_async_copy(source, to, out_sems.at[SIDE + n]))
+        done[-1].start()
     for copy in long_copies:
         copy.wait()
-    done.append(pltpu.make_async_copy(packed, packed_out, out_sems.at[SIDE + 1]))
+    done.append(pltpu.make_async_copy(packed, packed_out, out_sems.at[SIDE + 2]))
     done[-1].start()
     for copy in done:
         copy.wait()
 
 
 def split(home, fill, docs, keys, values, queries, long_keys, long_values):
-    shapes = [(PIECE, KVW)] + [(PIECE, KVW + QW)] * (SIDE - 1)
-    shapes += [(ROWS, QW), (LROWS + EXTRA, 2 * KVH * HD)]
+    shapes = [(PIECE, KVW + QW if k & 1 else KVW) for k in range(SIDE)]
+    shapes += [(ROWS, QW)] * 2 + [(LROWS + EXTRA, 2 * KVH * HD)]
     return pl.pallas_call(
         split_kernel,
         out_shape=[jax.ShapeDtypeStruct(shape, jnp.bfloat16) for shape in shapes],
         in_specs=[FAR] * 8,
-        out_specs=[FAR] * (SIDE + 2),
+        out_specs=[FAR] * (SIDE + 3),
         scratch_shapes=[
             pltpu.SMEM((SB,), jnp.int32),
             pltpu.SMEM((SB,), jnp.int32),
@@ -185,27 +187,11 @@
             pltpu.VMEM((LROWS + EXTRA, 2 * KVH * HD), jnp.bfloat16),
             pltpu.SemaphoreType.DMA((SIDE + 1, 3)),
             pltpu.SemaphoreType.DMA((3,)),
-            pltpu.SemaphoreType.DMA((SIDE + 2,)),
+            pltpu.SemaphoreType.DMA((SIDE + 3,)),
         ],
         compiler_params=pltpu.CompilerParams(vmem_limit_bytes=60 * MIB),
         cost_estimate=busy(2),
     )(home, fill, docs, keys, values, queries, long_keys, long_values)
-
-
-def stack_kernel(*refs):
-    for n in range(SIDE):
-        refs[-1][n * PIECE : (n + 1) * PIECE] = refs[n][:, :KVW]
-
-
-def stack(pieces):
-    return pl.pallas_call(
-        stack_kernel,
-        out_shape=jax.ShapeDtypeStruct((SIDE * PIECE, KVW), jnp.bfloat16),
-        in_specs=[VM] * SIDE,
-        out_specs=VM,
-        compiler_params=pltpu.CompilerParams(vmem_limit_bytes=2 * MIB),
-        cost_estimate=busy(1),
-    )(*pieces)
 
 
 def join_kernel(*refs):
@@ -319,7 +305,7 @@
     ]
     copies += [
         pltpu.make_async_copy(
-            q_parts[n].at[pl.ds(0, ROWS), pl.ds(KVW if k else 0, QW)],
+            q_parts[n].at[pl.ds(0, ROWS), pl.ds(KVW if k & 1 else 0, QW)],
             q_ref.at[pl.ds(n * ROWS, ROWS)],
             q_sems.at[n],
         )
@@ -466,7 +452,7 @@
     return (found[:count], found[count]) if first else (found, table)
 
 
-def long_kernel(q_in, *refs):
+def long_kernel(q_in, after, *refs):
     parts = refs[:5]
     out_ref, token, q_ref, bias_ref, sem = refs[5:]
     copy = pltpu.make_async_copy(q_in, q_ref, sem)
@@ -498,14 +484,14 @@
     lax.fori_loop(0, KVH, one_head, 0)
 
 
-def long_attention(queries, parts):
+def long_attention(queries, after, parts):
     return pl.pallas_call(
         long_kernel,
         out_shape=[
             jax.ShapeDtypeStruct((LROWS, QH * HD), jnp.bfloat16),
             jax.ShapeDtypeStruct((1,), jnp.int32),
         ],
-        in_specs=[FAR] + [VM] * 5,
+        in_specs=[FAR, HB] + [VM] * 5,
         out_specs=[VM, SM],
         scratch_shapes=[
             pltpu.VMEM((LROWS, QH * HD), jnp.bfloat16),
@@ -514,7 +500,7 @@
         ],
         compiler_params=pltpu.CompilerParams(vmem_limit_bytes=20 * MIB),
         cost_estimate=busy(0.1),
-    )(queries, *parts)
+    )(queries, after, *parts)
 
 
 def shards(
@@ -528,7 +514,7 @@
     long_values,
     long_docs,
 ):
-    *own, own_q, packed = split(
+    *own, own_q, far_q, packed = split(
         block_home.reshape(SB),
         block_fill.reshape(SB),
         long_docs.reshape(1, LROWS),
@@ -540,9 +526,10 @@
     )
     sent = {k: send(own[k], along_head(k)) for k in ORDER}
     line_parts = [sent[k] for k in (1, 2, 3)]
+    far_q = send(far_q, along_head(2))
     long_one = send(packed, up_chips(1))
     long_two = send(packed, up_chips(2))
-    stacked = stack([own[0]] + line_parts)
+    stacked = jnp.concatenate([own[0]] + [part[:, :KVW] for part in line_parts], axis=0)
     sent = {k: send(stacked, along_rows(k)) for k in ORDER[::-1]}
     kv_parts = [stacked] + [sent[k] for k in (1, 2, 3)]
     long_side = send(long_one, other_core)
@@ -550,10 +537,13 @@
     long_cross = send(jnp.where(core == 0, packed, long_two), other_core)
     long_out, token = long_attention(
         long_queries.reshape(LROWS, QH * HD),
+        far_q,
         [packed, long_one, long_two, long_side, long_cross],
     )
 
-    mixed, table = short_attention((1, 2, 3), None, [token], line_parts, kv_parts)
+    mixed, table = short_attention(
+        (1, 2, 3), None, [token], [line_parts[0], far_q, line_parts[2]], kv_parts
+    )
     back = [send(piece, along_head(-k)) for k, piece in zip((1, 2, 3), mixed)]
     kept, _ = short_attention((0,), table, [], [own_q], kv_parts)
     short_out = join([kept[0]] + back)

time: 92.3 us -> 87.2 us (0.945)
  waiting for transfers between devices: 31 us -> 24.1 us
  other arithmetic: 0.06 us -> 1.08 us
    ppermute x13 -> x14, waiting for transfers between devices: 31 us -> 24.1 us  [send(): return lax.ppermute(value, ('dp', 'ctx'), pairs(step))]
    concatenate x0 -> x1, other arithmetic: none -> 1.02 us  [shards(): jnp.concatenate([own[0]] + [part[:, :KVW] for part in line_parts], axis=0)]
    ppermute x13 -> x14, starting transfers between devices: 24.6 us -> 25.4 us  [send(): return lax.ppermute(value, ('dp', 'ctx'), pairs(step))]
  transfers between devices with their start and end apart: 13 -> 14, of which waited for: 8 -> 7; matrix products, arithmetic and copies ran while one was open for 0% -> 1% of each run, Pallas kernels for 19% -> 20%
where the time goes in v4:
time: 87.2 us; the launch traced here: 87 us
  Pallas kernels  34.5 us (40%)
  starting transfers between devices  25.4 us (29%)
  waiting for transfers between devices  24.1 us (28%)
  other arithmetic  1.08 us (1%)
  local copies, waits for them, and re-layouts  0.95 us (1%)
  between operations  0.93 us (1%)
    ppermute x14, starting transfers between devices, send(): return lax.ppermute(value, ('dp', 'ctx'), pairs(step))  25.4 us
    ppermute x14, waiting for transfers between devices, send(): return lax.ppermute(value, ('dp', 'ctx'), pairs(step))  24.1 us
    pallas_call x2, Pallas kernels, short_attention(): pl.pallas_call(functools.partial(short_kernel, shifts, first, len(after))...  16.4 us
    pallas_call x1, Pallas kernels, long_attention(): pl.pallas_call(long_kernel, out_shape=[jax.ShapeDtypeStruct((LROWS, QH *...  12.8 us
    pallas_call x1, Pallas kernels, split(): pl.pallas_call(split_kernel, out_shape=[jax.ShapeDtypeStruct(shape, jnp.b...  3.91 us
  transfers between devices with their start and end apart: 14, of which 7 were waited for; matrix products, arithmetic and copies ran while one was open for 1% of the time, Pallas kernels for 20%

profile of v4, /device:TPU:0, one launch (start us, length us, event | category | flops | bytes accessed | tf_op | source)
XLA Modules:
  0.0 87.0 jit_solution(4367207111944132116)
XLA Ops:
  0.6 3.9 %shard_map.104 = (bf16[528,256]{1,0:T(8,128)(2,1)}, bf16[528,768]{1,0:T(8,128)(2,1)}, bf16[528,256]{1,0:T(8,128)(2,1)}, bf16[528,768]{1,0:T(8,128)(2,1)}, bf16[5...) custom-call(s32[8]{0:T(128)} %bitcast.17, s32[8]{0:T(128)} %bitcast.18, s32[1,256]{1,0:T(1,128)} %doc_in.1, ...), custom_call_target="tpu_custom_call" | custom-call | flops 2000000000 | bytes 1048576 | tf_op jit(solution)/shard_map/pallas_call | solution.py:176
  4.6 0.0 copy-start
  4.6 1.6 %collective-permute-start = (bf16[528,768]{1,0:T(8,128)(2,1)}, bf16[528,768]{1,0:T(8,128)(2,1)S(1)}, u32[]{:S(2)}, u32[]{:S(2)}) collective-permute-start(bf16[528,768]{1,0:T(8,128)(2,1)} %get-tuple-element.17), channel_id=1, source_target_pairs={{0,32},{1,9},{2,34},{3,11},{4,36},{5,13},{6,38},{7,15},{8,40},{9,1... | collective-permute-start | bytes 2433032 | tf_op jit(solution)/shard_map/ppermute | solution.py:58
  6.2 1.7 %collective-permute-start.2 = (bf16[528,768]{1,0:T(8,128)(2,1)}, bf16[528,768]{1,0:T(8,128)(2,1)S(1)}, u32[]{:S(2)}, u32[]{:S(2)}) collective-permute-start(bf16[528,768]{1,0:T(8,128)(2,1)} %get-tuple-element.19), channel_id=1, source_target_pairs={{0,96},{1,25},{2,98},{3,27},{4,100},{5,29},{6,102},{7,31},{8,104},... | collective-permute-start | bytes 2433032 | tf_op jit(solution)/shard_map/ppermute | solution.py:58
  7.9 1.9 %collective-permute-start.1 = (bf16[528,256]{1,0:T(8,128)(2,1)}, bf16[528,256]{1,0:T(8,128)(2,1)S(1)}, u32[]{:S(2)}, u32[]{:S(2)}) collective-permute-start(bf16[528,256]{1,0:T(8,128)(2,1)} %get-tuple-element.18), channel_id=1, source_target_pairs={{0,64},{1,17},{2,66},{3,19},{4,68},{5,21},{6,70},{7,23},{8,72},{9,... | collective-permute-start | bytes 811016 | tf_op jit(solution)/shard_map/ppermute | solution.py:58
  9.8 5.8 %collective-permute-start.8 = (bf16[272,1024]{1,0:T(8,128)(2,1)}, bf16[272,1024]{1,0:T(8,128)(2,1)S(1)}, u32[]{:S(2)}, u32[]{:S(2)}) collective-permute-start(bf16[272,1024]{1,0:T(8,128)(2,1)} %get-tuple-element.21.refs_0_), channel_id=1, source_target_pairs={{0,4},{1,5},{2,6},{3,7},{8,12},{9,13},{10,14},{11,15},{16,20},{17,... | collective-permute-start | bytes 1671176 | tf_op jit(solution)/shard_map/ppermute | solution.py:58
  15.6 3.7 %collective-permute-start.7 = (bf16[272,1024]{1,0:T(8,128)(2,1)}, bf16[272,1024]{1,0:T(8,128)(2,1)}, u32[]{:S(2)}, u32[]{:S(2)}) collective-permute-start(bf16[272,1024]{1,0:T(8,128)(2,1)} %get-tuple-element.21.refs_0_), channel_id=1, source_target_pairs={{0,2},{1,3},{2,4},{3,5},{4,6},{5,7},{8,10},{9,11},{10,12},{11,13},... | collective-permute-start | bytes 1671176 | tf_op jit(solution)/shard_map/ppermute | solution.py:58
  19.3 0.0 collective-permute-done.refs_0_
  19.3 0.0 copy-start.2
  19.3 1.7 %collective-permute-start.6 = (bf16[512,512]{1,0:T(8,128)(2,1)}, bf16[512,512]{1,0:T(8,128)(2,1)}, u32[]{:S(2)}, u32[]{:S(2)}) collective-permute-start(bf16[512,512]{1,0:T(8,128)(2,1)} %get-tuple-element.20), channel_id=1, source_target_pairs={{0,64},{1,17},{2,66},{3,19},{4,68},{5,21},{6,70},{7,23},{8,72},{9,... | collective-permute-start | bytes 1572872 | tf_op jit(solution)/shard_map/ppermute | solution.py:58
  21.1 0.0 copy-start.1
  21.1 0.0 collective-permute-done.2.refs_2_
  21.1 0.0 copy-start.4
  21.1 0.9 %copy-done.4 = bf16[528,768]{1,0:T(8,128)(2,1)} copy-done((bf16[528,768]{1,0:T(8,128)(2,1)}, bf16[528,768]{1,0:T(8,128)(2,1)S(1)}, u32[]{:S(2)}) %copy-start.4) | copy-done | bytes 811032
  22.0 0.3 collective-permute-done.1
  22.3 0.0 copy-done.2
  22.3 1.0 %pad_maximum_fusion.refs_3_.refs_1_ = bf16[2112,256]{1,0:T(8,128)(2,1)S(1)} fusion(bf16[528,256]{1,0:T(8,128)(2,1)S(1)} %slice.9, bf16[528,256]{1,0:T(8,128)(2,1)S(1)} %collective-permute-done.1, bf16[528,256]{1,0:T(8,128)(2,1)S(1)} %slice.8, bf16[528,256]{1,0:T(8,128)(2,1)} %get-tuple-element.16), kind=kLoop, calls=%fused_computation | loop fusion | flops 4325376 | bytes 2162688 | tf_op jit(solution)/shard_map/concatenate | solution.py:532
  23.3 3.1 %collective-permute-start.5 = (bf16[2112,256]{1,0:T(8,128)(2,1)S(1)}, bf16[2112,256]{1,0:T(8,128)(2,1)}, u32[]{:S(2)}, u32[]{:S(2)}) collective-permute-start(bf16[2112,256]{1,0:T(8,128)(2,1)S(1)} %pad_maximum_fusion.refs_3_.refs_1_), channel_id=1, source_target_pairs={{0,24},{1,97},{2,26},{3,99},{4,28},{5,101},{6,30},{7,103},{8,0},{9... | collective-permute-start | bytes 3244040 | tf_op jit(solution)/shard_map/ppermute | solution.py:58
  26.4 0.6 collective-permute-start.4
  27.0 2.0 %collective-permute-done.8.refs_2_ = bf16[272,1024]{1,0:T(8,128)(2,1)S(1)} collective-permute-done((bf16[272,1024]{1,0:T(8,128)(2,1)}, bf16[272,1024]{1,0:T(8,128)(2,1)S(1)}, u32[]{:S(2)}, u32[]{:S(2)}) %collective-permute-start.8) | collective-permute-done | bytes 557088 | tf_op jit(solution)/shard_map/ppermute | solution.py:58
  29.0 1.6 %collective-permute-start.3 = (bf16[2112,256]{1,0:T(8,128)(2,1)S(1)}, bf16[2112,256]{1,0:T(8,128)(2,1)}, u32[]{:S(2)}, u32[]{:S(2)}) collective-permute-start(bf16[2112,256]{1,0:T(8,128)(2,1)S(1)} %pad_maximum_fusion.refs_3_.refs_1_), channel_id=1, source_target_pairs={{0,8},{1,33},{2,10},{3,35},{4,12},{5,37},{6,14},{7,39},{8,16},{9,4... | collective-permute-start | bytes 3244040 | tf_op jit(solution)/shard_map/ppermute | solution.py:58
  30.5 0.0 copy-done
  30.5 0.1 broadcast_select_fusion
  30.6 0.0 collective-permute-done.6.after.refs_1_
  30.6 0.1 collective-permute-start.10
  30.7 8.3 %collective-permute-done.7.refs_1_ = bf16[272,1024]{1,0:T(8,128)(2,1)} collective-permute-done((bf16[272,1024]{1,0:T(8,128)(2,1)}, bf16[272,1024]{1,0:T(8,128)(2,1)}, u32[]{:S(2)}, u32[]{:S(2)}) %collective-permute-start.7) | collective-permute-done | bytes 557088 | tf_op jit(solution)/shard_map/ppermute | solution.py:58
  39.0 0.0 collective-permute-start.9
  39.0 0.0 collective-permute-done.10.refs_4_
  39.0 2.2 %collective-permute-done.9.refs_3_ = bf16[272,1024]{1,0:T(8,128)(2,1)S(1)} collective-permute-done((bf16[272,1024]{1,0:T(8,128)(2,1)}, bf16[272,1024]{1,0:T(8,128)(2,1)S(1)}, u32[]{:S(2)}, u32[]{:S(2)}) %collective-permute-start.9) | collective-permute-done | bytes 557088 | tf_op jit(solution)/shard_map/ppermute | solution.py:58
  41.2 0.0 copy-done.1
  41.2 0.0 copy-start.3
  41.2 0.0 copy-start.5
  41.2 12.8 %shard_map.105 = (bf16[256,2048]{1,0:T(8,128)(2,1)}, s32[1]{0:T(128)}) custom-call(bf16[256,2048]{1,0:T(8,128)(2,1)S(1)} %bitcast.10, bf16[512,512]{1,0:T(8,128)(2,1)} %collective-permute-done.6.after.refs_1_, bf16[272,1024]{1,0:T(8,128)(2,1)S(1)} %copy-done, bf16[272,1024]{1,0:T(8,128)(2,1)} %collective-permute-done.7.refs_1_, ...), custom_call_target="tpu_custom_call" | custom-call | flops 100000000 | bytes 1048576 | tf_op jit(solution)/shard_map/pallas_call | solution.py:488
  54.1 0.0 collective-permute-done.5.refs_6_.refs_4_
  54.1 0.0 collective-permute-done.4.refs_5_.refs_3_
  54.1 0.6 collective-permute-done.3.refs_4_.refs_2_
  54.7 0.0 copy-done.3
  54.7 0.0 copy-done.5
  54.7 12.0 %shard_map.106 = (bf16[512,512]{1,0:T(8,128)(2,1)S(1)}, bf16[512,512]{1,0:T(8,128)(2,1)S(1)}, bf16[512,512]{1,0:T(8,128)(2,1)S(1)}, s32[64,128]{1,0:T(8,128)S(1)}) custom-call(bf16[528,768]{1,0:T(8,128)(2,1)S(1)} %copy-done.3, bf16[512,512]{1,0:T(8,128)(2,1)} %collective-permute-done.6.after.refs_1_, bf16[528,768]{1,0:T(8,128)(2,1)S(1)} %copy-done.5, ...), custom_call_target="tpu_custom_call" | custom-call | flops 12000000000 | bytes 1048576 | tf_op jit(solution)/shard_map/pallas_call | solution.py:441
  66.7 2.4 %collective-permute-start.11 = (bf16[512,512]{1,0:T(8,128)(2,1)S(1)}, bf16[512,512]{1,0:T(8,128)(2,1)S(1)}, u32[]{:S(2)}, u32[]{:S(2)}) collective-permute-start(bf16[512,512]{1,0:T(8,128)(2,1)S(1)} %get-tuple-element.24), channel_id=1, source_target_pairs={{0,96},{1,25},{2,98},{3,27},{4,100},{5,29},{6,102},{7,31},{8,104},... | collective-permute-start | bytes 1572872 | tf_op jit(solution)/shard_map/ppermute | solution.py:58
  69.1 1.1 %collective-permute-start.12 = (bf16[512,512]{1,0:T(8,128)(2,1)S(1)}, bf16[512,512]{1,0:T(8,128)(2,1)S(1)}, u32[]{:S(2)}, u32[]{:S(2)}) collective-permute-start(bf16[512,512]{1,0:T(8,128)(2,1)S(1)} %get-tuple-element.25), channel_id=1, source_target_pairs={{0,64},{1,17},{2,66},{3,19},{4,68},{5,21},{6,70},{7,23},{8,72},{9,... | collective-permute-start | bytes 1572872 | tf_op jit(solution)/shard_map/ppermute | solution.py:58
  70.3 0.0 collective-permute-start.13
  70.3 0.0 copy-done.6
  70.3 4.4 %shard_map.107.refs_0_ = bf16[512,512]{1,0:T(8,128)(2,1)S(1)} custom-call(bf16[512,512]{1,0:T(8,128)(2,1)S(1)} %copy-done.6, bf16[2112,256]{1,0:T(8,128)(2,1)S(1)} %pad_maximum_fusion.refs_3_.refs_1_, bf16[2112,256]{1,0:T(8,128)(2,1)} %collective-permute-done.3.refs_4_.refs_2_, bf16[2112,256]{1,0:T(8,128)(2,1)} %collective-permute-done.4.refs_5_.refs_3_, ...), custom_call_target="tpu_custom_call" | custom-call | flops 4000000000 | bytes 1048576 | tf_op jit(solution)/shard_map/pallas_call | solution.py:441
  74.7 6.8 %collective-permute-done.11.refs_1_ = bf16[512,512]{1,0:T(8,128)(2,1)S(1)} collective-permute-done((bf16[512,512]{1,0:T(8,128)(2,1)S(1)}, bf16[512,512]{1,0:T(8,128)(2,1)S(1)}, u32[]{:S(2)}, u32[]{:S(2)}) %collective-permute-start.11) | collective-permute-done | bytes 524320 | tf_op jit(solution)/shard_map/ppermute | solution.py:58
  81.5 0.0 collective-permute-done.12.refs_2_
  81.5 3.9 %collective-permute-done.13.refs_3_ = bf16[512,512]{1,0:T(8,128)(2,1)S(1)} collective-permute-done((bf16[512,512]{1,0:T(8,128)(2,1)S(1)}, bf16[512,512]{1,0:T(8,128)(2,1)S(1)}, u32[]{:S(2)}, u32[]{:S(2)}) %collective-permute-start.13) | collective-permute-done | bytes 524320 | tf_op jit(solution)/shard_map/ppermute | solution.py:58
  85.4 1.3 %shard_map.108 = bf16[512,2048]{1,0:T(8,128)(2,1)} custom-call(bf16[512,512]{1,0:T(8,128)(2,1)S(1)} %shard_map.107.refs_0_, bf16[512,512]{1,0:T(8,128)(2,1)S(1)} %collective-permute-done.11.refs_1_, bf16[512,512]{1,0:T(8,128)(2,1)S(1)} %collective-permute-done.12.refs_2_, bf16[512,512]{1,0:T(8,128)(2,1)S(1)} %collective-permute-done.13.refs_3_), custom_call_target="tpu_custom_call" | custom-call | flops 2000000000 | bytes 1048576 | tf_op jit(solution)/shard_map/pallas_call | solution.py:213
  (3 shorter events, 0.0 us)
Async XLA Ops:
  4.6 26.0 %copy-start = (bf16[272,1024]{1,0:T(8,128)(2,1)S(1)}, bf16[272,1024]{1,0:T(8,128)(2,1)}, u32[]{:S(2)}) copy-start(bf16[272,1024]{1,0:T(8,128)(2,1)} %get-tuple-element.21.refs_0_) | copy-start | bytes 1671172
  4.6 14.8 %collective-permute-start = (bf16[528,768]{1,0:T(8,128)(2,1)}, bf16[528,768]{1,0:T(8,128)(2,1)S(1)}, u32[]{:S(2)}, u32[]{:S(2)}) collective-permute-start(bf16[528,768]{1,0:T(8,128)(2,1)} %get-tuple-element.17), channel_id=1, source_target_pairs={{0,32},{1,9},{2,34},{3,11},{4,36},{5,13},{6,38},{7,15},{8,40},{9,1... | collective-permute-start | bytes 2433032 | tf_op jit(solution)/shard_map/ppermute | solution.py:58
  6.2 14.9 %collective-permute-start.2 = (bf16[528,768]{1,0:T(8,128)(2,1)}, bf16[528,768]{1,0:T(8,128)(2,1)S(1)}, u32[]{:S(2)}, u32[]{:S(2)}) collective-permute-start(bf16[528,768]{1,0:T(8,128)(2,1)} %get-tuple-element.19), channel_id=1, source_target_pairs={{0,96},{1,25},{2,98},{3,27},{4,100},{5,29},{6,102},{7,31},{8,104},... | collective-permute-start | bytes 2433032 | tf_op jit(solution)/shard_map/ppermute | solution.py:58
  7.9 14.4 %collective-permute-start.1 = (bf16[528,256]{1,0:T(8,128)(2,1)}, bf16[528,256]{1,0:T(8,128)(2,1)S(1)}, u32[]{:S(2)}, u32[]{:S(2)}) collective-permute-start(bf16[528,256]{1,0:T(8,128)(2,1)} %get-tuple-element.18), channel_id=1, source_target_pairs={{0,64},{1,17},{2,66},{3,19},{4,68},{5,21},{6,70},{7,23},{8,72},{9,... | collective-permute-start | bytes 811016 | tf_op jit(solution)/shard_map/ppermute | solution.py:58
  9.8 19.2 %collective-permute-start.8 = (bf16[272,1024]{1,0:T(8,128)(2,1)}, bf16[272,1024]{1,0:T(8,128)(2,1)S(1)}, u32[]{:S(2)}, u32[]{:S(2)}) collective-permute-start(bf16[272,1024]{1,0:T(8,128)(2,1)} %get-tuple-element.21.refs_0_), channel_id=1, source_target_pairs={{0,4},{1,5},{2,6},{3,7},{8,12},{9,13},{10,14},{11,15},{16,20},{17,... | collective-permute-start | bytes 1671176 | tf_op jit(solution)/shard_map/ppermute | solution.py:58
  15.6 23.5 %collective-permute-start.7 = (bf16[272,1024]{1,0:T(8,128)(2,1)}, bf16[272,1024]{1,0:T(8,128)(2,1)}, u32[]{:S(2)}, u32[]{:S(2)}) collective-permute-start(bf16[272,1024]{1,0:T(8,128)(2,1)} %get-tuple-element.21.refs_0_), channel_id=1, source_target_pairs={{0,2},{1,3},{2,4},{3,5},{4,6},{5,7},{8,10},{9,11},{10,12},{11,13},... | collective-permute-start | bytes 1671176 | tf_op jit(solution)/shard_map/ppermute | solution.py:58
  19.3 3.0 %copy-start.2 = (bf16[528,768]{1,0:T(8,128)(2,1)}, bf16[528,768]{1,0:T(8,128)(2,1)S(1)}, u32[]{:S(2)}) copy-start(bf16[528,768]{1,0:T(8,128)(2,1)S(1)} %collective-permute-done.refs_0_) | copy-start | bytes 2433028
  19.3 11.3 %collective-permute-start.6 = (bf16[512,512]{1,0:T(8,128)(2,1)}, bf16[512,512]{1,0:T(8,128)(2,1)}, u32[]{:S(2)}, u32[]{:S(2)}) collective-permute-start(bf16[512,512]{1,0:T(8,128)(2,1)} %get-tuple-element.20), channel_id=1, source_target_pairs={{0,64},{1,17},{2,66},{3,19},{4,68},{5,21},{6,70},{7,23},{8,72},{9,... | collective-permute-start | bytes 1572872 | tf_op jit(solution)/shard_map/ppermute | solution.py:58
  21.1 20.1 %copy-start.1 = (bf16[1,256,2048]{2,1,0:T(8,128)(2,1)S(1)}, bf16[1,256,2048]{2,1,0:T(8,128)(2,1)}, u32[]{:S(2)}) copy-start(bf16[1,256,2048]{2,1,0:T(8,128)(2,1)} %param.14) | copy-start | bytes 3145732
  21.1 0.9 %copy-start.4 = (bf16[528,768]{1,0:T(8,128)(2,1)}, bf16[528,768]{1,0:T(8,128)(2,1)S(1)}, u32[]{:S(2)}) copy-start(bf16[528,768]{1,0:T(8,128)(2,1)S(1)} %collective-permute-done.2.refs_2_) | copy-start | bytes 2433028
  23.3 30.8 %collective-permute-start.5 = (bf16[2112,256]{1,0:T(8,128)(2,1)S(1)}, bf16[2112,256]{1,0:T(8,128)(2,1)}, u32[]{:S(2)}, u32[]{:S(2)}) collective-permute-start(bf16[2112,256]{1,0:T(8,128)(2,1)S(1)} %pad_maximum_fusion.refs_3_.refs_1_), channel_id=1, source_target_pairs={{0,24},{1,97},{2,26},{3,99},{4,28},{5,101},{6,30},{7,103},{8,0},{9... | collective-permute-start | bytes 3244040 | tf_op jit(solution)/shard_map/ppermute | solution.py:58
  26.4 27.7 %collective-permute-start.4 = (bf16[2112,256]{1,0:T(8,128)(2,1)S(1)}, bf16[2112,256]{1,0:T(8,128)(2,1)}, u32[]{:S(2)}, u32[]{:S(2)}) collective-permute-start(bf16[2112,256]{1,0:T(8,128)(2,1)S(1)} %pad_maximum_fusion.refs_3_.refs_1_), channel_id=1, source_target_pairs={{0,16},{1,65},{2,18},{3,67},{4,20},{5,69},{6,22},{7,71},{8,24},{9,... | collective-permute-start | bytes 3244040 | tf_op jit(solution)/shard_map/ppermute | solution.py:58
  29.0 25.8 %collective-permute-start.3 = (bf16[2112,256]{1,0:T(8,128)(2,1)S(1)}, bf16[2112,256]{1,0:T(8,128)(2,1)}, u32[]{:S(2)}, u32[]{:S(2)}) collective-permute-start(bf16[2112,256]{1,0:T(8,128)(2,1)S(1)} %pad_maximum_fusion.refs_3_.refs_1_), channel_id=1, source_target_pairs={{0,8},{1,33},{2,10},{3,35},{4,12},{5,37},{6,14},{7,39},{8,16},{9,4... | collective-permute-start | bytes 3244040 | tf_op jit(solution)/shard_map/ppermute | solution.py:58
  30.6 8.4 %collective-permute-start.10 = (bf16[272,1024]{1,0:T(8,128)(2,1)S(1)}, bf16[272,1024]{1,0:T(8,128)(2,1)S(1)}, u32[]{:S(2)}, u32[]{:S(2)}) collective-permute-start(bf16[272,1024]{1,0:T(8,128)(2,1)S(1)} %broadcast_select_fusion), channel_id=1, source_target_pairs={{0,1},{1,0},{2,3},{3,2},{4,5},{5,4},{6,7},{7,6},{8,9},{9,8},{10,11... | collective-permute-start | bytes 1671176 | tf_op jit(solution)/shard_map/ppermute | solution.py:58
  39.0 2.2 %collective-permute-start.9 = (bf16[272,1024]{1,0:T(8,128)(2,1)}, bf16[272,1024]{1,0:T(8,128)(2,1)S(1)}, u32[]{:S(2)}, u32[]{:S(2)}) collective-permute-start(bf16[272,1024]{1,0:T(8,128)(2,1)} %collective-permute-done.7.refs_1_), channel_id=1, source_target_pairs={{0,1},{1,0},{2,3},{3,2},{4,5},{5,4},{6,7},{7,6},{8,9},{9,8},{10,11... | collective-permute-start | bytes 1671176 | tf_op jit(solution)/shard_map/ppermute | solution.py:58
  41.2 13.5 %copy-start.3 = (bf16[528,768]{1,0:T(8,128)(2,1)S(1)}, bf16[528,768]{1,0:T(8,128)(2,1)}, u32[]{:S(2)}) copy-start(bf16[528,768]{1,0:T(8,128)(2,1)} %copy-done.2) | copy-start | bytes 2433028
  41.2 13.5 %copy-start.5 = (bf16[528,768]{1,0:T(8,128)(2,1)S(1)}, bf16[528,768]{1,0:T(8,128)(2,1)}, u32[]{:S(2)}) copy-start(bf16[528,768]{1,0:T(8,128)(2,1)} %copy-done.4) | copy-start | bytes 2433028
  54.7 15.6 %copy-start.6 = (bf16[512,512]{1,0:T(8,128)(2,1)S(1)}, bf16[512,512]{1,0:T(8,128)(2,1)}, u32[]{:S(2)}) copy-start(bf16[512,512]{1,0:T(8,128)(2,1)} %get-tuple-element.15.refs_0_) | copy-start | bytes 1572868
  66.7 14.8 %collective-permute-start.11 = (bf16[512,512]{1,0:T(8,128)(2,1)S(1)}, bf16[512,512]{1,0:T(8,128)(2,1)S(1)}, u32[]{:S(2)}, u32[]{:S(2)}) collective-permute-start(bf16[512,512]{1,0:T(8,128)(2,1)S(1)} %get-tuple-element.24), channel_id=1, source_target_pairs={{0,96},{1,25},{2,98},{3,27},{4,100},{5,29},{6,102},{7,31},{8,104},... | collective-permute-start | bytes 1572872 | tf_op jit(solution)/shard_map/ppermute | solution.py:58
  69.1 12.4 %collective-permute-start.12 = (bf16[512,512]{1,0:T(8,128)(2,1)S(1)}, bf16[512,512]{1,0:T(8,128)(2,1)S(1)}, u32[]{:S(2)}, u32[]{:S(2)}) collective-permute-start(bf16[512,512]{1,0:T(8,128)(2,1)S(1)} %get-tuple-element.25), channel_id=1, source_target_pairs={{0,64},{1,17},{2,66},{3,19},{4,68},{5,21},{6,70},{7,23},{8,72},{9,... | collective-permute-start | bytes 1572872 | tf_op jit(solution)/shard_map/ppermute | solution.py:58
  70.3 15.2 %collective-permute-start.13 = (bf16[512,512]{1,0:T(8,128)(2,1)S(1)}, bf16[512,512]{1,0:T(8,128)(2,1)S(1)}, u32[]{:S(2)}, u32[]{:S(2)}) collective-permute-start(bf16[512,512]{1,0:T(8,128)(2,1)S(1)} %get-tuple-element.26), channel_id=1, source_target_pairs={{0,32},{1,9},{2,34},{3,11},{4,36},{5,13},{6,38},{7,15},{8,40},{9,1... | collective-permute-start | bytes 1572872 | tf_op jit(solution)/shard_map/ppermute | solution.py:58

commit v5 on v4

--- a/solution.py
+++ b/solution.py
@@ -221,14 +221,14 @@
     )(*pieces)
 
 
-def fill_table(kv_ref, table_ref):
+def fill_table(facts_ref, table_ref):
     head, line, core = where_am_i()
     shape = (GROUPS, HD)
     lane = lax.broadcasted_iota(jnp.int32, shape, 1)
     row = lax.broadcasted_iota(jnp.int32, shape, 0)
     facts = jnp.full(shape, -1.0, jnp.float32)
     for p in range(GROUPS):
-        piece = kv_ref[p * PIECE + ROWS : (p + 1) * PIECE, :HD].astype(jnp.float32)
+        piece = facts_ref[p].astype(jnp.float32)
         facts = jnp.where(lane == p, piece, facts)
     facts = facts.astype(jnp.int32)
 
@@ -290,7 +290,7 @@
     refs = refs[count + SIDE + waits :]
     if first:
         out_parts, table = refs[:count], refs[count]
-        table_ref, table_sem = refs[-2:]
+        table_ref, facts_ref, table_sem, facts_sems = refs[-4:]
         refs = refs[count + 1 :]
     else:
         table, out_parts = refs[0], refs[1 : 1 + count]
@@ -311,12 +311,25 @@
         )
         for n, k in enumerate(shifts)
     ]
+    if first:
+        fact_copies = [
+            pltpu.make_async_copy(
+                kv_parts[p // SIDE].at[
+                    pl.ds(p % SIDE * PIECE + ROWS, EXTRA), pl.ds(0, HD)
+                ],
+                facts_ref.at[p],
+                facts_sems.at[p],
+            )
+            for p in range(GROUPS)
+        ]
+        for copy in fact_copies:
+            copy.start()
     for copy in copies:
         copy.start()
-    for copy in copies:
-        copy.wait()
     if first:
-        fill_table(kv_ref, table_ref)
+        for copy in fact_copies:
+            copy.wait()
+        fill_table(facts_ref, table_ref)
         table_copy = pltpu.make_async_copy(table_ref, table, table_sem)
         table_copy.start()
         table_copy.wait()
@@ -345,6 +358,9 @@
         list_ref[2, spot] = ranks[n]
         list_ref[3, spot] = table[SB + b, k]
         spots = [old + jnp.where(level == i, 1, 0) for i, old in enumerate(spots)]
+
+    for copy in copies:
+        copy.wait()
 
     def rows_of(at):
         return pl.ds(pl.multiple_of(list_ref[0, at] * BLOCK, BLOCK), BLOCK)
@@ -437,7 +453,12 @@
     ]
     if first:
         outs = outs + [jax.ShapeDtypeStruct((4 * GROUPS, HD), jnp.int32)]
-        scratch += [pltpu.VMEM((4 * GROUPS, HD), jnp.int32), pltpu.SemaphoreType.DMA(())]
+        scratch += [
+            pltpu.VMEM((4 * GROUPS, HD), jnp.int32),
+            pltpu.VMEM((GROUPS, EXTRA, HD), jnp.bfloat16),
+            pltpu.SemaphoreType.DMA(()),
+            pltpu.SemaphoreType.DMA((GROUPS,)),
+        ]
     found = pl.pallas_call(
         functools.partial(short_kernel, shifts, first, len(after)),
         out_shape=outs,

time: 87.2 us -> 86 us (0.986)
  Pallas kernels: 34.5 us -> 33.3 us
    pallas_call x2, Pallas kernels: 16.4 us -> 15.2 us  [short_attention(): pl.pallas_call(functools.partial(short_kernel, shifts, first, len(after))...]
where the time goes in v5:
time: 86 us; the launch traced here: 85.7 us
  Pallas kernels  33.3 us (39%)
  starting transfers between devices  25.4 us (30%)
  waiting for transfers between devices  24.1 us (28%)
  other arithmetic  1.08 us (1%)
  local copies, waits for them, and re-layouts  0.95 us (1%)
  between operations  0.93 us (1%)
    ppermute x14, starting transfers between devices, send(): return lax.ppermute(value, ('dp', 'ctx'), pairs(step))  25.4 us
    ppermute x14, waiting for transfers between devices, send(): return lax.ppermute(value, ('dp', 'ctx'), pairs(step))  24.1 us
    pallas_call x2, Pallas kernels, short_attention(): pl.pallas_call(functools.partial(short_kernel, shifts, first, len(after))...  15.2 us
    pallas_call x1, Pallas kernels, long_attention(): pl.pallas_call(long_kernel, out_shape=[jax.ShapeDtypeStruct((LROWS, QH *...  12.8 us
    pallas_call x1, Pallas kernels, split(): pl.pallas_call(split_kernel, out_shape=[jax.ShapeDtypeStruct(shape, jnp.b...  3.91 us
  transfers between devices with their start and end apart: 14, of which 7 were waited for; matrix products, arithmetic and copies ran while one was open for 1% of the time, Pallas kernels for 20%

profile of v5, /device:TPU:0, one launch (start us, length us, event | category | flops | bytes accessed | tf_op | source)
XLA Modules:
  0.0 85.7 jit_solution(14435300451363682711)
XLA Ops:
  0.6 3.9 %shard_map.104 = (bf16[528,256]{1,0:T(8,128)(2,1)}, bf16[528,768]{1,0:T(8,128)(2,1)}, bf16[528,256]{1,0:T(8,128)(2,1)}, bf16[528,768]{1,0:T(8,128)(2,1)}, bf16[5...) custom-call(s32[8]{0:T(128)} %bitcast.17, s32[8]{0:T(128)} %bitcast.18, s32[1,256]{1,0:T(1,128)} %doc_in.1, ...), custom_call_target="tpu_custom_call" | custom-call | flops 2000000000 | bytes 1048576 | tf_op jit(solution)/shard_map/pallas_call | solution.py:176
  4.6 0.0 copy-start
  4.6 1.6 %collective-permute-start = (bf16[528,768]{1,0:T(8,128)(2,1)}, bf16[528,768]{1,0:T(8,128)(2,1)S(1)}, u32[]{:S(2)}, u32[]{:S(2)}) collective-permute-start(bf16[528,768]{1,0:T(8,128)(2,1)} %get-tuple-element.17), channel_id=1, source_target_pairs={{0,32},{1,9},{2,34},{3,11},{4,36},{5,13},{6,38},{7,15},{8,40},{9,1... | collective-permute-start | bytes 2433032 | tf_op jit(solution)/shard_map/ppermute | solution.py:58
  6.2 1.7 %collective-permute-start.2 = (bf16[528,768]{1,0:T(8,128)(2,1)}, bf16[528,768]{1,0:T(8,128)(2,1)S(1)}, u32[]{:S(2)}, u32[]{:S(2)}) collective-permute-start(bf16[528,768]{1,0:T(8,128)(2,1)} %get-tuple-element.19), channel_id=1, source_target_pairs={{0,96},{1,25},{2,98},{3,27},{4,100},{5,29},{6,102},{7,31},{8,104},... | collective-permute-start | bytes 2433032 | tf_op jit(solution)/shard_map/ppermute | solution.py:58
  7.9 1.9 %collective-permute-start.1 = (bf16[528,256]{1,0:T(8,128)(2,1)}, bf16[528,256]{1,0:T(8,128)(2,1)S(1)}, u32[]{:S(2)}, u32[]{:S(2)}) collective-permute-start(bf16[528,256]{1,0:T(8,128)(2,1)} %get-tuple-element.18), channel_id=1, source_target_pairs={{0,64},{1,17},{2,66},{3,19},{4,68},{5,21},{6,70},{7,23},{8,72},{9,... | collective-permute-start | bytes 811016 | tf_op jit(solution)/shard_map/ppermute | solution.py:58
  9.8 5.8 %collective-permute-start.8 = (bf16[272,1024]{1,0:T(8,128)(2,1)}, bf16[272,1024]{1,0:T(8,128)(2,1)S(1)}, u32[]{:S(2)}, u32[]{:S(2)}) collective-permute-start(bf16[272,1024]{1,0:T(8,128)(2,1)} %get-tuple-element.21.refs_0_), channel_id=1, source_target_pairs={{0,4},{1,5},{2,6},{3,7},{8,12},{9,13},{10,14},{11,15},{16,20},{17,... | collective-permute-start | bytes 1671176 | tf_op jit(solution)/shard_map/ppermute | solution.py:58
  15.6 3.7 %collective-permute-start.7 = (bf16[272,1024]{1,0:T(8,128)(2,1)}, bf16[272,1024]{1,0:T(8,128)(2,1)}, u32[]{:S(2)}, u32[]{:S(2)}) collective-permute-start(bf16[272,1024]{1,0:T(8,128)(2,1)} %get-tuple-element.21.refs_0_), channel_id=1, source_target_pairs={{0,2},{1,3},{2,4},{3,5},{4,6},{5,7},{8,10},{9,11},{10,12},{11,13},... | collective-permute-start | bytes 1671176 | tf_op jit(solution)/shard_map/ppermute | solution.py:58
  19.3 0.0 collective-permute-done.refs_0_
  19.3 1.7 %collective-permute-start.6 = (bf16[512,512]{1,0:T(8,128)(2,1)}, bf16[512,512]{1,0:T(8,128)(2,1)}, u32[]{:S(2)}, u32[]{:S(2)}) collective-permute-start(bf16[512,512]{1,0:T(8,128)(2,1)} %get-tuple-element.20), channel_id=1, source_target_pairs={{0,64},{1,17},{2,66},{3,19},{4,68},{5,21},{6,70},{7,23},{8,72},{9,... | collective-permute-start | bytes 1572872 | tf_op jit(solution)/shard_map/ppermute | solution.py:58
  21.1 0.0 copy-start.1
  21.1 0.0 collective-permute-done.2.refs_2_
  21.1 0.0 copy-start.4
  21.1 0.9 %copy-done.4 = bf16[528,768]{1,0:T(8,128)(2,1)} copy-done((bf16[528,768]{1,0:T(8,128)(2,1)}, bf16[528,768]{1,0:T(8,128)(2,1)S(1)}, u32[]{:S(2)}) %copy-start.4) | copy-done | bytes 811032
  22.0 0.3 collective-permute-done.1
  22.3 0.0 copy-done.2
  22.3 1.0 %pad_maximum_fusion.refs_3_.refs_1_ = bf16[2112,256]{1,0:T(8,128)(2,1)S(1)} fusion(bf16[528,256]{1,0:T(8,128)(2,1)S(1)} %slice.9, bf16[528,256]{1,0:T(8,128)(2,1)S(1)} %collective-permute-done.1, bf16[528,256]{1,0:T(8,128)(2,1)S(1)} %slice.8, bf16[528,256]{1,0:T(8,128)(2,1)} %get-tuple-element.16), kind=kLoop, calls=%fused_computation | loop fusion | flops 4325376 | bytes 2162688 | tf_op jit(solution)/shard_map/concatenate | solution.py:553
  23.3 3.1 %collective-permute-start.5 = (bf16[2112,256]{1,0:T(8,128)(2,1)S(1)}, bf16[2112,256]{1,0:T(8,128)(2,1)}, u32[]{:S(2)}, u32[]{:S(2)}) collective-permute-start(bf16[2112,256]{1,0:T(8,128)(2,1)S(1)} %pad_maximum_fusion.refs_3_.refs_1_), channel_id=1, source_target_pairs={{0,24},{1,97},{2,26},{3,99},{4,28},{5,101},{6,30},{7,103},{8,0},{9... | collective-permute-start | bytes 3244040 | tf_op jit(solution)/shard_map/ppermute | solution.py:58
  26.4 0.6 collective-permute-start.4
  27.0 2.0 %collective-permute-done.8.refs_2_ = bf16[272,1024]{1,0:T(8,128)(2,1)S(1)} collective-permute-done((bf16[272,1024]{1,0:T(8,128)(2,1)}, bf16[272,1024]{1,0:T(8,128)(2,1)S(1)}, u32[]{:S(2)}, u32[]{:S(2)}) %collective-permute-start.8) | collective-permute-done | bytes 557088 | tf_op jit(solution)/shard_map/ppermute | solution.py:58
  29.0 1.6 %collective-permute-start.3 = (bf16[2112,256]{1,0:T(8,128)(2,1)S(1)}, bf16[2112,256]{1,0:T(8,128)(2,1)}, u32[]{:S(2)}, u32[]{:S(2)}) collective-permute-start(bf16[2112,256]{1,0:T(8,128)(2,1)S(1)} %pad_maximum_fusion.refs_3_.refs_1_), channel_id=1, source_target_pairs={{0,8},{1,33},{2,10},{3,35},{4,12},{5,37},{6,14},{7,39},{8,16},{9,4... | collective-permute-start | bytes 3244040 | tf_op jit(solution)/shard_map/ppermute | solution.py:58
  30.5 0.0 copy-done
  30.5 0.1 broadcast_select_fusion
  30.6 0.0 collective-permute-done.6.after.refs_1_
  30.6 0.1 collective-permute-start.10
  30.7 8.3 %collective-permute-done.7.refs_1_ = bf16[272,1024]{1,0:T(8,128)(2,1)} collective-permute-done((bf16[272,1024]{1,0:T(8,128)(2,1)}, bf16[272,1024]{1,0:T(8,128)(2,1)}, u32[]{:S(2)}, u32[]{:S(2)}) %collective-permute-start.7) | collective-permute-done | bytes 557088 | tf_op jit(solution)/shard_map/ppermute | solution.py:58
  39.0 0.0 collective-permute-start.9
  39.0 0.0 collective-permute-done.10.refs_4_
  39.0 2.2 %collective-permute-done.9.refs_3_ = bf16[272,1024]{1,0:T(8,128)(2,1)S(1)} collective-permute-done((bf16[272,1024]{1,0:T(8,128)(2,1)}, bf16[272,1024]{1,0:T(8,128)(2,1)S(1)}, u32[]{:S(2)}, u32[]{:S(2)}) %collective-permute-start.9) | collective-permute-done | bytes 557088 | tf_op jit(solution)/shard_map/ppermute | solution.py:58
  41.2 0.0 copy-done.1
  41.2 0.0 copy-start.3
  41.2 0.0 copy-start.5
  41.2 12.8 %shard_map.105 = (bf16[256,2048]{1,0:T(8,128)(2,1)}, s32[1]{0:T(128)}) custom-call(bf16[256,2048]{1,0:T(8,128)(2,1)S(1)} %bitcast.10, bf16[512,512]{1,0:T(8,128)(2,1)} %collective-permute-done.6.after.refs_1_, bf16[272,1024]{1,0:T(8,128)(2,1)S(1)} %copy-done, bf16[272,1024]{1,0:T(8,128)(2,1)} %collective-permute-done.7.refs_1_, ...), custom_call_target="tpu_custom_call" | custom-call | flops 100000000 | bytes 1048576 | tf_op jit(solution)/shard_map/pallas_call | solution.py:509
  54.1 0.0 collective-permute-done.5.refs_6_.refs_4_
  54.1 0.0 collective-permute-done.4.refs_5_.refs_3_
  54.1 0.6 collective-permute-done.3.refs_4_.refs_2_
  54.7 0.0 copy-done.3
  54.7 0.0 copy-done.5
  54.7 0.0 copy-start.6
  54.7 10.7 %shard_map.106 = (bf16[512,512]{1,0:T(8,128)(2,1)S(1)}, bf16[512,512]{1,0:T(8,128)(2,1)S(1)}, bf16[512,512]{1,0:T(8,128)(2,1)S(1)}, s32[64,128]{1,0:T(8,128)S(1)}) custom-call(bf16[528,768]{1,0:T(8,128)(2,1)S(1)} %copy-done.3, bf16[512,512]{1,0:T(8,128)(2,1)} %collective-permute-done.6.after.refs_1_, bf16[528,768]{1,0:T(8,128)(2,1)S(1)} %copy-done.5, ...), custom_call_target="tpu_custom_call" | custom-call | flops 12000000000 | bytes 1048576 | tf_op jit(solution)/shard_map/pallas_call | solution.py:462
  65.5 2.4 %collective-permute-start.11 = (bf16[512,512]{1,0:T(8,128)(2,1)S(1)}, bf16[512,512]{1,0:T(8,128)(2,1)S(1)}, u32[]{:S(2)}, u32[]{:S(2)}) collective-permute-start(bf16[512,512]{1,0:T(8,128)(2,1)S(1)} %get-tuple-element.24), channel_id=1, source_target_pairs={{0,96},{1,25},{2,98},{3,27},{4,100},{5,29},{6,102},{7,31},{8,104},... | collective-permute-start | bytes 1572872 | tf_op jit(solution)/shard_map/ppermute | solution.py:58
  67.9 1.2 %collective-permute-start.12 = (bf16[512,512]{1,0:T(8,128)(2,1)S(1)}, bf16[512,512]{1,0:T(8,128)(2,1)S(1)}, u32[]{:S(2)}, u32[]{:S(2)}) collective-permute-start(bf16[512,512]{1,0:T(8,128)(2,1)S(1)} %get-tuple-element.25), channel_id=1, source_target_pairs={{0,64},{1,17},{2,66},{3,19},{4,68},{5,21},{6,70},{7,23},{8,72},{9,... | collective-permute-start | bytes 1572872 | tf_op jit(solution)/shard_map/ppermute | solution.py:58
  69.1 0.0 collective-permute-start.13
  69.1 0.0 copy-done.6
  69.1 4.4 %shard_map.107.refs_0_ = bf16[512,512]{1,0:T(8,128)(2,1)S(1)} custom-call(bf16[512,512]{1,0:T(8,128)(2,1)S(1)} %copy-done.6, bf16[2112,256]{1,0:T(8,128)(2,1)S(1)} %pad_maximum_fusion.refs_3_.refs_1_, bf16[2112,256]{1,0:T(8,128)(2,1)} %collective-permute-done.3.refs_4_.refs_2_, bf16[2112,256]{1,0:T(8,128)(2,1)} %collective-permute-done.4.refs_5_.refs_3_, ...), custom_call_target="tpu_custom_call" | custom-call | flops 4000000000 | bytes 1048576 | tf_op jit(solution)/shard_map/pallas_call | solution.py:462
  73.5 6.7 %collective-permute-done.11.refs_1_ = bf16[512,512]{1,0:T(8,128)(2,1)S(1)} collective-permute-done((bf16[512,512]{1,0:T(8,128)(2,1)S(1)}, bf16[512,512]{1,0:T(8,128)(2,1)S(1)}, u32[]{:S(2)}, u32[]{:S(2)}) %collective-permute-start.11) | collective-permute-done | bytes 524320 | tf_op jit(solution)/shard_map/ppermute | solution.py:58
  80.3 0.0 collective-permute-done.12.refs_2_
  80.3 3.9 %collective-permute-done.13.refs_3_ = bf16[512,512]{1,0:T(8,128)(2,1)S(1)} collective-permute-done((bf16[512,512]{1,0:T(8,128)(2,1)S(1)}, bf16[512,512]{1,0:T(8,128)(2,1)S(1)}, u32[]{:S(2)}, u32[]{:S(2)}) %collective-permute-start.13) | collective-permute-done | bytes 524320 | tf_op jit(solution)/shard_map/ppermute | solution.py:58
  84.2 1.3 %shard_map.108 = bf16[512,2048]{1,0:T(8,128)(2,1)} custom-call(bf16[512,512]{1,0:T(8,128)(2,1)S(1)} %shard_map.107.refs_0_, bf16[512,512]{1,0:T(8,128)(2,1)S(1)} %collective-permute-done.11.refs_1_, bf16[512,512]{1,0:T(8,128)(2,1)S(1)} %collective-permute-done.12.refs_2_, bf16[512,512]{1,0:T(8,128)(2,1)S(1)} %collective-permute-done.13.refs_3_), custom_call_target="tpu_custom_call" | custom-call | flops 2000000000 | bytes 1048576 | tf_op jit(solution)/shard_map/pallas_call | solution.py:213
  (3 shorter events, 0.0 us)
Async XLA Ops:
  4.6 26.0 %copy-start = (bf16[272,1024]{1,0:T(8,128)(2,1)S(1)}, bf16[272,1024]{1,0:T(8,128)(2,1)}, u32[]{:S(2)}) copy-start(bf16[272,1024]{1,0:T(8,128)(2,1)} %get-tuple-element.21.refs_0_) | copy-start | bytes 1671172
  4.6 14.8 %collective-permute-start = (bf16[528,768]{1,0:T(8,128)(2,1)}, bf16[528,768]{1,0:T(8,128)(2,1)S(1)}, u32[]{:S(2)}, u32[]{:S(2)}) collective-permute-start(bf16[528,768]{1,0:T(8,128)(2,1)} %get-tuple-element.17), channel_id=1, source_target_pairs={{0,32},{1,9},{2,34},{3,11},{4,36},{5,13},{6,38},{7,15},{8,40},{9,1... | collective-permute-start | bytes 2433032 | tf_op jit(solution)/shard_map/ppermute | solution.py:58
  6.2 14.9 %collective-permute-start.2 = (bf16[528,768]{1,0:T(8,128)(2,1)}, bf16[528,768]{1,0:T(8,128)(2,1)S(1)}, u32[]{:S(2)}, u32[]{:S(2)}) collective-permute-start(bf16[528,768]{1,0:T(8,128)(2,1)} %get-tuple-element.19), channel_id=1, source_target_pairs={{0,96},{1,25},{2,98},{3,27},{4,100},{5,29},{6,102},{7,31},{8,104},... | collective-permute-start | bytes 2433032 | tf_op jit(solution)/shard_map/ppermute | solution.py:58
  7.9 14.4 %collective-permute-start.1 = (bf16[528,256]{1,0:T(8,128)(2,1)}, bf16[528,256]{1,0:T(8,128)(2,1)S(1)}, u32[]{:S(2)}, u32[]{:S(2)}) collective-permute-start(bf16[528,256]{1,0:T(8,128)(2,1)} %get-tuple-element.18), channel_id=1, source_target_pairs={{0,64},{1,17},{2,66},{3,19},{4,68},{5,21},{6,70},{7,23},{8,72},{9,... | collective-permute-start | bytes 811016 | tf_op jit(solution)/shard_map/ppermute | solution.py:58
  9.8 19.2 %collective-permute-start.8 = (bf16[272,1024]{1,0:T(8,128)(2,1)}, bf16[272,1024]{1,0:T(8,128)(2,1)S(1)}, u32[]{:S(2)}, u32[]{:S(2)}) collective-permute-start(bf16[272,1024]{1,0:T(8,128)(2,1)} %get-tuple-element.21.refs_0_), channel_id=1, source_target_pairs={{0,4},{1,5},{2,6},{3,7},{8,12},{9,13},{10,14},{11,15},{16,20},{17,... | collective-permute-start | bytes 1671176 | tf_op jit(solution)/shard_map/ppermute | solution.py:58
  15.6 23.5 %collective-permute-start.7 = (bf16[272,1024]{1,0:T(8,128)(2,1)}, bf16[272,1024]{1,0:T(8,128)(2,1)}, u32[]{:S(2)}, u32[]{:S(2)}) collective-permute-start(bf16[272,1024]{1,0:T(8,128)(2,1)} %get-tuple-element.21.refs_0_), channel_id=1, source_target_pairs={{0,2},{1,3},{2,4},{3,5},{4,6},{5,7},{8,10},{9,11},{10,12},{11,13},... | collective-permute-start | bytes 1671176 | tf_op jit(solution)/shard_map/ppermute | solution.py:58
  19.3 3.0 %copy-start.2 = (bf16[528,768]{1,0:T(8,128)(2,1)}, bf16[528,768]{1,0:T(8,128)(2,1)S(1)}, u32[]{:S(2)}) copy-start(bf16[528,768]{1,0:T(8,128)(2,1)S(1)} %collective-permute-done.refs_0_) | copy-start | bytes 2433028
  19.3 11.3 %collective-permute-start.6 = (bf16[512,512]{1,0:T(8,128)(2,1)}, bf16[512,512]{1,0:T(8,128)(2,1)}, u32[]{:S(2)}, u32[]{:S(2)}) collective-permute-start(bf16[512,512]{1,0:T(8,128)(2,1)} %get-tuple-element.20), channel_id=1, source_target_pairs={{0,64},{1,17},{2,66},{3,19},{4,68},{5,21},{6,70},{7,23},{8,72},{9,... | collective-permute-start | bytes 1572872 | tf_op jit(solution)/shard_map/ppermute | solution.py:58
  21.1 20.1 %copy-start.1 = (bf16[1,256,2048]{2,1,0:T(8,128)(2,1)S(1)}, bf16[1,256,2048]{2,1,0:T(8,128)(2,1)}, u32[]{:S(2)}) copy-start(bf16[1,256,2048]{2,1,0:T(8,128)(2,1)} %param.14) | copy-start | bytes 3145732
  21.1 0.9 %copy-start.4 = (bf16[528,768]{1,0:T(8,128)(2,1)}, bf16[528,768]{1,0:T(8,128)(2,1)S(1)}, u32[]{:S(2)}) copy-start(bf16[528,768]{1,0:T(8,128)(2,1)S(1)} %collective-permute-done.2.refs_2_) | copy-start | bytes 2433028
  23.3 30.8 %collective-permute-start.5 = (bf16[2112,256]{1,0:T(8,128)(2,1)S(1)}, bf16[2112,256]{1,0:T(8,128)(2,1)}, u32[]{:S(2)}, u32[]{:S(2)}) collective-permute-start(bf16[2112,256]{1,0:T(8,128)(2,1)S(1)} %pad_maximum_fusion.refs_3_.refs_1_), channel_id=1, source_target_pairs={{0,24},{1,97},{2,26},{3,99},{4,28},{5,101},{6,30},{7,103},{8,0},{9... | collective-permute-start | bytes 3244040 | tf_op jit(solution)/shard_map/ppermute | solution.py:58
  26.4 27.7 %collective-permute-start.4 = (bf16[2112,256]{1,0:T(8,128)(2,1)S(1)}, bf16[2112,256]{1,0:T(8,128)(2,1)}, u32[]{:S(2)}, u32[]{:S(2)}) collective-permute-start(bf16[2112,256]{1,0:T(8,128)(2,1)S(1)} %pad_maximum_fusion.refs_3_.refs_1_), channel_id=1, source_target_pairs={{0,16},{1,65},{2,18},{3,67},{4,20},{5,69},{6,22},{7,71},{8,24},{9,... | collective-permute-start | bytes 3244040 | tf_op jit(solution)/shard_map/ppermute | solution.py:58
  29.0 25.8 %collective-permute-start.3 = (bf16[2112,256]{1,0:T(8,128)(2,1)S(1)}, bf16[2112,256]{1,0:T(8,128)(2,1)}, u32[]{:S(2)}, u32[]{:S(2)}) collective-permute-start(bf16[2112,256]{1,0:T(8,128)(2,1)S(1)} %pad_maximum_fusion.refs_3_.refs_1_), channel_id=1, source_target_pairs={{0,8},{1,33},{2,10},{3,35},{4,12},{5,37},{6,14},{7,39},{8,16},{9,4... | collective-permute-start | bytes 3244040 | tf_op jit(solution)/shard_map/ppermute | solution.py:58
  30.6 8.4 %collective-permute-start.10 = (bf16[272,1024]{1,0:T(8,128)(2,1)S(1)}, bf16[272,1024]{1,0:T(8,128)(2,1)S(1)}, u32[]{:S(2)}, u32[]{:S(2)}) collective-permute-start(bf16[272,1024]{1,0:T(8,128)(2,1)S(1)} %broadcast_select_fusion), channel_id=1, source_target_pairs={{0,1},{1,0},{2,3},{3,2},{4,5},{5,4},{6,7},{7,6},{8,9},{9,8},{10,11... | collective-permute-start | bytes 1671176 | tf_op jit(solution)/shard_map/ppermute | solution.py:58
  39.0 2.2 %collective-permute-start.9 = (bf16[272,1024]{1,0:T(8,128)(2,1)}, bf16[272,1024]{1,0:T(8,128)(2,1)S(1)}, u32[]{:S(2)}, u32[]{:S(2)}) collective-permute-start(bf16[272,1024]{1,0:T(8,128)(2,1)} %collective-permute-done.7.refs_1_), channel_id=1, source_target_pairs={{0,1},{1,0},{2,3},{3,2},{4,5},{5,4},{6,7},{7,6},{8,9},{9,8},{10,11... | collective-permute-start | bytes 1671176 | tf_op jit(solution)/shard_map/ppermute | solution.py:58
  41.2 13.5 %copy-start.3 = (bf16[528,768]{1,0:T(8,128)(2,1)S(1)}, bf16[528,768]{1,0:T(8,128)(2,1)}, u32[]{:S(2)}) copy-start(bf16[528,768]{1,0:T(8,128)(2,1)} %copy-done.2) | copy-start | bytes 2433028
  41.2 13.5 %copy-start.5 = (bf16[528,768]{1,0:T(8,128)(2,1)S(1)}, bf16[528,768]{1,0:T(8,128)(2,1)}, u32[]{:S(2)}) copy-start(bf16[528,768]{1,0:T(8,128)(2,1)} %copy-done.4) | copy-start | bytes 2433028
  54.7 14.3 %copy-start.6 = (bf16[512,512]{1,0:T(8,128)(2,1)S(1)}, bf16[512,512]{1,0:T(8,128)(2,1)}, u32[]{:S(2)}) copy-start(bf16[512,512]{1,0:T(8,128)(2,1)} %get-tuple-element.15.refs_0_) | copy-start | bytes 1572868
  65.5 14.8 %collective-permute-start.11 = (bf16[512,512]{1,0:T(8,128)(2,1)S(1)}, bf16[512,512]{1,0:T(8,128)(2,1)S(1)}, u32[]{:S(2)}, u32[]{:S(2)}) collective-permute-start(bf16[512,512]{1,0:T(8,128)(2,1)S(1)} %get-tuple-element.24), channel_id=1, source_target_pairs={{0,96},{1,25},{2,98},{3,27},{4,100},{5,29},{6,102},{7,31},{8,104},... | collective-permute-start | bytes 1572872 | tf_op jit(solution)/shard_map/ppermute | solution.py:58
  67.9 12.4 %collective-permute-start.12 = (bf16[512,512]{1,0:T(8,128)(2,1)S(1)}, bf16[512,512]{1,0:T(8,128)(2,1)S(1)}, u32[]{:S(2)}, u32[]{:S(2)}) collective-permute-start(bf16[512,512]{1,0:T(8,128)(2,1)S(1)} %get-tuple-element.25), channel_id=1, source_target_pairs={{0,64},{1,17},{2,66},{3,19},{4,68},{5,21},{6,70},{7,23},{8,72},{9,... | collective-permute-start | bytes 1572872 | tf_op jit(solution)/shard_map/ppermute | solution.py:58
  69.1 15.2 %collective-permute-start.13 = (bf16[512,512]{1,0:T(8,128)(2,1)S(1)}, bf16[512,512]{1,0:T(8,128)(2,1)S(1)}, u32[]{:S(2)}, u32[]{:S(2)}) collective-permute-start(bf16[512,512]{1,0:T(8,128)(2,1)S(1)} %get-tuple-element.26), channel_id=1, source_target_pairs={{0,32},{1,9},{2,34},{3,11},{4,36},{5,13},{6,38},{7,15},{8,40},{9,1... | collective-permute-start | bytes 1572872 | tf_op jit(solution)/shard_map/ppermute | solution.py:58

commit v6 on v5

--- a/solution.py
+++ b/solution.py
@@ -268,16 +268,6 @@
     table_ref[4 * SB + GROUPS :] = fill_list
 
 
-def soften(scores, value_rows):
-    row_max = jnp.max(scores, axis=-1, keepdims=True)
-    weights = jnp.exp2((scores - row_max) * SCALE)
-    totals = jnp.sum(weights, axis=-1, keepdims=True)
-    mixture = jnp.dot(
-        weights.astype(jnp.bfloat16), value_rows, preferred_element_type=jnp.float32
-    )
-    return mixture / totals
-
-
 def inner(queries, key_rows):
     return lax.dot_general(
         queries, key_rows, (((1,), (1,)), ((), ())), preferred_element_type=jnp.float32
@@ -474,7 +464,7 @@
 
 
 def long_kernel(q_in, after, *refs):
-    parts = refs[:5]
+    parts = list(refs[:5])
     out_ref, token, q_ref, bias_ref, sem = refs[5:]
     copy = pltpu.make_async_copy(q_in, q_ref, sem)
     copy.start()
@@ -488,18 +478,29 @@
         allowed = own_doc == docs[n]
         if n == 0:
             allowed = allowed & (lane <= row)
-        bias_ref[:, n * LROWS : (n + 1) * LROWS] = jnp.where(allowed, 0.0, MASKED)
+        at = (n + 4) % 5 * LROWS
+        bias_ref[:, at : at + LROWS] = jnp.where(allowed, 0.0, MASKED)
     copy.wait()
 
     def one_head(h, _):
         col = pl.multiple_of(h * HD, HD)
         vcol = pl.multiple_of((KVH + h) * HD, HD)
-        keys = jnp.concatenate([p[:LROWS, pl.ds(col, HD)] for p in parts], axis=0)
-        values = jnp.concatenate([p[:LROWS, pl.ds(vcol, HD)] for p in parts], axis=0)
+        order = parts[1:] + parts[:1]
+        keys = jnp.concatenate([p[:LROWS, pl.ds(col, HD)] for p in order], axis=0)
+        values = jnp.concatenate([p[:LROWS, pl.ds(vcol, HD)] for p in order], axis=0)
+        values = jnp.concatenate([values, jnp.ones((5 * LROWS, HD), jnp.bfloat16)], axis=1)
         for i in range(GROUP):
             qcol = pl.multiple_of((h * GROUP + i) * HD, HD)
-            scores = inner(q_ref[:, pl.ds(qcol, HD)], keys) + bias_ref[...]
-            out_ref[:, pl.ds(qcol, HD)] = soften(scores, values).astype(jnp.bfloat16)
+            for half in range(2):
+                rows = slice(half * HD, (half + 1) * HD)
+                seen = (8 + half + 1) * HD
+                scores = inner(q_ref[rows, pl.ds(qcol, HD)], keys[:seen])
+                scores = scores + bias_ref[rows, :seen]
+                top = jnp.max(scores, axis=-1, keepdims=True)
+                weights = jnp.exp2((scores - top) * SCALE).astype(jnp.bfloat16)
+                mixed = jnp.dot(weights, values[:seen], preferred_element_type=jnp.float32)
+                mixed = mixed[:, :HD] / mixed[:, HD:]
+                out_ref[rows, pl.ds(qcol, HD)] = mixed.astype(jnp.bfloat16)
         return 0
 
     lax.fori_loop(0, KVH, one_head, 0)

time: 86 us -> 85.9 us (level)
  Pallas kernels: 33.3 us -> 31 us
  waiting for transfers between devices: 24.1 us -> 26 us
    ppermute x14, waiting for transfers between devices: 24.1 us -> 26 us  [send(): return lax.ppermute(value, ('dp', 'ctx'), pairs(step))]
    pallas_call x1, Pallas kernels: 12.8 us -> 10.9 us  [long_attention(): pl.pallas_call(long_kernel, out_shape=[jax.ShapeDtypeStruct((LROWS, QH *...]
  transfers between devices with their start and end apart: 14 -> 14, of which waited for: 7 -> 7; matrix products, arithmetic and copies ran while one was open for 1% -> 1% of each run, Pallas kernels for 20% -> 18%
where the time goes in v6:
time: 85.9 us; the launch traced here: 85.3 us
  Pallas kernels  31 us (36%)
  waiting for transfers between devices  26 us (30%)
  starting transfers between devices  25.4 us (30%)
  other arithmetic  1.08 us (1%)
  local copies, waits for them, and re-layouts  0.95 us (1%)
  between operations  0.93 us (1%)
    ppermute x14, waiting for transfers between devices, send(): return lax.ppermute(value, ('dp', 'ctx'), pairs(step))  26 us
    ppermute x14, starting transfers between devices, send(): return lax.ppermute(value, ('dp', 'ctx'), pairs(step))  25.4 us
    pallas_call x2, Pallas kernels, short_attention(): pl.pallas_call(functools.partial(short_kernel, shifts, first, len(after))...  14.8 us
    pallas_call x1, Pallas kernels, long_attention(): pl.pallas_call(long_kernel, out_shape=[jax.ShapeDtypeStruct((LROWS, QH *...  10.9 us
    pallas_call x1, Pallas kernels, split(): pl.pallas_call(split_kernel, out_shape=[jax.ShapeDtypeStruct(shape, jnp.b...  3.91 us
  transfers between devices with their start and end apart: 14, of which 7 were waited for; matrix products, arithmetic and copies ran while one was open for 1% of the time, Pallas kernels for 18%

profile of v6, /device:TPU:0, one launch (start us, length us, event | category | flops | bytes accessed | tf_op | source)
XLA Modules:
  0.0 85.3 jit_solution(5690930878790321460)
XLA Ops:
  0.6 3.9 %shard_map.104 = (bf16[528,256]{1,0:T(8,128)(2,1)}, bf16[528,768]{1,0:T(8,128)(2,1)}, bf16[528,256]{1,0:T(8,128)(2,1)}, bf16[528,768]{1,0:T(8,128)(2,1)}, bf16[5...) custom-call(s32[8]{0:T(128)} %bitcast.17, s32[8]{0:T(128)} %bitcast.18, s32[1,256]{1,0:T(1,128)} %doc_in.1, ...), custom_call_target="tpu_custom_call" | custom-call | flops 2000000000 | bytes 1048576 | tf_op jit(solution)/shard_map/pallas_call | solution.py:176
  4.6 0.0 copy-start
  4.6 1.6 %collective-permute-start = (bf16[528,768]{1,0:T(8,128)(2,1)}, bf16[528,768]{1,0:T(8,128)(2,1)S(1)}, u32[]{:S(2)}, u32[]{:S(2)}) collective-permute-start(bf16[528,768]{1,0:T(8,128)(2,1)} %get-tuple-element.17), channel_id=1, source_target_pairs={{0,32},{1,9},{2,34},{3,11},{4,36},{5,13},{6,38},{7,15},{8,40},{9,1... | collective-permute-start | bytes 2433032 | tf_op jit(solution)/shard_map/ppermute | solution.py:58
  6.2 1.7 %collective-permute-start.2 = (bf16[528,768]{1,0:T(8,128)(2,1)}, bf16[528,768]{1,0:T(8,128)(2,1)S(1)}, u32[]{:S(2)}, u32[]{:S(2)}) collective-permute-start(bf16[528,768]{1,0:T(8,128)(2,1)} %get-tuple-element.19), channel_id=1, source_target_pairs={{0,96},{1,25},{2,98},{3,27},{4,100},{5,29},{6,102},{7,31},{8,104},... | collective-permute-start | bytes 2433032 | tf_op jit(solution)/shard_map/ppermute | solution.py:58
  7.9 1.9 %collective-permute-start.1 = (bf16[528,256]{1,0:T(8,128)(2,1)}, bf16[528,256]{1,0:T(8,128)(2,1)S(1)}, u32[]{:S(2)}, u32[]{:S(2)}) collective-permute-start(bf16[528,256]{1,0:T(8,128)(2,1)} %get-tuple-element.18), channel_id=1, source_target_pairs={{0,64},{1,17},{2,66},{3,19},{4,68},{5,21},{6,70},{7,23},{8,72},{9,... | collective-permute-start | bytes 811016 | tf_op jit(solution)/shard_map/ppermute | solution.py:58
  9.8 5.8 %collective-permute-start.8 = (bf16[272,1024]{1,0:T(8,128)(2,1)}, bf16[272,1024]{1,0:T(8,128)(2,1)S(1)}, u32[]{:S(2)}, u32[]{:S(2)}) collective-permute-start(bf16[272,1024]{1,0:T(8,128)(2,1)} %get-tuple-element.21.refs_0_), channel_id=1, source_target_pairs={{0,4},{1,5},{2,6},{3,7},{8,12},{9,13},{10,14},{11,15},{16,20},{17,... | collective-permute-start | bytes 1671176 | tf_op jit(solution)/shard_map/ppermute | solution.py:58
  15.6 3.7 %collective-permute-start.7 = (bf16[272,1024]{1,0:T(8,128)(2,1)}, bf16[272,1024]{1,0:T(8,128)(2,1)}, u32[]{:S(2)}, u32[]{:S(2)}) collective-permute-start(bf16[272,1024]{1,0:T(8,128)(2,1)} %get-tuple-element.21.refs_0_), channel_id=1, source_target_pairs={{0,2},{1,3},{2,4},{3,5},{4,6},{5,7},{8,10},{9,11},{10,12},{11,13},... | collective-permute-start | bytes 1671176 | tf_op jit(solution)/shard_map/ppermute | solution.py:58
  19.3 0.0 collective-permute-done.refs_0_
  19.3 0.0 copy-start.2
  19.3 1.7 %collective-permute-start.6 = (bf16[512,512]{1,0:T(8,128)(2,1)}, bf16[512,512]{1,0:T(8,128)(2,1)}, u32[]{:S(2)}, u32[]{:S(2)}) collective-permute-start(bf16[512,512]{1,0:T(8,128)(2,1)} %get-tuple-element.20), channel_id=1, source_target_pairs={{0,64},{1,17},{2,66},{3,19},{4,68},{5,21},{6,70},{7,23},{8,72},{9,... | collective-permute-start | bytes 1572872 | tf_op jit(solution)/shard_map/ppermute | solution.py:58
  21.1 0.0 copy-start.1
  21.1 0.0 collective-permute-done.2.refs_2_
  21.1 0.0 copy-start.4
  21.1 0.9 %copy-done.4 = bf16[528,768]{1,0:T(8,128)(2,1)} copy-done((bf16[528,768]{1,0:T(8,128)(2,1)}, bf16[528,768]{1,0:T(8,128)(2,1)S(1)}, u32[]{:S(2)}) %copy-start.4) | copy-done | bytes 811032
  22.0 0.3 collective-permute-done.1
  22.3 0.0 copy-done.2
  22.3 1.0 %pad_maximum_fusion.refs_3_.refs_1_ = bf16[2112,256]{1,0:T(8,128)(2,1)S(1)} fusion(bf16[528,256]{1,0:T(8,128)(2,1)S(1)} %slice.9, bf16[528,256]{1,0:T(8,128)(2,1)S(1)} %collective-permute-done.1, bf16[528,256]{1,0:T(8,128)(2,1)S(1)} %slice.8, bf16[528,256]{1,0:T(8,128)(2,1)} %get-tuple-element.16), kind=kLoop, calls=%fused_computation | loop fusion | flops 4325376 | bytes 2162688 | tf_op jit(solution)/shard_map/concatenate | solution.py:554
  23.3 3.1 %collective-permute-start.5 = (bf16[2112,256]{1,0:T(8,128)(2,1)S(1)}, bf16[2112,256]{1,0:T(8,128)(2,1)}, u32[]{:S(2)}, u32[]{:S(2)}) collective-permute-start(bf16[2112,256]{1,0:T(8,128)(2,1)S(1)} %pad_maximum_fusion.refs_3_.refs_1_), channel_id=1, source_target_pairs={{0,24},{1,97},{2,26},{3,99},{4,28},{5,101},{6,30},{7,103},{8,0},{9... | collective-permute-start | bytes 3244040 | tf_op jit(solution)/shard_map/ppermute | solution.py:58
  26.4 0.6 collective-permute-start.4
  27.0 2.0 %collective-permute-done.8.refs_2_ = bf16[272,1024]{1,0:T(8,128)(2,1)S(1)} collective-permute-done((bf16[272,1024]{1,0:T(8,128)(2,1)}, bf16[272,1024]{1,0:T(8,128)(2,1)S(1)}, u32[]{:S(2)}, u32[]{:S(2)}) %collective-permute-start.8) | collective-permute-done | bytes 557088 | tf_op jit(solution)/shard_map/ppermute | solution.py:58
  29.0 1.6 %collective-permute-start.3 = (bf16[2112,256]{1,0:T(8,128)(2,1)S(1)}, bf16[2112,256]{1,0:T(8,128)(2,1)}, u32[]{:S(2)}, u32[]{:S(2)}) collective-permute-start(bf16[2112,256]{1,0:T(8,128)(2,1)S(1)} %pad_maximum_fusion.refs_3_.refs_1_), channel_id=1, source_target_pairs={{0,8},{1,33},{2,10},{3,35},{4,12},{5,37},{6,14},{7,39},{8,16},{9,4... | collective-permute-start | bytes 3244040 | tf_op jit(solution)/shard_map/ppermute | solution.py:58
  30.5 0.0 copy-done
  30.5 0.1 broadcast_select_fusion
  30.6 0.0 collective-permute-done.6.after.refs_1_
  30.6 0.1 collective-permute-start.10
  30.7 8.3 %collective-permute-done.7.refs_1_ = bf16[272,1024]{1,0:T(8,128)(2,1)} collective-permute-done((bf16[272,1024]{1,0:T(8,128)(2,1)}, bf16[272,1024]{1,0:T(8,128)(2,1)}, u32[]{:S(2)}, u32[]{:S(2)}) %collective-permute-start.7) | collective-permute-done | bytes 557088 | tf_op jit(solution)/shard_map/ppermute | solution.py:58
  39.0 0.0 collective-permute-start.9
  39.0 0.0 collective-permute-done.10.refs_4_
  39.0 2.2 %collective-permute-done.9.refs_3_ = bf16[272,1024]{1,0:T(8,128)(2,1)S(1)} collective-permute-done((bf16[272,1024]{1,0:T(8,128)(2,1)}, bf16[272,1024]{1,0:T(8,128)(2,1)S(1)}, u32[]{:S(2)}, u32[]{:S(2)}) %collective-permute-start.9) | collective-permute-done | bytes 557088 | tf_op jit(solution)/shard_map/ppermute | solution.py:58
  41.2 0.0 copy-done.1
  41.2 0.0 copy-start.3
  41.2 0.0 copy-start.5
  41.2 10.9 %shard_map.105 = (bf16[256,2048]{1,0:T(8,128)(2,1)}, s32[1]{0:T(128)}) custom-call(bf16[256,2048]{1,0:T(8,128)(2,1)S(1)} %bitcast.10, bf16[512,512]{1,0:T(8,128)(2,1)} %collective-permute-done.6.after.refs_1_, bf16[272,1024]{1,0:T(8,128)(2,1)S(1)} %copy-done, bf16[272,1024]{1,0:T(8,128)(2,1)} %collective-permute-done.7.refs_1_, ...), custom_call_target="tpu_custom_call" | custom-call | flops 100000000 | bytes 1048576 | tf_op jit(solution)/shard_map/pallas_call | solution.py:510
  52.2 0.0 collective-permute-done.5.refs_6_.refs_4_
  52.2 0.0 collective-permute-done.4.refs_5_.refs_3_
  52.2 2.5 %collective-permute-done.3.refs_4_.refs_2_ = bf16[2112,256]{1,0:T(8,128)(2,1)} collective-permute-done((bf16[2112,256]{1,0:T(8,128)(2,1)S(1)}, bf16[2112,256]{1,0:T(8,128)(2,1)}, u32[]{:S(2)}, u32[]{:S(2)}) %collective-permute-start.3) | collective-permute-done | bytes 1081376 | tf_op jit(solution)/shard_map/ppermute | solution.py:58
  54.7 0.0 copy-done.3
  54.7 0.0 copy-done.5
  54.7 10.3 %shard_map.106 = (bf16[512,512]{1,0:T(8,128)(2,1)S(1)}, bf16[512,512]{1,0:T(8,128)(2,1)S(1)}, bf16[512,512]{1,0:T(8,128)(2,1)S(1)}, s32[64,128]{1,0:T(8,128)S(1)}) custom-call(bf16[528,768]{1,0:T(8,128)(2,1)S(1)} %copy-done.3, bf16[512,512]{1,0:T(8,128)(2,1)} %collective-permute-done.6.after.refs_1_, bf16[528,768]{1,0:T(8,128)(2,1)S(1)} %copy-done.5, ...), custom_call_target="tpu_custom_call" | custom-call | flops 12000000000 | bytes 1048576 | tf_op jit(solution)/shard_map/pallas_call | solution.py:452
  65.1 2.4 %collective-permute-start.11 = (bf16[512,512]{1,0:T(8,128)(2,1)S(1)}, bf16[512,512]{1,0:T(8,128)(2,1)S(1)}, u32[]{:S(2)}, u32[]{:S(2)}) collective-permute-start(bf16[512,512]{1,0:T(8,128)(2,1)S(1)} %get-tuple-element.24), channel_id=1, source_target_pairs={{0,96},{1,25},{2,98},{3,27},{4,100},{5,29},{6,102},{7,31},{8,104},... | collective-permute-start | bytes 1572872 | tf_op jit(solution)/shard_map/ppermute | solution.py:58
  67.5 1.1 %collective-permute-start.12 = (bf16[512,512]{1,0:T(8,128)(2,1)S(1)}, bf16[512,512]{1,0:T(8,128)(2,1)S(1)}, u32[]{:S(2)}, u32[]{:S(2)}) collective-permute-start(bf16[512,512]{1,0:T(8,128)(2,1)S(1)} %get-tuple-element.25), channel_id=1, source_target_pairs={{0,64},{1,17},{2,66},{3,19},{4,68},{5,21},{6,70},{7,23},{8,72},{9,... | collective-permute-start | bytes 1572872 | tf_op jit(solution)/shard_map/ppermute | solution.py:58
  68.6 0.0 collective-permute-start.13
  68.6 0.0 copy-done.6
  68.7 4.4 %shard_map.107.refs_0_ = bf16[512,512]{1,0:T(8,128)(2,1)S(1)} custom-call(bf16[512,512]{1,0:T(8,128)(2,1)S(1)} %copy-done.6, bf16[2112,256]{1,0:T(8,128)(2,1)S(1)} %pad_maximum_fusion.refs_3_.refs_1_, bf16[2112,256]{1,0:T(8,128)(2,1)} %collective-permute-done.3.refs_4_.refs_2_, bf16[2112,256]{1,0:T(8,128)(2,1)} %collective-permute-done.4.refs_5_.refs_3_, ...), custom_call_target="tpu_custom_call" | custom-call | flops 4000000000 | bytes 1048576 | tf_op jit(solution)/shard_map/pallas_call | solution.py:452
  73.1 6.8 %collective-permute-done.11.refs_1_ = bf16[512,512]{1,0:T(8,128)(2,1)S(1)} collective-permute-done((bf16[512,512]{1,0:T(8,128)(2,1)S(1)}, bf16[512,512]{1,0:T(8,128)(2,1)S(1)}, u32[]{:S(2)}, u32[]{:S(2)}) %collective-permute-start.11) | collective-permute-done | bytes 524320 | tf_op jit(solution)/shard_map/ppermute | solution.py:58
  79.9 0.0 collective-permute-done.12.refs_2_
  79.9 3.9 %collective-permute-done.13.refs_3_ = bf16[512,512]{1,0:T(8,128)(2,1)S(1)} collective-permute-done((bf16[512,512]{1,0:T(8,128)(2,1)S(1)}, bf16[512,512]{1,0:T(8,128)(2,1)S(1)}, u32[]{:S(2)}, u32[]{:S(2)}) %collective-permute-start.13) | collective-permute-done | bytes 524320 | tf_op jit(solution)/shard_map/ppermute | solution.py:58
  83.8 1.3 %shard_map.108 = bf16[512,2048]{1,0:T(8,128)(2,1)} custom-call(bf16[512,512]{1,0:T(8,128)(2,1)S(1)} %shard_map.107.refs_0_, bf16[512,512]{1,0:T(8,128)(2,1)S(1)} %collective-permute-done.11.refs_1_, bf16[512,512]{1,0:T(8,128)(2,1)S(1)} %collective-permute-done.12.refs_2_, bf16[512,512]{1,0:T(8,128)(2,1)S(1)} %collective-permute-done.13.refs_3_), custom_call_target="tpu_custom_call" | custom-call | flops 2000000000 | bytes 1048576 | tf_op jit(solution)/shard_map/pallas_call | solution.py:213
  (3 shorter events, 0.0 us)
Async XLA Ops:
  4.6 26.0 %copy-start = (bf16[272,1024]{1,0:T(8,128)(2,1)S(1)}, bf16[272,1024]{1,0:T(8,128)(2,1)}, u32[]{:S(2)}) copy-start(bf16[272,1024]{1,0:T(8,128)(2,1)} %get-tuple-element.21.refs_0_) | copy-start | bytes 1671172
  4.6 14.8 %collective-permute-start = (bf16[528,768]{1,0:T(8,128)(2,1)}, bf16[528,768]{1,0:T(8,128)(2,1)S(1)}, u32[]{:S(2)}, u32[]{:S(2)}) collective-permute-start(bf16[528,768]{1,0:T(8,128)(2,1)} %get-tuple-element.17), channel_id=1, source_target_pairs={{0,32},{1,9},{2,34},{3,11},{4,36},{5,13},{6,38},{7,15},{8,40},{9,1... | collective-permute-start | bytes 2433032 | tf_op jit(solution)/shard_map/ppermute | solution.py:58
  6.2 14.9 %collective-permute-start.2 = (bf16[528,768]{1,0:T(8,128)(2,1)}, bf16[528,768]{1,0:T(8,128)(2,1)S(1)}, u32[]{:S(2)}, u32[]{:S(2)}) collective-permute-start(bf16[528,768]{1,0:T(8,128)(2,1)} %get-tuple-element.19), channel_id=1, source_target_pairs={{0,96},{1,25},{2,98},{3,27},{4,100},{5,29},{6,102},{7,31},{8,104},... | collective-permute-start | bytes 2433032 | tf_op jit(solution)/shard_map/ppermute | solution.py:58
  7.9 14.4 %collective-permute-start.1 = (bf16[528,256]{1,0:T(8,128)(2,1)}, bf16[528,256]{1,0:T(8,128)(2,1)S(1)}, u32[]{:S(2)}, u32[]{:S(2)}) collective-permute-start(bf16[528,256]{1,0:T(8,128)(2,1)} %get-tuple-element.18), channel_id=1, source_target_pairs={{0,64},{1,17},{2,66},{3,19},{4,68},{5,21},{6,70},{7,23},{8,72},{9,... | collective-permute-start | bytes 811016 | tf_op jit(solution)/shard_map/ppermute | solution.py:58
  9.8 19.2 %collective-permute-start.8 = (bf16[272,1024]{1,0:T(8,128)(2,1)}, bf16[272,1024]{1,0:T(8,128)(2,1)S(1)}, u32[]{:S(2)}, u32[]{:S(2)}) collective-permute-start(bf16[272,1024]{1,0:T(8,128)(2,1)} %get-tuple-element.21.refs_0_), channel_id=1, source_target_pairs={{0,4},{1,5},{2,6},{3,7},{8,12},{9,13},{10,14},{11,15},{16,20},{17,... | collective-permute-start | bytes 1671176 | tf_op jit(solution)/shard_map/ppermute | solution.py:58
  15.6 23.5 %collective-permute-start.7 = (bf16[272,1024]{1,0:T(8,128)(2,1)}, bf16[272,1024]{1,0:T(8,128)(2,1)}, u32[]{:S(2)}, u32[]{:S(2)}) collective-permute-start(bf16[272,1024]{1,0:T(8,128)(2,1)} %get-tuple-element.21.refs_0_), channel_id=1, source_target_pairs={{0,2},{1,3},{2,4},{3,5},{4,6},{5,7},{8,10},{9,11},{10,12},{11,13},... | collective-permute-start | bytes 1671176 | tf_op jit(solution)/shard_map/ppermute | solution.py:58
  19.3 3.0 %copy-start.2 = (bf16[528,768]{1,0:T(8,128)(2,1)}, bf16[528,768]{1,0:T(8,128)(2,1)S(1)}, u32[]{:S(2)}) copy-start(bf16[528,768]{1,0:T(8,128)(2,1)S(1)} %collective-permute-done.refs_0_) | copy-start | bytes 2433028
  19.3 11.3 %collective-permute-start.6 = (bf16[512,512]{1,0:T(8,128)(2,1)}, bf16[512,512]{1,0:T(8,128)(2,1)}, u32[]{:S(2)}, u32[]{:S(2)}) collective-permute-start(bf16[512,512]{1,0:T(8,128)(2,1)} %get-tuple-element.20), channel_id=1, source_target_pairs={{0,64},{1,17},{2,66},{3,19},{4,68},{5,21},{6,70},{7,23},{8,72},{9,... | collective-permute-start | bytes 1572872 | tf_op jit(solution)/shard_map/ppermute | solution.py:58
  21.1 20.1 %copy-start.1 = (bf16[1,256,2048]{2,1,0:T(8,128)(2,1)S(1)}, bf16[1,256,2048]{2,1,0:T(8,128)(2,1)}, u32[]{:S(2)}) copy-start(bf16[1,256,2048]{2,1,0:T(8,128)(2,1)} %param.14) | copy-start | bytes 3145732
  21.1 0.9 %copy-start.4 = (bf16[528,768]{1,0:T(8,128)(2,1)}, bf16[528,768]{1,0:T(8,128)(2,1)S(1)}, u32[]{:S(2)}) copy-start(bf16[528,768]{1,0:T(8,128)(2,1)S(1)} %collective-permute-done.2.refs_2_) | copy-start | bytes 2433028
  23.3 28.9 %collective-permute-start.5 = (bf16[2112,256]{1,0:T(8,128)(2,1)S(1)}, bf16[2112,256]{1,0:T(8,128)(2,1)}, u32[]{:S(2)}, u32[]{:S(2)}) collective-permute-start(bf16[2112,256]{1,0:T(8,128)(2,1)S(1)} %pad_maximum_fusion.refs_3_.refs_1_), channel_id=1, source_target_pairs={{0,24},{1,97},{2,26},{3,99},{4,28},{5,101},{6,30},{7,103},{8,0},{9... | collective-permute-start | bytes 3244040 | tf_op jit(solution)/shard_map/ppermute | solution.py:58
  26.4 25.8 %collective-permute-start.4 = (bf16[2112,256]{1,0:T(8,128)(2,1)S(1)}, bf16[2112,256]{1,0:T(8,128)(2,1)}, u32[]{:S(2)}, u32[]{:S(2)}) collective-permute-start(bf16[2112,256]{1,0:T(8,128)(2,1)S(1)} %pad_maximum_fusion.refs_3_.refs_1_), channel_id=1, source_target_pairs={{0,16},{1,65},{2,18},{3,67},{4,20},{5,69},{6,22},{7,71},{8,24},{9,... | collective-permute-start | bytes 3244040 | tf_op jit(solution)/shard_map/ppermute | solution.py:58
  29.0 25.8 %collective-permute-start.3 = (bf16[2112,256]{1,0:T(8,128)(2,1)S(1)}, bf16[2112,256]{1,0:T(8,128)(2,1)}, u32[]{:S(2)}, u32[]{:S(2)}) collective-permute-start(bf16[2112,256]{1,0:T(8,128)(2,1)S(1)} %pad_maximum_fusion.refs_3_.refs_1_), channel_id=1, source_target_pairs={{0,8},{1,33},{2,10},{3,35},{4,12},{5,37},{6,14},{7,39},{8,16},{9,4... | collective-permute-start | bytes 3244040 | tf_op jit(solution)/shard_map/ppermute | solution.py:58
  30.6 8.4 %collective-permute-start.10 = (bf16[272,1024]{1,0:T(8,128)(2,1)S(1)}, bf16[272,1024]{1,0:T(8,128)(2,1)S(1)}, u32[]{:S(2)}, u32[]{:S(2)}) collective-permute-start(bf16[272,1024]{1,0:T(8,128)(2,1)S(1)} %broadcast_select_fusion), channel_id=1, source_target_pairs={{0,1},{1,0},{2,3},{3,2},{4,5},{5,4},{6,7},{7,6},{8,9},{9,8},{10,11... | collective-permute-start | bytes 1671176 | tf_op jit(solution)/shard_map/ppermute | solution.py:58
  39.0 2.2 %collective-permute-start.9 = (bf16[272,1024]{1,0:T(8,128)(2,1)}, bf16[272,1024]{1,0:T(8,128)(2,1)S(1)}, u32[]{:S(2)}, u32[]{:S(2)}) collective-permute-start(bf16[272,1024]{1,0:T(8,128)(2,1)} %collective-permute-done.7.refs_1_), channel_id=1, source_target_pairs={{0,1},{1,0},{2,3},{3,2},{4,5},{5,4},{6,7},{7,6},{8,9},{9,8},{10,11... | collective-permute-start | bytes 1671176 | tf_op jit(solution)/shard_map/ppermute | solution.py:58
  41.2 13.5 %copy-start.3 = (bf16[528,768]{1,0:T(8,128)(2,1)S(1)}, bf16[528,768]{1,0:T(8,128)(2,1)}, u32[]{:S(2)}) copy-start(bf16[528,768]{1,0:T(8,128)(2,1)} %copy-done.2) | copy-start | bytes 2433028
  41.2 13.5 %copy-start.5 = (bf16[528,768]{1,0:T(8,128)(2,1)S(1)}, bf16[528,768]{1,0:T(8,128)(2,1)}, u32[]{:S(2)}) copy-start(bf16[528,768]{1,0:T(8,128)(2,1)} %copy-done.4) | copy-start | bytes 2433028
  54.7 13.9 %copy-start.6 = (bf16[512,512]{1,0:T(8,128)(2,1)S(1)}, bf16[512,512]{1,0:T(8,128)(2,1)}, u32[]{:S(2)}) copy-start(bf16[512,512]{1,0:T(8,128)(2,1)} %get-tuple-element.15.refs_0_) | copy-start | bytes 1572868
  65.1 14.8 %collective-permute-start.11 = (bf16[512,512]{1,0:T(8,128)(2,1)S(1)}, bf16[512,512]{1,0:T(8,128)(2,1)S(1)}, u32[]{:S(2)}, u32[]{:S(2)}) collective-permute-start(bf16[512,512]{1,0:T(8,128)(2,1)S(1)} %get-tuple-element.24), channel_id=1, source_target_pairs={{0,96},{1,25},{2,98},{3,27},{4,100},{5,29},{6,102},{7,31},{8,104},... | collective-permute-start | bytes 1572872 | tf_op jit(solution)/shard_map/ppermute | solution.py:58
  67.5 12.4 %collective-permute-start.12 = (bf16[512,512]{1,0:T(8,128)(2,1)S(1)}, bf16[512,512]{1,0:T(8,128)(2,1)S(1)}, u32[]{:S(2)}, u32[]{:S(2)}) collective-permute-start(bf16[512,512]{1,0:T(8,128)(2,1)S(1)} %get-tuple-element.25), channel_id=1, source_target_pairs={{0,64},{1,17},{2,66},{3,19},{4,68},{5,21},{6,70},{7,23},{8,72},{9,... | collective-permute-start | bytes 1572872 | tf_op jit(solution)/shard_map/ppermute | solution.py:58
  68.6 15.2 %collective-permute-start.13 = (bf16[512,512]{1,0:T(8,128)(2,1)S(1)}, bf16[512,512]{1,0:T(8,128)(2,1)S(1)}, u32[]{:S(2)}, u32[]{:S(2)}) collective-permute-start(bf16[512,512]{1,0:T(8,128)(2,1)S(1)} %get-tuple-element.26), channel_id=1, source_target_pairs={{0,32},{1,9},{2,34},{3,11},{4,36},{5,13},{6,38},{7,15},{8,40},{9,1... | collective-permute-start | bytes 1572872 | tf_op jit(solution)/shard_map/ppermute | solution.py:58

commit v7 on v6

--- a/solution.py
+++ b/solution.py
@@ -331,12 +331,12 @@
     over = [0, 0, 0]
     ranks = []
     for n in range(total):
-        rank = table[2 * SB + n % SB, shifts[0] + n // SB]
+        rank = table[2 * SB + n % SB, shifts[n // SB]]
         ranks.append(rank)
         over = [old + jnp.where(rank >= 4 * (i + 1), 1, 0) for i, old in enumerate(over)]
     spots = [over[0], over[1], over[2], 0]
     for n in range(total):
-        b, k = n % SB, shifts[0] + n // SB
+        b, k = n % SB, shifts[n // SB]
         level = lax.shift_right_logical(ranks[n], 2)
         spot = jnp.where(
             level < 2,
@@ -458,7 +458,7 @@
         out_specs=[VM] * count + ([SM] if first else []),
         scratch_shapes=scratch,
         compiler_params=pltpu.CompilerParams(vmem_limit_bytes=24 * MIB),
-        cost_estimate=busy(4 * count),
+        cost_estimate=busy(30),
     )(*q_parts, *kv_parts, *after, *([] if first else [table]))
     return (found[:count], found[count]) if first else (found, table)
 
@@ -563,10 +563,15 @@
         [packed, long_one, long_two, long_side, long_cross],
     )
 
-    mixed, table = short_attention(
-        (1, 2, 3), None, [token], [line_parts[0], far_q, line_parts[2]], kv_parts
-    )
-    back = [send(piece, along_head(-k)) for k, piece in zip((1, 2, 3), mixed)]
+    q_parts = {1: line_parts[0], 2: far_q, 3: line_parts[2]}
+    back, table = {}, None
+    for shifts in ((1, 2), (3,)):
+        mixed, table = short_attention(
+            shifts, table, [] if table is not None else [token], [q_parts[k] for k in shifts], kv_parts
+        )
+        for k, piece in zip(shifts, mixed):
+            back[k] = send(piece, along_head(-k))
+    back = [back[k] for k in (1, 2, 3)]
     kept, _ = short_attention((0,), table, [], [own_q], kv_parts)
     short_out = join([kept[0]] + back)
     return short_out.reshape(short_queries.shape), long_out.reshape(long_queries.shape)

time: 85.9 us -> 84.8 us (0.987)
  waiting for transfers between devices: 26 us -> 20.2 us
  Pallas kernels: 31 us -> 35.5 us
    ppermute x14, waiting for transfers between devices: 26 us -> 20.2 us  [send(): return lax.ppermute(value, ('dp', 'ctx'), pairs(step))]
    pallas_call x2 -> x3, Pallas kernels: 14.8 us -> 19.3 us  [short_attention(): pl.pallas_call(functools.partial(short_kernel, shifts, first, len(after))...]
  transfers between devices with their start and end apart: 14 -> 14, of which waited for: 7 -> 7; matrix products, arithmetic and copies ran while one was open for 1% -> 1% of each run, Pallas kernels for 18% -> 24%
where the time goes in v7:
time: 84.8 us; the launch traced here: 84.7 us
  Pallas kernels  35.5 us (42%)
  starting transfers between devices  26.1 us (31%)
  waiting for transfers between devices  20.2 us (24%)
  other arithmetic  1.08 us (1%)
  local copies, waits for them, and re-layouts  0.95 us (1%)
  between operations  0.94 us (1%)
    ppermute x14, starting transfers between devices, send(): return lax.ppermute(value, ('dp', 'ctx'), pairs(step))  26.1 us
    ppermute x14, waiting for transfers between devices, send(): return lax.ppermute(value, ('dp', 'ctx'), pairs(step))  20.2 us
    pallas_call x3, Pallas kernels, short_attention(): pl.pallas_call(functools.partial(short_kernel, shifts, first, len(after))...  19.3 us
    pallas_call x1, Pallas kernels, long_attention(): pl.pallas_call(long_kernel, out_shape=[jax.ShapeDtypeStruct((LROWS, QH *...  10.9 us
    pallas_call x1, Pallas kernels, split(): pl.pallas_call(split_kernel, out_shape=[jax.ShapeDtypeStruct(shape, jnp.b...  3.91 us
  transfers between devices with their start and end apart: 14, of which 7 were waited for; matrix products, arithmetic and copies ran while one was open for 1% of the time, Pallas kernels for 24%

profile of v7, /device:TPU:0, one launch (start us, length us, event | category | flops | bytes accessed | tf_op | source)
XLA Modules:
  0.0 84.7 jit_solution(8421726791561197441)
XLA Ops:
  0.6 3.9 %shard_map.104 = (bf16[528,256]{1,0:T(8,128)(2,1)}, bf16[528,768]{1,0:T(8,128)(2,1)}, bf16[528,256]{1,0:T(8,128)(2,1)}, bf16[528,768]{1,0:T(8,128)(2,1)}, bf16[5...) custom-call(s32[8]{0:T(128)} %bitcast.17, s32[8]{0:T(128)} %bitcast.18, s32[1,256]{1,0:T(1,128)} %doc_in.1, ...), custom_call_target="tpu_custom_call" | custom-call | flops 2000000000 | bytes 1048576 | tf_op jit(solution)/shard_map/pallas_call | solution.py:176
  4.6 0.0 copy-start
  4.6 1.6 %collective-permute-start = (bf16[528,768]{1,0:T(8,128)(2,1)}, bf16[528,768]{1,0:T(8,128)(2,1)S(1)}, u32[]{:S(2)}, u32[]{:S(2)}) collective-permute-start(bf16[528,768]{1,0:T(8,128)(2,1)} %get-tuple-element.16), channel_id=1, source_target_pairs={{0,32},{1,9},{2,34},{3,11},{4,36},{5,13},{6,38},{7,15},{8,40},{9,1... | collective-permute-start | bytes 2433032 | tf_op jit(solution)/shard_map/ppermute | solution.py:58
  6.2 1.7 %collective-permute-start.2 = (bf16[528,768]{1,0:T(8,128)(2,1)}, bf16[528,768]{1,0:T(8,128)(2,1)S(1)}, u32[]{:S(2)}, u32[]{:S(2)}) collective-permute-start(bf16[528,768]{1,0:T(8,128)(2,1)} %get-tuple-element.18), channel_id=1, source_target_pairs={{0,96},{1,25},{2,98},{3,27},{4,100},{5,29},{6,102},{7,31},{8,104},... | collective-permute-start | bytes 2433032 | tf_op jit(solution)/shard_map/ppermute | solution.py:58
  7.9 1.9 %collective-permute-start.1 = (bf16[528,256]{1,0:T(8,128)(2,1)}, bf16[528,256]{1,0:T(8,128)(2,1)S(1)}, u32[]{:S(2)}, u32[]{:S(2)}) collective-permute-start(bf16[528,256]{1,0:T(8,128)(2,1)} %get-tuple-element.17), channel_id=1, source_target_pairs={{0,64},{1,17},{2,66},{3,19},{4,68},{5,21},{6,70},{7,23},{8,72},{9,... | collective-permute-start | bytes 811016 | tf_op jit(solution)/shard_map/ppermute | solution.py:58
  9.8 5.8 %collective-permute-start.8 = (bf16[272,1024]{1,0:T(8,128)(2,1)}, bf16[272,1024]{1,0:T(8,128)(2,1)S(1)}, u32[]{:S(2)}, u32[]{:S(2)}) collective-permute-start(bf16[272,1024]{1,0:T(8,128)(2,1)} %get-tuple-element.20.refs_0_), channel_id=1, source_target_pairs={{0,4},{1,5},{2,6},{3,7},{8,12},{9,13},{10,14},{11,15},{16,20},{17,... | collective-permute-start | bytes 1671176 | tf_op jit(solution)/shard_map/ppermute | solution.py:58
  15.6 3.7 %collective-permute-start.7 = (bf16[272,1024]{1,0:T(8,128)(2,1)}, bf16[272,1024]{1,0:T(8,128)(2,1)}, u32[]{:S(2)}, u32[]{:S(2)}) collective-permute-start(bf16[272,1024]{1,0:T(8,128)(2,1)} %get-tuple-element.20.refs_0_), channel_id=1, source_target_pairs={{0,2},{1,3},{2,4},{3,5},{4,6},{5,7},{8,10},{9,11},{10,12},{11,13},... | collective-permute-start | bytes 1671176 | tf_op jit(solution)/shard_map/ppermute | solution.py:58
  19.3 0.0 collective-permute-done.refs_0_
  19.3 0.0 copy-start.4
  19.3 1.7 %collective-permute-start.6 = (bf16[512,512]{1,0:T(8,128)(2,1)}, bf16[512,512]{1,0:T(8,128)(2,1)}, u32[]{:S(2)}, u32[]{:S(2)}) collective-permute-start(bf16[512,512]{1,0:T(8,128)(2,1)} %get-tuple-element.19), channel_id=1, source_target_pairs={{0,64},{1,17},{2,66},{3,19},{4,68},{5,21},{6,70},{7,23},{8,72},{9,... | collective-permute-start | bytes 1572872 | tf_op jit(solution)/shard_map/ppermute | solution.py:58
  21.1 0.0 copy-start.1
  21.1 0.0 collective-permute-done.2.refs_0_
  21.1 0.0 copy-start.2
  21.1 0.9 %copy-done.2 = bf16[528,768]{1,0:T(8,128)(2,1)} copy-done((bf16[528,768]{1,0:T(8,128)(2,1)}, bf16[528,768]{1,0:T(8,128)(2,1)S(1)}, u32[]{:S(2)}) %copy-start.2) | copy-done | bytes 811032
  22.0 0.3 collective-permute-done.1
  22.3 0.0 copy-done.4
  22.3 1.0 %pad_maximum_fusion.refs_2_.refs_1_ = bf16[2112,256]{1,0:T(8,128)(2,1)S(1)} fusion(bf16[528,256]{1,0:T(8,128)(2,1)S(1)} %slice.9, bf16[528,256]{1,0:T(8,128)(2,1)S(1)} %collective-permute-done.1, bf16[528,256]{1,0:T(8,128)(2,1)S(1)} %slice.8, bf16[528,256]{1,0:T(8,128)(2,1)} %get-tuple-element.15), kind=kLoop, calls=%fused_computation | loop fusion | flops 4325376 | bytes 2162688 | tf_op jit(solution)/shard_map/concatenate | solution.py:554
  23.3 3.1 %collective-permute-start.5 = (bf16[2112,256]{1,0:T(8,128)(2,1)S(1)}, bf16[2112,256]{1,0:T(8,128)(2,1)}, u32[]{:S(2)}, u32[]{:S(2)}) collective-permute-start(bf16[2112,256]{1,0:T(8,128)(2,1)S(1)} %pad_maximum_fusion.refs_2_.refs_1_), channel_id=1, source_target_pairs={{0,24},{1,97},{2,26},{3,99},{4,28},{5,101},{6,30},{7,103},{8,0},{9... | collective-permute-start | bytes 3244040 | tf_op jit(solution)/shard_map/ppermute | solution.py:58
  26.4 0.6 collective-permute-start.4
  27.0 2.0 %collective-permute-done.8.refs_2_ = bf16[272,1024]{1,0:T(8,128)(2,1)S(1)} collective-permute-done((bf16[272,1024]{1,0:T(8,128)(2,1)}, bf16[272,1024]{1,0:T(8,128)(2,1)S(1)}, u32[]{:S(2)}, u32[]{:S(2)}) %collective-permute-start.8) | collective-permute-done | bytes 557088 | tf_op jit(solution)/shard_map/ppermute | solution.py:58
  29.0 1.6 %collective-permute-start.3 = (bf16[2112,256]{1,0:T(8,128)(2,1)S(1)}, bf16[2112,256]{1,0:T(8,128)(2,1)}, u32[]{:S(2)}, u32[]{:S(2)}) collective-permute-start(bf16[2112,256]{1,0:T(8,128)(2,1)S(1)} %pad_maximum_fusion.refs_2_.refs_1_), channel_id=1, source_target_pairs={{0,8},{1,33},{2,10},{3,35},{4,12},{5,37},{6,14},{7,39},{8,16},{9,4... | collective-permute-start | bytes 3244040 | tf_op jit(solution)/shard_map/ppermute | solution.py:58
  30.5 0.0 copy-done
  30.5 0.1 broadcast_select_fusion
  30.6 0.0 collective-permute-done.6.after.refs_1_
  30.6 0.1 collective-permute-start.10
  30.7 8.3 %collective-permute-done.7.refs_1_ = bf16[272,1024]{1,0:T(8,128)(2,1)} collective-permute-done((bf16[272,1024]{1,0:T(8,128)(2,1)}, bf16[272,1024]{1,0:T(8,128)(2,1)}, u32[]{:S(2)}, u32[]{:S(2)}) %collective-permute-start.7) | collective-permute-done | bytes 557088 | tf_op jit(solution)/shard_map/ppermute | solution.py:58
  39.0 0.0 collective-permute-start.9
  39.0 0.0 collective-permute-done.10.refs_4_
  39.0 2.2 %collective-permute-done.9.refs_3_ = bf16[272,1024]{1,0:T(8,128)(2,1)S(1)} collective-permute-done((bf16[272,1024]{1,0:T(8,128)(2,1)}, bf16[272,1024]{1,0:T(8,128)(2,1)S(1)}, u32[]{:S(2)}, u32[]{:S(2)}) %collective-permute-start.9) | collective-permute-done | bytes 557088 | tf_op jit(solution)/shard_map/ppermute | solution.py:58
  41.2 0.0 copy-done.1
  41.2 0.0 copy-start.5
  41.2 10.9 %shard_map.105 = (bf16[256,2048]{1,0:T(8,128)(2,1)}, s32[1]{0:T(128)}) custom-call(bf16[256,2048]{1,0:T(8,128)(2,1)S(1)} %bitcast.10, bf16[512,512]{1,0:T(8,128)(2,1)} %collective-permute-done.6.after.refs_1_, bf16[272,1024]{1,0:T(8,128)(2,1)S(1)} %copy-done, bf16[272,1024]{1,0:T(8,128)(2,1)} %collective-permute-done.7.refs_1_, ...), custom_call_target="tpu_custom_call" | custom-call | flops 100000000 | bytes 1048576 | tf_op jit(solution)/shard_map/pallas_call | solution.py:510
  52.1 0.0 collective-permute-done.5.refs_5_.refs_4_
  52.1 0.0 collective-permute-done.4.refs_4_.refs_3_
  52.1 2.6 %collective-permute-done.3.refs_3_.refs_2_ = bf16[2112,256]{1,0:T(8,128)(2,1)} collective-permute-done((bf16[2112,256]{1,0:T(8,128)(2,1)S(1)}, bf16[2112,256]{1,0:T(8,128)(2,1)}, u32[]{:S(2)}, u32[]{:S(2)}) %collective-permute-start.3) | collective-permute-done | bytes 1081376 | tf_op jit(solution)/shard_map/ppermute | solution.py:58
  54.7 0.0 copy-done.5
  54.7 10.0 %shard_map.106 = (bf16[512,512]{1,0:T(8,128)(2,1)S(1)}, bf16[512,512]{1,0:T(8,128)(2,1)S(1)}, s32[64,128]{1,0:T(8,128)S(1)}) custom-call(bf16[528,768]{1,0:T(8,128)(2,1)S(1)} %copy-done.5, bf16[512,512]{1,0:T(8,128)(2,1)} %collective-permute-done.6.after.refs_1_, bf16[2112,256]{1,0:T(8,128)(2,1)S(1)} %pad_maximum_fusion.refs_2_.refs_1_, ...), custom_call_target="tpu_custom_call" | custom-call | flops 30000001024 | bytes 1048576 | tf_op jit(solution)/shard_map/pallas_call | solution.py:452
  64.7 2.2 %collective-permute-start.11 = (bf16[512,512]{1,0:T(8,128)(2,1)S(1)}, bf16[512,512]{1,0:T(8,128)(2,1)S(1)}, u32[]{:S(2)}, u32[]{:S(2)}) collective-permute-start(bf16[512,512]{1,0:T(8,128)(2,1)S(1)} %get-tuple-element.23), channel_id=1, source_target_pairs={{0,96},{1,25},{2,98},{3,27},{4,100},{5,29},{6,102},{7,31},{8,104},... | collective-permute-start | bytes 1572872 | tf_op jit(solution)/shard_map/ppermute | solution.py:58
  66.9 0.0 collective-permute-start.12
  66.9 0.0 copy-done.3
  66.9 4.9 %shard_map.108 = bf16[512,512]{1,0:T(8,128)(2,1)S(1)} custom-call(bf16[528,768]{1,0:T(8,128)(2,1)S(1)} %copy-done.3, bf16[2112,256]{1,0:T(8,128)(2,1)S(1)} %pad_maximum_fusion.refs_2_.refs_1_, bf16[2112,256]{1,0:T(8,128)(2,1)} %collective-permute-done.3.refs_3_.refs_2_, bf16[2112,256]{1,0:T(8,128)(2,1)} %collective-permute-done.4.refs_4_.refs_3_, ...), custom_call_target="tpu_custom_call" | custom-call | flops 30000001024 | bytes 1048576 | tf_op jit(solution)/shard_map/pallas_call | solution.py:452
  71.8 2.1 %collective-permute-start.13 = (bf16[512,512]{1,0:T(8,128)(2,1)S(1)}, bf16[512,512]{1,0:T(8,128)(2,1)S(1)}, u32[]{:S(2)}, u32[]{:S(2)}) collective-permute-start(bf16[512,512]{1,0:T(8,128)(2,1)S(1)} %shard_map.108), channel_id=1, source_target_pairs={{0,32},{1,9},{2,34},{3,11},{4,36},{5,13},{6,38},{7,15},{8,40},{9,1... | collective-permute-start | bytes 1572872 | tf_op jit(solution)/shard_map/ppermute | solution.py:58
  73.9 0.0 copy-done.6
  73.9 4.4 %shard_map.107.refs_0_ = bf16[512,512]{1,0:T(8,128)(2,1)S(1)} custom-call(bf16[512,512]{1,0:T(8,128)(2,1)S(1)} %copy-done.6, bf16[2112,256]{1,0:T(8,128)(2,1)S(1)} %pad_maximum_fusion.refs_2_.refs_1_, bf16[2112,256]{1,0:T(8,128)(2,1)} %collective-permute-done.3.refs_3_.refs_2_, bf16[2112,256]{1,0:T(8,128)(2,1)} %collective-permute-done.4.refs_4_.refs_3_, ...), custom_call_target="tpu_custom_call" | custom-call | flops 30000001024 | bytes 1048576 | tf_op jit(solution)/shard_map/pallas_call | solution.py:452
  78.3 0.9 %collective-permute-done.11.refs_1_ = bf16[512,512]{1,0:T(8,128)(2,1)S(1)} collective-permute-done((bf16[512,512]{1,0:T(8,128)(2,1)S(1)}, bf16[512,512]{1,0:T(8,128)(2,1)S(1)}, u32[]{:S(2)}, u32[]{:S(2)}) %collective-permute-start.11) | collective-permute-done | bytes 524320 | tf_op jit(solution)/shard_map/ppermute | solution.py:58
  79.3 0.0 collective-permute-done.12.refs_2_
  79.3 3.9 %collective-permute-done.13.refs_3_ = bf16[512,512]{1,0:T(8,128)(2,1)S(1)} collective-permute-done((bf16[512,512]{1,0:T(8,128)(2,1)S(1)}, bf16[512,512]{1,0:T(8,128)(2,1)S(1)}, u32[]{:S(2)}, u32[]{:S(2)}) %collective-permute-start.13) | collective-permute-done | bytes 524320 | tf_op jit(solution)/shard_map/ppermute | solution.py:58
  83.2 1.3 %shard_map.109 = bf16[512,2048]{1,0:T(8,128)(2,1)} custom-call(bf16[512,512]{1,0:T(8,128)(2,1)S(1)} %shard_map.107.refs_0_, bf16[512,512]{1,0:T(8,128)(2,1)S(1)} %collective-permute-done.11.refs_1_, bf16[512,512]{1,0:T(8,128)(2,1)S(1)} %collective-permute-done.12.refs_2_, bf16[512,512]{1,0:T(8,128)(2,1)S(1)} %collective-permute-done.13.refs_3_), custom_call_target="tpu_custom_call" | custom-call | flops 2000000000 | bytes 1048576 | tf_op jit(solution)/shard_map/pallas_call | solution.py:213
  (4 shorter events, 0.0 us)
Async XLA Ops:
  4.6 26.0 %copy-start = (bf16[272,1024]{1,0:T(8,128)(2,1)S(1)}, bf16[272,1024]{1,0:T(8,128)(2,1)}, u32[]{:S(2)}) copy-start(bf16[272,1024]{1,0:T(8,128)(2,1)} %get-tuple-element.20.refs_0_) | copy-start | bytes 1671172
  4.6 14.8 %collective-permute-start = (bf16[528,768]{1,0:T(8,128)(2,1)}, bf16[528,768]{1,0:T(8,128)(2,1)S(1)}, u32[]{:S(2)}, u32[]{:S(2)}) collective-permute-start(bf16[528,768]{1,0:T(8,128)(2,1)} %get-tuple-element.16), channel_id=1, source_target_pairs={{0,32},{1,9},{2,34},{3,11},{4,36},{5,13},{6,38},{7,15},{8,40},{9,1... | collective-permute-start | bytes 2433032 | tf_op jit(solution)/shard_map/ppermute | solution.py:58
  6.2 14.9 %collective-permute-start.2 = (bf16[528,768]{1,0:T(8,128)(2,1)}, bf16[528,768]{1,0:T(8,128)(2,1)S(1)}, u32[]{:S(2)}, u32[]{:S(2)}) collective-permute-start(bf16[528,768]{1,0:T(8,128)(2,1)} %get-tuple-element.18), channel_id=1, source_target_pairs={{0,96},{1,25},{2,98},{3,27},{4,100},{5,29},{6,102},{7,31},{8,104},... | collective-permute-start | bytes 2433032 | tf_op jit(solution)/shard_map/ppermute | solution.py:58
  7.9 14.4 %collective-permute-start.1 = (bf16[528,256]{1,0:T(8,128)(2,1)}, bf16[528,256]{1,0:T(8,128)(2,1)S(1)}, u32[]{:S(2)}, u32[]{:S(2)}) collective-permute-start(bf16[528,256]{1,0:T(8,128)(2,1)} %get-tuple-element.17), channel_id=1, source_target_pairs={{0,64},{1,17},{2,66},{3,19},{4,68},{5,21},{6,70},{7,23},{8,72},{9,... | collective-permute-start | bytes 811016 | tf_op jit(solution)/shard_map/ppermute | solution.py:58
  9.8 19.2 %collective-permute-start.8 = (bf16[272,1024]{1,0:T(8,128)(2,1)}, bf16[272,1024]{1,0:T(8,128)(2,1)S(1)}, u32[]{:S(2)}, u32[]{:S(2)}) collective-permute-start(bf16[272,1024]{1,0:T(8,128)(2,1)} %get-tuple-element.20.refs_0_), channel_id=1, source_target_pairs={{0,4},{1,5},{2,6},{3,7},{8,12},{9,13},{10,14},{11,15},{16,20},{17,... | collective-permute-start | bytes 1671176 | tf_op jit(solution)/shard_map/ppermute | solution.py:58
  15.6 23.5 %collective-permute-start.7 = (bf16[272,1024]{1,0:T(8,128)(2,1)}, bf16[272,1024]{1,0:T(8,128)(2,1)}, u32[]{:S(2)}, u32[]{:S(2)}) collective-permute-start(bf16[272,1024]{1,0:T(8,128)(2,1)} %get-tuple-element.20.refs_0_), channel_id=1, source_target_pairs={{0,2},{1,3},{2,4},{3,5},{4,6},{5,7},{8,10},{9,11},{10,12},{11,13},... | collective-permute-start | bytes 1671176 | tf_op jit(solution)/shard_map/ppermute | solution.py:58
  19.3 3.0 %copy-start.4 = (bf16[528,768]{1,0:T(8,128)(2,1)}, bf16[528,768]{1,0:T(8,128)(2,1)S(1)}, u32[]{:S(2)}) copy-start(bf16[528,768]{1,0:T(8,128)(2,1)S(1)} %collective-permute-done.refs_0_) | copy-start | bytes 2433028
  19.3 11.3 %collective-permute-start.6 = (bf16[512,512]{1,0:T(8,128)(2,1)}, bf16[512,512]{1,0:T(8,128)(2,1)}, u32[]{:S(2)}, u32[]{:S(2)}) collective-permute-start(bf16[512,512]{1,0:T(8,128)(2,1)} %get-tuple-element.19), channel_id=1, source_target_pairs={{0,64},{1,17},{2,66},{3,19},{4,68},{5,21},{6,70},{7,23},{8,72},{9,... | collective-permute-start | bytes 1572872 | tf_op jit(solution)/shard_map/ppermute | solution.py:58
  21.1 20.1 %copy-start.1 = (bf16[1,256,2048]{2,1,0:T(8,128)(2,1)S(1)}, bf16[1,256,2048]{2,1,0:T(8,128)(2,1)}, u32[]{:S(2)}) copy-start(bf16[1,256,2048]{2,1,0:T(8,128)(2,1)} %param.14) | copy-start | bytes 3145732
  21.1 0.9 %copy-start.2 = (bf16[528,768]{1,0:T(8,128)(2,1)}, bf16[528,768]{1,0:T(8,128)(2,1)S(1)}, u32[]{:S(2)}) copy-start(bf16[528,768]{1,0:T(8,128)(2,1)S(1)} %collective-permute-done.2.refs_0_) | copy-start | bytes 2433028
  23.3 28.8 %collective-permute-start.5 = (bf16[2112,256]{1,0:T(8,128)(2,1)S(1)}, bf16[2112,256]{1,0:T(8,128)(2,1)}, u32[]{:S(2)}, u32[]{:S(2)}) collective-permute-start(bf16[2112,256]{1,0:T(8,128)(2,1)S(1)} %pad_maximum_fusion.refs_2_.refs_1_), channel_id=1, source_target_pairs={{0,24},{1,97},{2,26},{3,99},{4,28},{5,101},{6,30},{7,103},{8,0},{9... | collective-permute-start | bytes 3244040 | tf_op jit(solution)/shard_map/ppermute | solution.py:58
  26.4 25.7 %collective-permute-start.4 = (bf16[2112,256]{1,0:T(8,128)(2,1)S(1)}, bf16[2112,256]{1,0:T(8,128)(2,1)}, u32[]{:S(2)}, u32[]{:S(2)}) collective-permute-start(bf16[2112,256]{1,0:T(8,128)(2,1)S(1)} %pad_maximum_fusion.refs_2_.refs_1_), channel_id=1, source_target_pairs={{0,16},{1,65},{2,18},{3,67},{4,20},{5,69},{6,22},{7,71},{8,24},{9,... | collective-permute-start | bytes 3244040 | tf_op jit(solution)/shard_map/ppermute | solution.py:58
  29.0 25.8 %collective-permute-start.3 = (bf16[2112,256]{1,0:T(8,128)(2,1)S(1)}, bf16[2112,256]{1,0:T(8,128)(2,1)}, u32[]{:S(2)}, u32[]{:S(2)}) collective-permute-start(bf16[2112,256]{1,0:T(8,128)(2,1)S(1)} %pad_maximum_fusion.refs_2_.refs_1_), channel_id=1, source_target_pairs={{0,8},{1,33},{2,10},{3,35},{4,12},{5,37},{6,14},{7,39},{8,16},{9,4... | collective-permute-start | bytes 3244040 | tf_op jit(solution)/shard_map/ppermute | solution.py:58
  30.6 8.4 %collective-permute-start.10 = (bf16[272,1024]{1,0:T(8,128)(2,1)S(1)}, bf16[272,1024]{1,0:T(8,128)(2,1)S(1)}, u32[]{:S(2)}, u32[]{:S(2)}) collective-permute-start(bf16[272,1024]{1,0:T(8,128)(2,1)S(1)} %broadcast_select_fusion), channel_id=1, source_target_pairs={{0,1},{1,0},{2,3},{3,2},{4,5},{5,4},{6,7},{7,6},{8,9},{9,8},{10,11... | collective-permute-start | bytes 1671176 | tf_op jit(solution)/shard_map/ppermute | solution.py:58
  39.0 2.2 %collective-permute-start.9 = (bf16[272,1024]{1,0:T(8,128)(2,1)}, bf16[272,1024]{1,0:T(8,128)(2,1)S(1)}, u32[]{:S(2)}, u32[]{:S(2)}) collective-permute-start(bf16[272,1024]{1,0:T(8,128)(2,1)} %collective-permute-done.7.refs_1_), channel_id=1, source_target_pairs={{0,1},{1,0},{2,3},{3,2},{4,5},{5,4},{6,7},{7,6},{8,9},{9,8},{10,11... | collective-permute-start | bytes 1671176 | tf_op jit(solution)/shard_map/ppermute | solution.py:58
  41.2 13.5 %copy-start.5 = (bf16[528,768]{1,0:T(8,128)(2,1)S(1)}, bf16[528,768]{1,0:T(8,128)(2,1)}, u32[]{:S(2)}) copy-start(bf16[528,768]{1,0:T(8,128)(2,1)} %copy-done.4) | copy-start | bytes 2433028
  54.7 12.2 %copy-start.3 = (bf16[528,768]{1,0:T(8,128)(2,1)S(1)}, bf16[528,768]{1,0:T(8,128)(2,1)}, u32[]{:S(2)}) copy-start(bf16[528,768]{1,0:T(8,128)(2,1)} %copy-done.2) | copy-start | bytes 2433028
  64.7 14.5 %collective-permute-start.11 = (bf16[512,512]{1,0:T(8,128)(2,1)S(1)}, bf16[512,512]{1,0:T(8,128)(2,1)S(1)}, u32[]{:S(2)}, u32[]{:S(2)}) collective-permute-start(bf16[512,512]{1,0:T(8,128)(2,1)S(1)} %get-tuple-element.23), channel_id=1, source_target_pairs={{0,96},{1,25},{2,98},{3,27},{4,100},{5,29},{6,102},{7,31},{8,104},... | collective-permute-start | bytes 1572872 | tf_op jit(solution)/shard_map/ppermute | solution.py:58
  66.9 12.4 %collective-permute-start.12 = (bf16[512,512]{1,0:T(8,128)(2,1)S(1)}, bf16[512,512]{1,0:T(8,128)(2,1)S(1)}, u32[]{:S(2)}, u32[]{:S(2)}) collective-permute-start(bf16[512,512]{1,0:T(8,128)(2,1)S(1)} %get-tuple-element.24), channel_id=1, source_target_pairs={{0,64},{1,17},{2,66},{3,19},{4,68},{5,21},{6,70},{7,23},{8,72},{9,... | collective-permute-start | bytes 1572872 | tf_op jit(solution)/shard_map/ppermute | solution.py:58
  66.9 7.0 %copy-start.6 = (bf16[512,512]{1,0:T(8,128)(2,1)S(1)}, bf16[512,512]{1,0:T(8,128)(2,1)}, u32[]{:S(2)}) copy-start(bf16[512,512]{1,0:T(8,128)(2,1)} %get-tuple-element.14.refs_0_) | copy-start | bytes 1572868
  71.8 11.4 %collective-permute-start.13 = (bf16[512,512]{1,0:T(8,128)(2,1)S(1)}, bf16[512,512]{1,0:T(8,128)(2,1)S(1)}, u32[]{:S(2)}, u32[]{:S(2)}) collective-permute-start(bf16[512,512]{1,0:T(8,128)(2,1)S(1)} %shard_map.108), channel_id=1, source_target_pairs={{0,32},{1,9},{2,34},{3,11},{4,36},{5,13},{6,38},{7,15},{8,40},{9,1... | collective-permute-start | bytes 1572872 | tf_op jit(solution)/shard_map/ppermute | solution.py:58
